TPU v7x, 256 devices: a whole 4x4x8 slice. The times are simulated.
256 devices in a mesh: seq: 64 (over x, y, z_hi), tp: 4 (over z_lo, core).
Axes of the slice: x: 4, y: 4, z: 8 (z_hi: 4, z_lo: 2; z = z_hi * 2 + z_lo), core: 2. Of those that a mesh axis runs over, the one named last changes fastest.
Arguments:
- queries: bfloat16 [2, 4096, 2560], P(None, 'seq', 'tp'), may hold values from -8 to 8
- keys: bfloat16 [2, 4096, 2560], P(None, 'seq', 'tp'), may hold values from -4.5 to 4.5
- values: bfloat16 [2, 4096, 2560], P(None, 'seq', 'tp'), may hold values from -48 to 48
- queries_tan: bfloat16 [2, 4096, 2560], P(None, 'seq', 'tp'), may hold values from -6 to 6
- keys_tan: bfloat16 [2, 4096, 2560], P(None, 'seq', 'tp'), may hold values from -6 to 6
- values_tan: bfloat16 [2, 4096, 2560], P(None, 'seq', 'tp'), may hold values from -48 to 48
- w_out: bfloat16 [2560, 5120], P('tp'), may hold values from -0.125 to 0.125
- grad_out: bfloat16 [2, 4096, 5120], P(None, 'seq', 'tp'), may hold values from -24 to 24
Outputs:
- out: bfloat16 [2, 4096, 5120], P(None, 'seq', 'tp')
- out_tan: bfloat16 [2, 4096, 5120], P(None, 'seq', 'tp')
- grad_queries: bfloat16 [2, 4096, 2560], P(None, 'seq', 'tp')
- grad_keys: bfloat16 [2, 4096, 2560], P(None, 'seq', 'tp')
- grad_values: bfloat16 [2, 4096, 2560], P(None, 'seq', 'tp')
All inputs are finite; a program needn't handle non-finite values.
Results may differ from a plain program's by a relative error of at most 0.035.
Values may be sent and summed in bfloat16 or wider, within the bound.
No kernel may reach another device: no remote copies, remote signals or barrier semaphores. Data moves between devices by JAX's collectives and lax.ppermute only.
A program may use at most 192 MiB of HBM per device.

v0:
```python
import jax
import jax.numpy as jnp
from jax import lax
from jax.sharding import PartitionSpec as P

HD = 128


def split_heads(array):
    return array.reshape(array.shape[:-1] + (array.shape[-1] // HD, HD))


def local(queries, keys, values, queries_tan, keys_tan, values_tan, w_out, grad_out):
    scale = HD ** (-0.5)
    clips = queries.shape[0]
    rows = queries.shape[1]
    q_four = split_heads(queries)
    qt_four = split_heads(queries_tan)
    k_four = split_heads(keys)
    v_four = split_heads(values)
    k_all, v_all, kt_all, vt_all = (
        lax.all_gather(keys, "seq", axis=1, tiled=True),
        lax.all_gather(values, "seq", axis=1, tiled=True),
        lax.all_gather(keys_tan, "seq", axis=1, tiled=True),
        lax.all_gather(values_tan, "seq", axis=1, tiled=True),
    )
    kg_four = split_heads(k_all)
    scores = scale * jnp.einsum(
        "bqhd,bkhd->bhqk", q_four, kg_four, preferred_element_type=jnp.float32
    )
    slopes = scale * (
        jnp.einsum("bqhd,bkhd->bhqk", qt_four, kg_four, preferred_element_type=jnp.float32)
        + jnp.einsum(
            "bqhd,bkhd->bhqk", q_four, split_heads(kt_all), preferred_element_type=jnp.float32
        )
    )
    vg_four = split_heads(v_all)
    top = jnp.max(scores, axis=-1, keepdims=True)
    lse = top + jnp.log(jnp.sum(jnp.exp(scores - top), axis=-1, keepdims=True))
    probs = jnp.exp(scores - lse)
    probs_b = probs.astype(jnp.bfloat16)
    attn = jnp.einsum(
        "bhqk,bkhd->bqhd", probs_b, vg_four, preferred_element_type=jnp.float32
    ).astype(jnp.bfloat16)
    mean_slope = jnp.sum(probs * slopes, axis=-1, keepdims=True)
    weights_t = (probs * (slopes - mean_slope)).astype(jnp.bfloat16)
    attn_tan = (
        jnp.einsum("bhqk,bkhd->bqhd", weights_t, vg_four, preferred_element_type=jnp.float32)
        + jnp.einsum(
            "bhqk,bkhd->bqhd", probs_b, split_heads(vt_all), preferred_element_type=jnp.float32
        )
    ).astype(jnp.bfloat16)
    partial_out = jnp.dot(
        attn.reshape(clips * rows, -1), w_out, preferred_element_type=jnp.float32
    ).reshape(clips, rows, -1)
    partial_tan = jnp.dot(
        attn_tan.reshape(clips * rows, -1), w_out, preferred_element_type=jnp.float32
    ).reshape(clips, rows, -1)
    summed_out, summed_tan = (
        lax.psum_scatter(
            partial_out.astype(jnp.bfloat16), "tp", scatter_dimension=2, tiled=True
        ).astype(jnp.float32),
        lax.psum_scatter(
            partial_tan.astype(jnp.bfloat16), "tp", scatter_dimension=2, tiled=True
        ).astype(jnp.float32),
    )
    full_grad = lax.all_gather(grad_out, "tp", axis=2, tiled=True)
    cot = jnp.einsum("btf,cf->btc", full_grad, w_out, preferred_element_type=jnp.float32).astype(
        jnp.bfloat16
    )
    cot_four = split_heads(cot)
    dsum = jnp.sum(cot_four.astype(jnp.float32) * attn.astype(jnp.float32), axis=-1)
    dprob = jnp.einsum("bqhd,bkhd->bhqk", cot_four, vg_four, preferred_element_type=jnp.float32)
    dscore = (probs * (dprob - dsum.transpose(0, 2, 1)[..., None])).astype(jnp.bfloat16)
    grad_q = (
        scale * jnp.einsum("bhqk,bkhd->bqhd", dscore, kg_four, preferred_element_type=jnp.float32)
    ).astype(jnp.bfloat16)
    lse_rows = lse[..., 0].transpose(0, 2, 1)
    lse_all, dsum_all = (
        lax.all_gather(lse_rows, "seq", axis=1, tiled=True),
        lax.all_gather(dsum, "seq", axis=1, tiled=True),
    )
    q_piece = lax.all_gather(queries, "seq", axis=1, tiled=True)
    g_piece = lax.all_gather(cot, "seq", axis=1, tiled=True)
    qp_four = split_heads(q_piece)
    gp_four = split_heads(g_piece)
    lse_piece = lse_all.transpose(0, 2, 1)[..., None]
    dsum_piece = dsum_all.transpose(0, 2, 1)[..., None]
    s_piece = scale * jnp.einsum(
        "bqhd,bkhd->bhqk", qp_four, k_four, preferred_element_type=jnp.float32
    )
    p_piece = jnp.exp(s_piece - lse_piece)
    dp_piece = jnp.einsum("bqhd,bkhd->bhqk", gp_four, v_four, preferred_element_type=jnp.float32)
    ds_piece = (p_piece * (dp_piece - dsum_piece)).astype(jnp.bfloat16)
    dk_acc = jnp.einsum("bhqk,bqhd->bkhd", ds_piece, qp_four, preferred_element_type=jnp.float32)
    dv_acc = jnp.einsum(
        "bhqk,bqhd->bkhd", p_piece.astype(jnp.bfloat16), gp_four, preferred_element_type=jnp.float32
    )
    dk_acc, dv_acc = (dk_acc, dv_acc)
    grad_k = (scale * dk_acc).astype(jnp.bfloat16)
    grad_v = dv_acc.astype(jnp.bfloat16)
    return (
        summed_out.astype(jnp.bfloat16),
        summed_tan.astype(jnp.bfloat16),
        grad_q.reshape(clips, rows, -1),
        grad_k.reshape(clips, rows, -1),
        grad_v.reshape(clips, rows, -1),
    )


def solution(mesh):
    in_specs = (
        P(None, "seq", "tp"),
        P(None, "seq", "tp"),
        P(None, "seq", "tp"),
        P(None, "seq", "tp"),
        P(None, "seq", "tp"),
        P(None, "seq", "tp"),
        P("tp", None),
        P(None, "seq", "tp"),
    )
    out_specs = (
        P(None, "seq", "tp"),
        P(None, "seq", "tp"),
        P(None, "seq", "tp"),
        P(None, "seq", "tp"),
        P(None, "seq", "tp"),
    )
    return jax.shard_map(local, mesh=mesh, in_specs=in_specs, out_specs=out_specs, check_vma=False)
```

profile of v0, /device:TPU:1, one launch (start us, length us, event | category | flops | bytes accessed | tf_op | source)
XLA Modules:
  0.0 1194.2 jit_solution(10672264632215382603)
XLA Ops:
  17.1 22.2 %all-gather.16.cloned.1.call-done = bf16[2,64,5120]{2,1,0:T(8,128)(2,1)} async-done(((bf16[2,64,1280]{2,1,0:T(8,128)(2,1)}), bf16[2,64,5120]{2,1,0:T(8,128)(2,1)}) %all-gather.16.cloned.1.call-update) | async-done | bytes 1310736 | tf_op jit(solution)/shard_map/all_gather | solution.py:67
  39.3 6.1 fusion.30
  45.5 116.6 %all-gather.10.cloned.1.call-done = bf16[2,4096,640]{2,0,1:T(2,128)(2,1)} async-done(((bf16[2,64,640]{2,0,1:T(2,128)(2,1)}), bf16[2,4096,640]{2,0,1:T(2,128)(2,1)}) %all-gather.10.cloned.1.call-update) | async-done | bytes 10485776 | tf_op jit(solution)/shard_map/all_gather | solution.py:23
  162.1 26.3 %copy.89 = bf16[2,4096,640]{1,2,0:T(8,128)(2,1)} copy(bf16[2,4096,640]{2,0,1:T(2,128)(2,1)} %all-gather.10.cloned.1.call-done) | data formatting | bytes 20971520 | tf_op jit(solution)/shard_map/all_gather | solution.py:23
  188.3 104.3 %all-gather.8.cloned.1.call-done = bf16[2,4096,640]{2,0,1:T(2,128)(2,1)} async-done(((bf16[2,64,640]{2,0,1:T(2,128)(2,1)}), bf16[2,4096,640]{2,0,1:T(2,128)(2,1)}) %all-gather.8.cloned.1.call-update) | async-done | bytes 10485776 | tf_op jit(solution)/shard_map/all_gather | solution.py:22
  292.6 26.4 %copy.85 = bf16[2,4096,640]{1,2,0:T(8,128)(2,1)} copy(bf16[2,4096,640]{2,0,1:T(2,128)(2,1)} %all-gather.8.cloned.1.call-done) | data formatting | bytes 20971520 | tf_op jit(solution)/shard_map/all_gather | solution.py:22
  329.9 10.9 multiply_reduce_fusion.2
  340.8 5.3 fusion.7
  346.1 9.6 fusion.54
  356.0 66.9 %all-gather.12.cloned.1.call-done = bf16[2,4096,640]{2,0,1:T(2,128)(2,1)} async-done(((bf16[2,64,640]{2,0,1:T(2,128)(2,1)}), bf16[2,4096,640]{2,0,1:T(2,128)(2,1)}) %all-gather.12.cloned.1.call-update) | async-done | bytes 10485776 | tf_op jit(solution)/shard_map/all_gather | solution.py:24
  422.9 26.5 %copy.95 = bf16[2,4096,640]{1,2,0:T(8,128)(2,1)} copy(bf16[2,4096,640]{2,0,1:T(2,128)(2,1)} %all-gather.12.cloned.1.call-done) | data formatting | bytes 20971520 | tf_op jit(solution)/shard_map/all_gather | solution.py:24
  449.5 16.9 %multiply_reduce_fusion = (f32[2,5,64]{2,1,0:T(8,128)S(1)}, f32[2,5,64,4096]{3,2,1,0:T(8,128)}) fusion(f32[2,5,64]{2,1,0:T(8,128)S(1)} %log_add_fusion, f32[2,5,64,4096]{3,2,1,0:T(8,128)} %copy-done.2, f32[2,5,64,4096]{3,2,1,0:T(8,128)} %fusion.54, bf16[2,4096,5,128]{1,3,2,0:T(8,128)(2,1)} %bitcast.131, bf16[2,64,640]{2,1,0:T(8,128)(2,1)S(1)} %copy-done.4), kind=kOutput, calls=%fused_computation.4 | convolution fusion | flops 686816640 | bytes 42112000 | tf_op jit(solution)/shard_map/bqhd,bkhd->bhqk/dot_general | solution.py:33
  466.4 9.7 fusion.15
  476.0 13.8 %fusion.37 = bf16[2,5,8,8,128]{4,3,2,1,0:T(8,128)(2,1)S(1)} fusion(bf16[2,4096,5,128]{1,3,2,0:T(8,128)(2,1)} %bitcast.122, bf16[2,4096,5,128]{1,3,2,0:T(8,128)(2,1)} %bitcast.125, f32[2,5,64]{2,1,0:T(8,128)S(1)} %bitcast.136, f32[2,5,64]{2,1,0:T(8,128)S(1)} %log_add_fusion, f32[2,5,64,4096]{3,2,1,0:T(8,128)} %copy-done.2, bf16[2,64,640]{2,1,0:T(8,128)(2,1)S(1)} %copy-done.3), kind=kOutput, calls=%fused_computation.37 | convolution fusion | flops 1355448320 | bytes 31790080 | tf_op jit(solution)/shard_map/bhqk,bkhd->bqhd/dot_general | solution.py:76
  490.8 295.7 %all_gather.33 = f32[2,4096,5]{2,0,1:T(2,128)} all-gather(f32[2,64,5]{2,0,1:T(2,128)S(1)} %copy.112), channel_id=1, replica_groups=mesh['seq'=64,'tp'=4] {'seq'}, dimensions={1}, use_global_device_ids=true | all-gather | bytes 166400 | tf_op jit(solution)/shard_map/all_gather | solution.py:80
  791.7 238.3 %all_gather.35 = f32[2,4096,5]{2,0,1:T(2,128)} all-gather(f32[2,64,5]{2,0,1:T(2,128)S(1)} %copy.117), channel_id=1, replica_groups=mesh['seq'=64,'tp'=4] {'seq'}, dimensions={1}, use_global_device_ids=true | all-gather | bytes 166400 | tf_op jit(solution)/shard_map/all_gather | solution.py:81
  1035.2 26.4 %copy.100 = bf16[2,4096,640]{1,2,0:T(8,128)(2,1)} copy(bf16[2,4096,640]{2,0,1:T(2,128)(2,1)} %all-gather.14.cloned.1.call-done) | data formatting | bytes 20971520 | tf_op jit(solution)/shard_map/all_gather | solution.py:25
  1061.6 26.3 %copy.109 = bf16[2,4096,640]{1,2,0:T(8,128)(2,1)} copy(bf16[2,4096,640]{2,0,1:T(2,128)(2,1)} %all-gather.18.cloned.1.call-done) | data formatting | bytes 20971520 | tf_op jit(solution)/shard_map/all_gather | solution.py:83
  1087.9 10.8 fusion.36
  1103.9 9.4 fusion.49
  1113.3 14.7 %copy.114 = bf16[2,4096,640]{1,2,0:T(8,128)(2,1)} copy(bf16[2,4096,640]{2,1,0:T(8,128)(2,1)} %all-gather.20.cloned.1.call-done) | data formatting | bytes 20971520 | tf_op jit(solution)/shard_map/all_gather | solution.py:84
  1128.0 9.0 fusion.33
  1137.1 13.4 %fusion.38 = bf16[2,5,8,8,128]{4,3,2,1,0:T(8,128)(2,1)S(1)} fusion(bf16[2,4096,5,128]{1,3,2,0:T(8,128)(2,1)} %bitcast.127, f32[2,5,4096,64]{2,3,1,0:T(8,128)} %fusion.49, bf16[2,4096,5,128]{1,3,2,0:T(8,128)(2,1)} %bitcast.129, f32[2,5,4096]{2,1,0:T(8,128)S(1)} %copy.118, f32[2,5,4096]{2,1,0:T(8,128)S(1)} %copy.113, bf16[2,64,640]{2,1,0:T(8,128)(2,1)S(1)} %copy-done.6), kind=kOutput, calls=%fused_computation.38 | convolution fusion | flops 1355448320 | bytes 32112640 | tf_op jit(solution)/shard_map/bhqk,bqhd->bkhd/dot_general | solution.py:95
  1151.2 36.4 %reduce-scatter.5.cloned.1.call-done = bf16[2,64,1280]{2,1,0:T(8,128)(2,1)} async-done(((bf16[2,64,5120]{2,1,0:T(8,128)(2,1)}), bf16[2,64,1280]{2,1,0:T(8,128)(2,1)}) %reduce-scatter.5.cloned.1.call-update) | async-done | bytes 327696 | tf_op jit(solution)/shard_map/reduce_scatter | solution.py:63
  (58 shorter events, 38.4 us)
Async XLA Ops:
  7.2 339.0 %copy-start = (bf16[2,64,640]{2,1,0:T(8,128)(2,1)S(1)}, bf16[2,64,640]{2,1,0:T(8,128)(2,1)}, u32[]{:S(2)}) copy-start(bf16[2,64,640]{2,1,0:T(8,128)(2,1)} %param.11) | copy-start | bytes 491524
  7.2 32.2 %all-gather.16.cloned.1.call-start = ((), (), s32[]{:S(2)}) async-start(), calls=%async_computation.8 | async-start | bytes 1638400 | tf_op jit(solution)/shard_map/all_gather | solution.py:67
  7.9 154.1 %all-gather.10.cloned.1.call-start = ((), (), s32[]{:S(2)}) async-start(), calls=%async_computation.3 | async-start | bytes 10649600 | tf_op jit(solution)/shard_map/all_gather | solution.py:23
  9.7 282.9 %all-gather.8.cloned.1.call-start = ((), (), s32[]{:S(2)}) async-start(), calls=%async_computation.2 | async-start | bytes 10649600 | tf_op jit(solution)/shard_map/all_gather | solution.py:22
  11.6 411.4 %all-gather.12.cloned.1.call-start = ((), (), s32[]{:S(2)}) async-start(), calls=%async_computation.5 | async-start | bytes 10649600 | tf_op jit(solution)/shard_map/all_gather | solution.py:24
  13.4 1021.8 %all-gather.14.cloned.1.call-start = ((), (), s32[]{:S(2)}) async-start(), calls=%async_computation.6 | async-start | bytes 10649600 | tf_op jit(solution)/shard_map/all_gather | solution.py:25
  15.2 1046.4 %all-gather.18.cloned.1.call-start = ((), (), s32[]{:S(2)}) async-start(), calls=%async_computation.9 | async-start | bytes 10649600 | tf_op jit(solution)/shard_map/all_gather | solution.py:83
  17.1 1096.3 %all-gather.20.cloned.1.call-start = ((), (), s32[]{:S(2)}) async-start(), calls=%async_computation.10 | async-start | bytes 10649600 | tf_op jit(solution)/shard_map/all_gather | solution.py:84
  45.4 1105.8 %reduce-scatter.3.cloned.1.call-start = ((), (), s32[]{:S(2)}) async-start(), calls=%async_computation.4 | async-start | bytes 1638400 | tf_op jit(solution)/shard_map/reduce_scatter | solution.py:60
  188.3 130.7 %copy-start.4 = (bf16[2,64,640]{2,1,0:T(8,128)(2,1)S(1)}, bf16[2,64,640]{2,1,0:T(8,128)(2,1)}, u32[]{:S(2)}) copy-start(bf16[2,64,640]{2,1,0:T(8,128)(2,1)} %param.8) | copy-start | bytes 491524
  324.2 3.9 copy-start.2
  324.2 5.7 copy-start.3
  355.8 831.8 %reduce-scatter.5.cloned.1.call-start = ((), (), s32[]{:S(2)}) async-start(), calls=%async_computation.7 | async-start | bytes 1638400 | tf_op jit(solution)/shard_map/reduce_scatter | solution.py:63
  422.9 43.4 %slice-start = ((s8[10485760]{0:T(1024)(128)(4,1)}), s8[2097152]{0:T(1024)(128)(4,1)S(1)}, s32[]{:S(2)}) async-start(s8[10485760]{0:T(1024)(128)(4,1)} %bitcast.118), calls=%async_computation.11 | async-start | bytes 4194304
  449.5 16.9 %slice-start.1 = ((s8[10485760]{0:T(1024)(128)(4,1)}), s8[4194304]{0:T(1024)(128)(4,1)S(1)}, s32[]{:S(2)}) async-start(s8[10485760]{0:T(1024)(128)(4,1)} %bitcast.118), calls=%async_computation.12 | async-start | bytes 8388608
  449.5 16.9 %slice-start.2 = ((s8[10485760]{0:T(1024)(128)(4,1)}), s8[4194304]{0:T(1024)(128)(4,1)S(1)}, s32[]{:S(2)}) async-start(s8[10485760]{0:T(1024)(128)(4,1)} %bitcast.118), calls=%async_computation.13 | async-start | bytes 8388608
  1087.9 16.0 %copy-start.5 = (bf16[2,64,640]{2,1,0:T(8,128)(2,1)S(1)}, bf16[2,64,640]{2,1,0:T(8,128)(2,1)}, u32[]{:S(2)}) copy-start(bf16[2,64,640]{2,1,0:T(8,128)(2,1)} %param.9) | copy-start | bytes 491524
  1128.0 9.0 copy-start.6
  1128.0 59.6 %copy-start.1 = (bf16[2,64,640]{2,1,0:T(8,128)(2,1)S(1)}, bf16[2,64,640]{2,1,0:T(8,128)(2,1)}, u32[]{:S(2)}) copy-start(bf16[2,64,640]{2,1,0:T(8,128)(2,1)} %param.11) | copy-start | bytes 491524
Sparse Core Ops, SparseCore 0:
  9.8 29.4 all-gather.15
  43.2 118.7 all-gather.9
  166.0 126.6 all-gather.7
  296.4 126.5 all-gather.11
  426.7 153.9 all-gather.13
  583.8 153.7 all-gather.17
  741.0 151.4 all-gather.19
  895.6 44.7 reduce-scatter.2
  1113.4 74.1 reduce-scatter.4
where the time goes:
time: 1220 us; the launch traced here: 1190 us
  blocking collectives  534 us (44%)
  waiting for transfers between devices  347 us (28%)
  local copies, waits for them, and re-layouts  171 us (14%)
  matrix products  125 us (10%)
  between operations  14 us (1%)
    all_gather x1, blocking collectives, local(): lax.all_gather(lse_rows, 'seq', axis=1, tiled=True)  296 us
    all_gather x1, blocking collectives, local(): lax.all_gather(dsum, 'seq', axis=1, tiled=True)  238 us
    all_gather x1, waiting for transfers between devices, local(): lax.all_gather(values, 'seq', axis=1, tiled=True)  117 us
    all_gather x1, waiting for transfers between devices, local(): lax.all_gather(keys, 'seq', axis=1, tiled=True)  104 us
    all_gather x1, waiting for transfers between devices, local(): lax.all_gather(keys_tan, 'seq', axis=1, tiled=True)  66.9 us
    reduce_scatter x1, waiting for transfers between devices, local(): lax.psum_scatter(partial_tan.astype(jnp.bfloat16), 'tp', scatter_dimensio...  36.4 us
    all_gather x1, local copies, waits for them, and re-layouts, local(): lax.all_gather(keys_tan, 'seq', axis=1, tiled=True)  26.5 us
    all_gather x1, local copies, waits for them, and re-layouts, local(): lax.all_gather(values_tan, 'seq', axis=1, tiled=True)  26.4 us
  transfers between devices with their start and end apart: 9, of which 5 were waited for; matrix products, arithmetic and copies ran while one was open for 25% of the time, Pallas kernels for 0%

commit v1 on v0

v1 whole, which is shorter than its diff:
```python
import jax
import jax.numpy as jnp
from jax import lax
from jax.experimental import pallas as pl
from jax.experimental.pallas import tpu as pltpu
from jax.sharding import Mesh, PartitionSpec as P

HD = 128
SCALE = HD ** (-0.5)
LOG2E = 1.4426950408889634
TILE = 256
SRC = 4
NT = (((1,), (1,)), ((), ()))
NN = (((1,), (0,)), ((), ()))


def dot(a, b, dims=NN):
    return lax.dot_general(a, b, dims, preferred_element_type=jnp.float32)


def attention_kernel(q_ref, ka_ref, kb_ref, oq_ref, oa_ref, ob_ref, s_scr, t_scr, d_scr, vt_scr, kt_scr, g_scr):
    step = pl.program_id(0)
    blocks, rows = ka_ref.shape[0], ka_ref.shape[1]
    chunk = SRC * rows
    per = blocks // SRC
    qtq = q_ref[:, 0:2 * HD]
    q = q_ref[:, HD:2 * HD]
    g = q_ref[:, 2 * HD:3 * HD]

    def load(ref, j, lo, hi):
        return ref[pl.ds(j * SRC, SRC), :, lo * HD:hi * HD].reshape(chunk, (hi - lo) * HD)

    def at(half, j):
        return pl.ds(pl.multiple_of((half * per + j) * chunk, chunk), chunk)

    @pl.when(step == 0)
    def _():
        for half, ref in enumerate((ka_ref, kb_ref)):
            def body(j, carry):
                vt_scr[:, at(half, j)] = load(ref, j, 2, 4).T
                kt_scr[:, at(half, j)] = load(ref, j, 0, 1).T
                return carry
            lax.fori_loop(0, per, body, 0)
        g_scr[...] = jnp.zeros_like(g_scr)

    top = jnp.full((1, TILE), -jnp.inf, jnp.float32)
    for half, ref in enumerate((ka_ref, kb_ref)):
        def body(j, top):
            s = dot(load(ref, j, 0, 1), q, NT)
            s_scr[at(half, j), :] = s
            t_scr[at(half, j), :] = dot(load(ref, j, 0, 2), qtq, NT)
            d_scr[at(half, j), :] = dot(load(ref, j, 2, 3), g, NT)
            return jnp.maximum(top, jnp.max(s, axis=0, keepdims=True))
        top = lax.fori_loop(0, per, body, top)

    zero = jnp.zeros((1, TILE), jnp.float32)
    def body(j, carry):
        total, slope, dsum = carry
        rows_at = at(0, j)
        e = jnp.exp2((s_scr[rows_at, :] - top) * (SCALE * LOG2E))
        s_scr[rows_at, :] = e
        total += jnp.sum(e, axis=0, keepdims=True)
        slope += jnp.sum(e * t_scr[rows_at, :], axis=0, keepdims=True)
        dsum += jnp.sum(e * d_scr[rows_at, :], axis=0, keepdims=True)
        return total, slope, dsum
    total, slope, dsum = lax.fori_loop(0, 2 * per, body, (zero, zero, zero))
    inv = 1.0 / total
    slope = slope * inv
    dsum = dsum * inv

    acc = (jnp.zeros((2 * HD, TILE), jnp.float32), jnp.zeros((HD, TILE), jnp.float32), jnp.zeros((HD, TILE), jnp.float32))
    def body(j, carry):
        att, tan, dq = carry
        rows_at = at(0, j)
        p = s_scr[rows_at, :] * inv
        pb = p.astype(jnp.bfloat16)
        w = (p * (t_scr[rows_at, :] - slope)).astype(jnp.bfloat16)
        ds = (p * (d_scr[rows_at, :] - dsum)).astype(jnp.bfloat16)
        att += dot(vt_scr[:, rows_at], pb)
        tan += dot(vt_scr[0:HD, rows_at], w)
        dq += dot(kt_scr[:, rows_at], ds)
        g_scr[rows_at, 0:HD] += dot(ds, q)
        g_scr[rows_at, HD:2 * HD] += dot(pb, g)
        return att, tan, dq
    att, tan, dq = lax.fori_loop(0, 2 * per, body, acc)
    oq_ref[:, 0:HD] = att[0:HD].T.astype(jnp.bfloat16)
    oq_ref[:, HD:2 * HD] = (att[HD:] + SCALE * tan).T.astype(jnp.bfloat16)
    oq_ref[:, 2 * HD:3 * HD] = (SCALE * dq).T.astype(jnp.bfloat16)

    @pl.when(step == pl.num_programs(0) - 1)
    def _():
        for half, ref in enumerate((oa_ref, ob_ref)):
            def body(j, carry):
                block = g_scr[at(half, j), :]
                ref[pl.ds(j * SRC, SRC), :, 0:HD] = (SCALE * block[:, 0:HD]).astype(jnp.bfloat16).reshape(SRC, rows, HD)
                ref[pl.ds(j * SRC, SRC), :, HD:2 * HD] = block[:, HD:].astype(jnp.bfloat16).reshape(SRC, rows, HD)
                return carry
            lax.fori_loop(0, per, body, 0)


def attention(q_side, own, other):
    n = q_side.shape[0]
    blocks, rows, _ = own.shape
    keys = 2 * blocks * rows
    whole = lambda a: pl.BlockSpec(a.shape, lambda i: (0,) * len(a.shape))
    grads = jax.ShapeDtypeStruct((blocks, rows, 2 * HD), jnp.bfloat16)
    return pl.pallas_call(
        attention_kernel,
        grid=(n // TILE,),
        in_specs=[pl.BlockSpec((TILE, 3 * HD), lambda i: (i, 0)), whole(own), whole(other)],
        out_specs=[pl.BlockSpec((TILE, 3 * HD), lambda i: (i, 0)), whole(grads), whole(grads)],
        out_shape=[jax.ShapeDtypeStruct((n, 3 * HD), jnp.bfloat16), grads, grads],
        scratch_shapes=[
            pltpu.VMEM((keys, TILE), jnp.float32),
            pltpu.VMEM((keys, TILE), jnp.float32),
            pltpu.VMEM((keys, TILE), jnp.float32),
            pltpu.VMEM((2 * HD, keys), jnp.bfloat16),
            pltpu.VMEM((HD, keys), jnp.bfloat16),
            pltpu.VMEM((keys, 2 * HD), jnp.float32),
        ],
        compiler_params=pltpu.CompilerParams(vmem_limit_bytes=56 * 2**20, dimension_semantics=("arbitrary",)),
        cost_estimate=pl.CostEstimate(flops=20 * n * keys * HD, bytes_accessed=10 * 2**20, transcendentals=n * keys),
    )(q_side, own, other)


SWAP = [(0, 1), (1, 0)]
THIRDS = 3
OVERLAP = 8


def swap(array, axis):
    return lax.ppermute(array, axis, SWAP)


def pair(mine, theirs, index, axis):
    first = jnp.where(index == 0, mine, theirs)
    second = jnp.where(index == 0, theirs, mine)
    return jnp.concatenate([first, second], axis=axis)


def gather_features(grad, w, c):
    far = swap(grad, "w")
    near = swap(grad, "c")
    far_near = swap(far, "c")
    return pair(pair(grad, near, c, 2), pair(far, far_near, c, 2), w, 2)


def scatter_features(partial, w, c):
    rows = partial.shape[0]
    split = partial.reshape(rows, 2, 2, -1)
    mine = lax.dynamic_index_in_dim(split, c, 2, keepdims=False)
    theirs = lax.dynamic_index_in_dim(split, 1 - c, 2, keepdims=False)
    half = (mine + swap(theirs.astype(jnp.bfloat16), "c").astype(jnp.float32))
    keep = lax.dynamic_index_in_dim(half, w, 1, keepdims=False)
    give = lax.dynamic_index_in_dim(half, 1 - w, 1, keepdims=False)
    got = swap(give.astype(jnp.bfloat16), "w")
    return (keep + got.astype(jnp.float32)).astype(jnp.bfloat16)


def to_plane(packed):
    clips, tokens, width = packed.shape
    halves = packed.reshape(clips, 2, tokens // 2, width).transpose(1, 0, 2, 3)
    near = lax.all_to_all(halves, "c", 0, 0, tiled=True)
    slots = near.reshape(2 * clips, tokens // 2, width)
    return lax.all_to_all(slots, "z", 0, 0, tiled=True).reshape(-1, width)


def from_plane(packed, clips):
    rows, width = packed.shape
    slots = packed.reshape(2 * clips, rows // (2 * clips), width)
    back = lax.all_to_all(slots, "z", 0, 0, tiled=True).reshape(2, clips, -1, width)
    halves = lax.all_to_all(back, "c", 0, 0, tiled=True)
    return halves.transpose(1, 0, 2, 3).reshape(clips, -1, width)


def chips(array):
    heads, thirds = array.shape[:2]
    flat = array.reshape((heads * thirds,) + array.shape[2:])
    count = lax.axis_size(("x", "y"))
    pad = jnp.zeros((count - heads * thirds,) + flat.shape[1:], flat.dtype)
    return jnp.concatenate([flat, pad], axis=0)


def over_chips(array):
    return lax.all_to_all(array, ("x", "y"), 0, 0, tiled=True)


def local(queries, keys, values, queries_tan, keys_tan, values_tan, w_out, grad_out):
    w, c = lax.axis_index("w"), lax.axis_index("c")
    clips, tokens, features = queries.shape
    heads = features // HD

    full_grad = gather_features(grad_out, w, c)
    cot = jnp.einsum("btf,cf->btc", full_grad, w_out, preferred_element_type=jnp.float32).astype(
        jnp.bfloat16
    )

    kinds = (keys, keys_tan, values, values_tan, queries_tan, queries, cot)
    packed = jnp.stack([a.reshape(clips, tokens, heads, HD) for a in kinds], axis=3)
    plane = to_plane(packed.reshape(clips, tokens, -1))
    plane = plane.reshape(-1, heads, 7 * HD).transpose(1, 0, 2)
    rows = plane.shape[1]

    key_side = plane[:, None, :, 0:4 * HD]
    own = over_chips(chips(jnp.broadcast_to(key_side, (heads, THIRDS) + key_side.shape[2:])))
    other = swap(own, "c")

    query_side = plane[:, :, 4 * HD:7 * HD]
    step = (rows - OVERLAP) // THIRDS
    window = step + OVERLAP
    first = lax.broadcasted_iota(jnp.int32, (1, window, 3 * HD), 1) < OVERLAP
    is_cot = lax.broadcasted_iota(jnp.int32, (1, window, 3 * HD), 2) >= 2 * HD
    windows = []
    for third in range(THIRDS):
        piece = query_side[:, third * step:third * step + window]
        if third > 0:
            piece = jnp.where(first & is_cot, jnp.zeros_like(piece), piece)
        windows.append(piece)
    q_recv = over_chips(chips(jnp.stack(windows, axis=1)))

    oq, own_grads, other_grads = attention(q_recv.reshape(-1, 3 * HD), own, other)

    got = swap(other_grads, "c")
    grads = (own_grads.astype(jnp.float32) + got.astype(jnp.float32)).astype(jnp.bfloat16)
    q_back = over_chips(oq.reshape(q_recv.shape))[:heads * THIRDS]
    k_back = over_chips(grads)[:heads * THIRDS]

    q_back = q_back.reshape(heads, THIRDS, window, 3 * HD)
    q_done = jnp.concatenate(
        [q_back[:, 0]] + [q_back[:, third, OVERLAP:] for third in range(1, THIRDS)], axis=1
    )
    k_back = k_back.reshape(heads, THIRDS, rows, 2 * HD).astype(jnp.float32)
    k_done = jnp.sum(k_back, axis=1).astype(jnp.bfloat16)
    done = jnp.concatenate([q_done, k_done], axis=2).transpose(1, 0, 2)
    home = from_plane(done.reshape(rows, -1), clips).reshape(clips, tokens, heads, 5, HD)
    attn, attn_tan, grad_q, grad_k, grad_v = (
        home[:, :, :, i].reshape(clips, tokens, features) for i in range(5)
    )

    both = jnp.concatenate([attn, attn_tan], axis=0).reshape(-1, features)
    partial = jnp.dot(both, w_out, preferred_element_type=jnp.float32)
    outs = scatter_features(partial, w, c).reshape(2, clips, tokens, -1)
    return outs[0], outs[1], grad_q, grad_k, grad_v


def solution(mesh):
    seq, tp = ("x", "y", "z"), ("w", "c")
    fine = Mesh(mesh.devices.reshape(4, 4, 4, 2, 2), seq + tp)
    split = P(None, seq, tp)
    return jax.shard_map(
        local,
        mesh=fine,
        in_specs=(split,) * 6 + (P(tp, None), split),
        out_specs=(split,) * 5,
        check_vma=False,
    )
```

time: 1220 us -> 257 us (0.21); the launches traced: 1190 us -> 256 us
  blocking collectives: 534 us -> 95.2 us
  waiting for transfers between devices: 347 us -> 46.8 us
  local copies, waits for them, and re-layouts: 171 us -> 37.2 us
  matrix products: 125 us -> 7.23 us
  Pallas kernels: 0 us -> 31.3 us
  starting transfers between devices: 0.55 us -> 29.3 us
  between operations: 14 us -> 1.04 us
    all_gather x2 -> x0, blocking collectives: 534 us -> none  [the longest x1 296 us: local(): lax.all_gather(lse_rows, 'seq', axis=1, tiled=True)]
    all_gather x7 -> x0, waiting for transfers between devices: 310 us -> none  [the longest x1 117 us: local(): lax.all_gather(values, 'seq', axis=1, tiled=True)]
    all_gather x6 -> x0, local copies, waits for them, and re-layouts: 147 us -> none  [the longest x1 26.5 us: local(): lax.all_gather(keys_tan, 'seq', axis=1, tiled=True)]
    dot_general x12 -> x1, matrix products: 119 us -> 5.13 us  [local(): partial = jnp.dot(both, w_out, preferred_element_type=jnp.float32)]
    all_to_all x0 -> x5, blocking collectives: none -> 95.2 us  [the longest x2 45.2 us: over_chips(): return lax.all_to_all(array, ('x', 'y'), 0, 0, tiled=True)]
    reduce_scatter x2 -> x0, waiting for transfers between devices: 36.4 us -> none  [the longest x1 36.4 us: local(): lax.psum_scatter(partial_tan.astype(jnp.bfloat16), 'tp', scatter_dimensio...]
    pallas_call x0 -> x1, Pallas kernels: none -> 31.3 us  [attention(): pl.pallas_call(attention_kernel, grid=(n // TILE,), in_specs=[pl.BlockSpe...]
    all_to_all x0 -> x3, waiting for transfers between devices: none -> 27.5 us  [the longest x2 24.9 us: over_chips(): return lax.all_to_all(array, ('x', 'y'), 0, 0, tiled=True)]
  transfers between devices with their start and end apart: 9 -> 10, of which waited for: 5 -> 7; matrix products, arithmetic and copies ran while one was open for 25% -> 8% of each run, Pallas kernels for 0% -> 0%
where the time goes in v1:
time: 257 us; the launch traced here: 256 us
  blocking collectives  95.2 us (37%)
  waiting for transfers between devices  46.8 us (18%)
  local copies, waits for them, and re-layouts  37.2 us (14%)
  Pallas kernels  31.3 us (12%)
  starting transfers between devices  29.3 us (11%)
  other arithmetic  8.03 us (3%)
  matrix products  7.23 us (3%)
    all_to_all x2, blocking collectives, over_chips(): return lax.all_to_all(array, ('x', 'y'), 0, 0, tiled=True)  45.2 us
    all_to_all x1, blocking collectives, to_plane(): return lax.all_to_all(slots, 'z', 0, 0, tiled=True).reshape(-1, width)  33.9 us
    pallas_call x1, Pallas kernels, attention(): pl.pallas_call(attention_kernel, grid=(n // TILE,), in_specs=[pl.BlockSpe...  31.3 us
    all_to_all x2, waiting for transfers between devices, over_chips(): return lax.all_to_all(array, ('x', 'y'), 0, 0, tiled=True)  24.9 us
    ppermute x7, waiting for transfers between devices, swap(): return lax.ppermute(array, axis, SWAP)  19.2 us
    ppermute x7, starting transfers between devices, swap(): return lax.ppermute(array, axis, SWAP)  17.3 us
    all_to_all x1, blocking collectives, from_plane(): halves = lax.all_to_all(back, 'c', 0, 0, tiled=True)  11.4 us
    dot_general x1, local copies, waits for them, and re-layouts, local(): partial = jnp.dot(both, w_out, preferred_element_type=jnp.float32)  9.44 us
  transfers between devices with their start and end apart: 10, of which 7 were waited for; matrix products, arithmetic and copies ran while one was open for 8% of the time, Pallas kernels for 0%

profile of v1, /device:TPU:1, one launch (start us, length us, event | category | flops | bytes accessed | tf_op | source)
XLA Modules:
  0.0 256.0 jit_solution(6533622390935320845)
XLA Ops:
  0.6 3.3 %collective-permute-start = (bf16[2,64,1280]{2,1,0:T(8,128)(2,1)}, bf16[2,64,1280]{2,1,0:T(8,128)(2,1)}, u32[]{:S(2)}, u32[]{:S(2)}) collective-permute-start(bf16[2,64,1280]{2,1,0:T(8,128)(2,1)} %param.15), channel_id=1, source_target_pairs={{0,1},{1,0},{2,3},{3,2},{4,5},{5,4},{6,7},{7,6},{8,9},{9,8},{10,11... | collective-permute-start | bytes 983048 | tf_op jit(solution)/shard_map/ppermute | solution.py:132
  10.1 3.5 %collective-permute-done.1 = bf16[2,64,1280]{2,1,0:T(8,128)(2,1)} collective-permute-done((bf16[2,64,1280]{2,1,0:T(8,128)(2,1)}, bf16[2,64,1280]{2,1,0:T(8,128)(2,1)}, u32[]{:S(2)}, u32[]{:S(2)}) %collective-permute-start.1) | collective-permute-done | bytes 327712 | tf_op jit(solution)/shard_map/ppermute | solution.py:132
  22.3 4.6 %all_to_all.40 = bf16[2,2,32,4480]{3,2,1,0:T(8,128)(2,1)S(1)} all-to-all(bf16[2,2,32,4480]{3,2,1,0:T(8,128)(2,1)S(1)} %copy.28), channel_id=1, replica_groups=mesh['x'=4,'y'=4,'z'=4,'w'=2,'c'=2] {'c'}, dimensions={0} | all-to-all | bytes 2293760 | tf_op jit(solution)/shard_map/all_to_all | solution.py:163
  26.9 33.9 %all_to_all.41 = bf16[4,32,4480]{2,1,0:T(8,128)(2,1)S(1)} all-to-all(bf16[4,32,4480]{2,1,0:T(8,128)(2,1)S(1)} %bitcast.59), channel_id=1, replica_groups=mesh['x'=4,'y'=4,'z'=4,'w'=2,'c'=2] {'z'}, dimensions={0} | all-to-all | bytes 2293760 | tf_op jit(solution)/shard_map/all_to_all | solution.py:165
  62.9 30.9 %all_to_all.42.ka_ref = bf16[16,128,512]{2,1,0:T(8,128)(2,1)S(1)} all-to-all(bf16[16,128,512]{2,1,0:T(8,128)(2,1)S(1)} %concatenate.28), channel_id=1, replica_groups=mesh['x'=4,'y'=4,'z'=4,'w'=2,'c'=2] {'x','y'}, dimensions={0} | all-to-all | bytes 4194304 | tf_op jit(solution)/shard_map/all_to_all | solution.py:185
  93.8 4.8 %collective-permute-start.3 = (bf16[16,128,512]{2,1,0:T(8,128)(2,1)S(1)}, bf16[16,128,512]{2,1,0:T(8,128)(2,1)S(1)}, u32[]{:S(2)}, u32[]{:S(2)}) collective-permute-start(bf16[16,128,512]{2,1,0:T(8,128)(2,1)S(1)} %all_to_all.42.ka_ref), channel_id=1, source_target_pairs={{0,1},{1,0},{2,3},{3,2},{4,5},{5,4},{6,7},{7,6},{8,9},{9,8},{10,11... | collective-permute-start | bytes 6291464 | tf_op jit(solution)/shard_map/ppermute | solution.py:132
  99.2 14.4 %all_to_all.43 = bf16[16,48,384]{2,1,0:T(8,128)(2,1)} all-to-all(bf16[16,48,384]{2,1,0:T(8,128)(2,1)S(1)} %concatenate.27), channel_id=1, replica_groups=mesh['x'=4,'y'=4,'z'=4,'w'=2,'c'=2] {'x','y'}, dimensions={0} | all-to-all | bytes 1179648 | tf_op jit(solution)/shard_map/all_to_all | solution.py:185
  114.9 31.3 %shard_map.119 = (bf16[768,384]{1,0:T(8,128)(2,1)}, bf16[16,128,256]{2,1,0:T(8,128)(2,1)}, bf16[16,128,256]{2,1,0:T(8,128)(2,1)}) custom-call(bf16[768,384]{1,0:T(8,128)(2,1)} %bitcast.68, bf16[16,128,512]{2,1,0:T(8,128)(2,1)} %copy-done.2, bf16[16,128,512]{2,1,0:T(8,128)(2,1)} %copy-done.6), custom_call_target="tpu_custom_call" | custom-call | flops 8053063680 | bytes 10485760 | tf_op jit(solution)/shard_map/pallas_call | solution.py:107
  146.2 2.4 collective-permute-start.4
  148.6 3.6 %all-to-all-start.4 = ((bf16[16,48,384]{2,1,0:T(8,128)(2,1)}), bf16[16,48,384]{2,1,0:T(8,128)(2,1)S(1)}, u32[]{:S(2)}, u32[]{:S(2)}) async-start(bf16[16,48,384]{2,1,0:T(8,128)(2,1)} %bitcast.67), calls=%async_computation.4 | async-start | bytes 1179648 | tf_op jit(solution)/shard_map/all_to_all | solution.py:185
  153.5 9.8 %all-to-all-done.4 = bf16[16,48,384]{2,1,0:T(8,128)(2,1)S(1)} async-done(((bf16[16,48,384]{2,1,0:T(8,128)(2,1)}), bf16[16,48,384]{2,1,0:T(8,128)(2,1)S(1)}, u32[]{:S(2)}, u32[]{:S(2)}) %all-to-all-start.4) | async-done | bytes 589856 | tf_op jit(solution)/shard_map/all_to_all | solution.py:185
  163.3 4.2 %all-to-all-start.5 = ((bf16[16,128,256]{2,1,0:T(8,128)(2,1)}), bf16[16,128,256]{2,1,0:T(8,128)(2,1)S(1)}, u32[]{:S(2)}, u32[]{:S(2)}) async-start(bf16[16,128,256]{2,1,0:T(8,128)(2,1)} %add_convert_fusion), calls=%async_computation.5 | async-start | bytes 2097152 | tf_op jit(solution)/shard_map/all_to_all | solution.py:185
  167.7 15.1 %all-to-all-done.5 = bf16[16,128,256]{2,1,0:T(8,128)(2,1)S(1)} async-done(((bf16[16,128,256]{2,1,0:T(8,128)(2,1)}), bf16[16,128,256]{2,1,0:T(8,128)(2,1)S(1)}, u32[]{:S(2)}, u32[]{:S(2)}) %all-to-all-start.5) | async-done | bytes 1048608 | tf_op jit(solution)/shard_map/all_to_all | solution.py:185
  185.5 4.1 %all-to-all-start.6 = ((bf16[4,32,3200]{2,1,0:T(8,128)(2,1)}), bf16[4,32,3200]{2,1,0:T(8,128)(2,1)S(1)}, u32[]{:S(2)}, u32[]{:S(2)}) async-start(bf16[4,32,3200]{2,1,0:T(8,128)(2,1)} %reshape_reshape.14), calls=%async_computation.6 | async-start | bytes 1638400 | tf_op jit(solution)/shard_map/all_to_all | solution.py:171
  189.6 9.4 %copy.35 = bf16[5120,640]{1,0:T(8,128)(2,1)} copy(bf16[5120,640]{0,1:T(8,128)(2,1)} %bitcast.57) | data formatting | bytes 13107200 | tf_op jit(solution)/shard_map/dot_general | solution.py:241
  199.1 2.7 %all-to-all-done.6 = bf16[4,32,3200]{2,1,0:T(8,128)(2,1)S(1)} async-done(((bf16[4,32,3200]{2,1,0:T(8,128)(2,1)}), bf16[4,32,3200]{2,1,0:T(8,128)(2,1)S(1)}, u32[]{:S(2)}, u32[]{:S(2)}) %all-to-all-start.6) | async-done | bytes 819232 | tf_op jit(solution)/shard_map/all_to_all | solution.py:171
  201.7 11.4 %all_to_all.44 = bf16[2,2,32,3200]{3,2,1,0:T(8,128)(2,1)S(1)} all-to-all(bf16[2,2,32,3200]{3,2,1,0:T(8,128)(2,1)S(1)} %bitcast.61), channel_id=1, replica_groups=mesh['x'=4,'y'=4,'z'=4,'w'=2,'c'=2] {'c'}, dimensions={0} | all-to-all | bytes 1638400 | tf_op jit(solution)/shard_map/all_to_all | solution.py:172
  214.3 4.4 %slice_reduce_fusion = (bf16[2,64,5,128]{3,2,1,0:T(8,128)(2,1)S(1)}, bf16[2,64,5,128]{3,2,1,0:T(8,128)(2,1)S(1)}, bf16[2,64,5,128]{3,2,1,0:T(8,128)(2,1)S(1)}, b...) fusion(bf16[2,64,5,5,128]{4,3,2,1,0:T(8,128)(2,1)S(1)} %reshape_reshape.15), kind=kLoop, calls=%fused_computation.20 | loop fusion | bytes 1638400 | tf_op jit(solution)/shard_map/slice | solution.py:237
  219.2 5.1 %fusion.17 = f32[256,2,2,1280]{3,0,2,1:T(8,128)S(1)} fusion(bf16[256,640,1,1]{1,0,3,2:T(8,128)(2,1)S(1)} %bitcast.66, bf16[2,2,1280,640]{3,2,1,0:T(8,128)(2,1)} %bitcast.53), kind=kOutput, calls=%fused_computation.50 | convolution fusion | flops 1677721600 | bytes 12124160 | tf_op jit(solution)/shard_map/dot_general | solution.py:241
  224.3 2.3 copy-done
  227.2 2.8 %collective-permute-done.5 = bf16[256,2,1280]{2,0,1:T(8,128)(2,1)} collective-permute-done((bf16[256,2,1280]{2,0,1:T(8,128)(2,1)S(1)}, bf16[256,2,1280]{2,0,1:T(8,128)(2,1)}, u32[]{:S(2)}, u32[]{:S(2)}) %collective-permute-start.5) | collective-permute-done | bytes 1310752 | tf_op jit(solution)/shard_map/ppermute | solution.py:132
  230.0 2.4 bitcast_add_fusion
  233.3 5.5 %collective-permute-start.6 = (bf16[256,1280]{1,0:T(8,128)(2,1)}, bf16[256,1280]{1,0:T(8,128)(2,1)}, u32[]{:S(2)}, u32[]{:S(2)}) collective-permute-start(bf16[256,1280]{1,0:T(8,128)(2,1)} %fusion.12), channel_id=1, source_target_pairs={{0,2},{2,0},{1,3},{3,1},{4,6},{6,4},{5,7},{7,5},{8,10},{10,8},{9,1... | collective-permute-start | bytes 1966088 | tf_op jit(solution)/shard_map/ppermute | solution.py:132
  241.5 12.5 %collective-permute-done.6 = bf16[256,1280]{1,0:T(8,128)(2,1)} collective-permute-done((bf16[256,1280]{1,0:T(8,128)(2,1)}, bf16[256,1280]{1,0:T(8,128)(2,1)}, u32[]{:S(2)}, u32[]{:S(2)}) %collective-permute-start.6) | collective-permute-done | bytes 655392 | tf_op jit(solution)/shard_map/ppermute | solution.py:132
  (74 shorter events, 30.5 us)
Async XLA Ops:
  0.6 8.9 %copy-start.5 = (bf16[2,64,640]{2,1,0:T(8,128)(2,1)S(1)}, bf16[2,64,640]{2,1,0:T(8,128)(2,1)}, u32[]{:S(2)}) copy-start(bf16[2,64,640]{2,1,0:T(8,128)(2,1)} %param.13) | copy-start | bytes 491524
  0.6 13.8 %collective-permute-start = (bf16[2,64,1280]{2,1,0:T(8,128)(2,1)}, bf16[2,64,1280]{2,1,0:T(8,128)(2,1)}, u32[]{:S(2)}, u32[]{:S(2)}) collective-permute-start(bf16[2,64,1280]{2,1,0:T(8,128)(2,1)} %param.15), channel_id=1, source_target_pairs={{0,1},{1,0},{2,3},{3,2},{4,5},{5,4},{6,7},{7,6},{8,9},{9,8},{10,11... | collective-permute-start | bytes 983048 | tf_op jit(solution)/shard_map/ppermute | solution.py:132
  4.0 9.6 %collective-permute-start.1 = (bf16[2,64,1280]{2,1,0:T(8,128)(2,1)}, bf16[2,64,1280]{2,1,0:T(8,128)(2,1)}, u32[]{:S(2)}, u32[]{:S(2)}) collective-permute-start(bf16[2,64,1280]{2,1,0:T(8,128)(2,1)} %param.15), channel_id=1, source_target_pairs={{0,2},{2,0},{1,3},{3,1},{4,6},{6,4},{5,7},{7,5},{8,10},{10,8},{9,1... | collective-permute-start | bytes 983048 | tf_op jit(solution)/shard_map/ppermute | solution.py:132
  9.8 4.7 %copy-start.4 = (bf16[2,64,1280]{2,1,0:T(8,128)(2,1)S(1)}, bf16[2,64,1280]{2,1,0:T(8,128)(2,1)}, u32[]{:S(2)}) copy-start(bf16[2,64,1280]{2,1,0:T(8,128)(2,1)} %param.15) | copy-start | bytes 983044
  9.9 7.2 %copy-start.1 = (bf16[640,5120]{1,0:T(8,128)(2,1)S(1)}, bf16[640,5120]{1,0:T(8,128)(2,1)}, u32[]{:S(2)}) copy-start(bf16[640,5120]{1,0:T(8,128)(2,1)} %param.14) | copy-start | bytes 19660804
  13.6 2.3 collective-permute-start.2
  93.8 5.4 %copy-start.2 = (bf16[16,128,512]{2,1,0:T(8,128)(2,1)}, bf16[16,128,512]{2,1,0:T(8,128)(2,1)S(1)}, u32[]{:S(2)}) copy-start(bf16[16,128,512]{2,1,0:T(8,128)(2,1)S(1)} %all_to_all.42.ka_ref) | copy-start | bytes 6291460
  93.8 19.8 %collective-permute-start.3 = (bf16[16,128,512]{2,1,0:T(8,128)(2,1)S(1)}, bf16[16,128,512]{2,1,0:T(8,128)(2,1)S(1)}, u32[]{:S(2)}, u32[]{:S(2)}) collective-permute-start(bf16[16,128,512]{2,1,0:T(8,128)(2,1)S(1)} %all_to_all.42.ka_ref), channel_id=1, source_target_pairs={{0,1},{1,0},{2,3},{3,2},{4,5},{5,4},{6,7},{7,6},{8,9},{9,8},{10,11... | collective-permute-start | bytes 6291464 | tf_op jit(solution)/shard_map/ppermute | solution.py:132
  113.6 1.3 copy-start.6
  146.2 6.0 %copy-start.3 = (bf16[16,128,256]{2,1,0:T(8,128)(2,1)S(1)}, bf16[16,128,256]{2,1,0:T(8,128)(2,1)}, u32[]{:S(2)}) copy-start(bf16[16,128,256]{2,1,0:T(8,128)(2,1)} %get-tuple-element.9) | copy-start | bytes 3145732
  146.2 6.0 %collective-permute-start.4 = (bf16[16,128,256]{2,1,0:T(8,128)(2,1)}, bf16[16,128,256]{2,1,0:T(8,128)(2,1)S(1)}, u32[]{:S(2)}, u32[]{:S(2)}) collective-permute-start(bf16[16,128,256]{2,1,0:T(8,128)(2,1)} %get-tuple-element.10), channel_id=1, source_target_pairs={{0,1},{1,0},{2,3},{3,2},{4,5},{5,4},{6,7},{7,6},{8,9},{9,8},{10,11... | collective-permute-start | bytes 3145736 | tf_op jit(solution)/shard_map/ppermute | solution.py:132
  148.6 14.7 %all-to-all-start.4 = ((bf16[16,48,384]{2,1,0:T(8,128)(2,1)}), bf16[16,48,384]{2,1,0:T(8,128)(2,1)S(1)}, u32[]{:S(2)}, u32[]{:S(2)}) async-start(bf16[16,48,384]{2,1,0:T(8,128)(2,1)} %bitcast.67), calls=%async_computation.4 | async-start | bytes 1179648 | tf_op jit(solution)/shard_map/all_to_all | solution.py:185
  163.3 19.5 %all-to-all-start.5 = ((bf16[16,128,256]{2,1,0:T(8,128)(2,1)}), bf16[16,128,256]{2,1,0:T(8,128)(2,1)S(1)}, u32[]{:S(2)}, u32[]{:S(2)}) async-start(bf16[16,128,256]{2,1,0:T(8,128)(2,1)} %add_convert_fusion), calls=%async_computation.5 | async-start | bytes 2097152 | tf_op jit(solution)/shard_map/all_to_all | solution.py:185
  185.5 16.2 %all-to-all-start.6 = ((bf16[4,32,3200]{2,1,0:T(8,128)(2,1)}), bf16[4,32,3200]{2,1,0:T(8,128)(2,1)S(1)}, u32[]{:S(2)}, u32[]{:S(2)}) async-start(bf16[4,32,3200]{2,1,0:T(8,128)(2,1)} %reshape_reshape.14), calls=%async_computation.6 | async-start | bytes 1638400 | tf_op jit(solution)/shard_map/all_to_all | solution.py:171
  224.3 2.3 copy-start
  226.8 3.3 %collective-permute-start.5 = (bf16[256,2,1280]{2,0,1:T(8,128)(2,1)S(1)}, bf16[256,2,1280]{2,0,1:T(8,128)(2,1)}, u32[]{:S(2)}, u32[]{:S(2)}) collective-permute-start(bf16[256,2,1280]{2,0,1:T(8,128)(2,1)S(1)} %fusion.2), channel_id=1, source_target_pairs={{0,1},{1,0},{2,3},{3,2},{4,5},{5,4},{6,7},{7,6},{8,9},{9,8},{10,11... | collective-permute-start | bytes 3932168 | tf_op jit(solution)/shard_map/ppermute | solution.py:132
  233.3 20.6 %collective-permute-start.6 = (bf16[256,1280]{1,0:T(8,128)(2,1)}, bf16[256,1280]{1,0:T(8,128)(2,1)}, u32[]{:S(2)}, u32[]{:S(2)}) collective-permute-start(bf16[256,1280]{1,0:T(8,128)(2,1)} %fusion.12), channel_id=1, source_target_pairs={{0,2},{2,0},{1,3},{3,1},{4,6},{6,4},{5,7},{7,5},{8,10},{10,8},{9,1... | collective-permute-start | bytes 1966088 | tf_op jit(solution)/shard_map/ppermute | solution.py:132

commit v2 on v0

v2 whole, which is shorter than its diff:
```python
import functools

import jax
import jax.numpy as jnp
from jax import lax
from jax.experimental import pallas as pl
from jax.experimental.pallas import tpu as pltpu
from jax.sharding import Mesh, PartitionSpec as P

HD = 128
SCALE = HD ** (-0.5)
LOG2E = 1.4426950408889634
SUB = 16
SRC = 4
NT = (((1,), (1,)), ((), ()))
NN = (((1,), (0,)), ((), ()))


def dot(a, b, dims=NN):
    return lax.dot_general(a, b, dims, preferred_element_type=jnp.float32)


def piece(ref, j, first, count, lanes=slice(None)):
    block = ref[pl.ds(j * SRC, SRC), first:first + count, lanes]
    return block.reshape(SRC * count, block.shape[-1])


def key_rows(half, j, blocks, rows):
    start = (half * blocks + j * SRC) * rows
    return pl.ds(pl.multiple_of(start, SRC * rows), SRC * rows)


def weights_kernel(rows, z_ref, q_ref, ka_ref, kb_ref, p_ref, w_ref, s_scr, t_scr):
    blocks = ka_ref.shape[0]
    tile = p_ref.shape[1]
    qtq = q_ref[...].reshape(tile, 2 * HD)
    q = qtq[:, HD:]

    top = jnp.full((1, tile), -jnp.inf, jnp.float32)
    for half, ref in enumerate((ka_ref, kb_ref)):
        def scores(j, top, half=half, ref=ref):
            here = key_rows(half, j, blocks, rows)
            both = piece(ref, j, 0, rows)
            s = dot(both[:, :HD], q, NT)
            s_scr[here, :] = s
            t_scr[here, :] = dot(both, qtq, NT)
            return jnp.maximum(top, jnp.max(s, axis=0, keepdims=True))
        top = lax.fori_loop(0, blocks // SRC, scores, top)

    zero = jnp.zeros((1, tile), jnp.float32)

    def sums(j, carry):
        total, slope = carry
        here = key_rows(0, j, blocks, rows)
        e = jnp.exp2((s_scr[here, :] - top) * (SCALE * LOG2E))
        s_scr[here, :] = e
        total += jnp.sum(e, axis=0, keepdims=True)
        slope += jnp.sum(e * t_scr[here, :], axis=0, keepdims=True)
        return total, slope

    total, slope = lax.fori_loop(0, 2 * blocks // SRC, sums, (zero, zero))
    inv = 1.0 / total
    slope = slope * inv

    def store(j, carry):
        here = key_rows(0, j, blocks, rows)
        p = s_scr[here, :] * inv
        p_ref[here, :] = p.astype(jnp.bfloat16)
        w_ref[here, :] = (p * (t_scr[here, :] - slope)).astype(jnp.bfloat16)
        return carry

    lax.fori_loop(0, 2 * blocks // SRC, store, 0)


def values_kernel(rows, z_ref, g_ref, va_ref, vb_ref, p_ref, w_ref, out_ref, d_ref, vt_scr):
    blocks = va_ref.shape[0]
    tile = p_ref.shape[1]

    @pl.when(pl.program_id(0) == 0)
    def _():
        for half, ref in enumerate((va_ref, vb_ref)):
            def turn(j, carry, half=half, ref=ref):
                here = key_rows(half, j, blocks, rows)
                vt_scr[0:HD, here] = piece(ref, j, 0, rows).T
                vt_scr[HD:, here] = piece(ref, j, rows, rows).T
                return carry
            lax.fori_loop(0, blocks // SRC, turn, 0)

    def add(j, carry):
        both, tan = carry
        here = key_rows(0, j, blocks, rows)
        both += dot(vt_scr[:, here], p_ref[here, :])
        tan += dot(vt_scr[0:HD, here], w_ref[here, :])
        return both, tan

    zeros = jnp.zeros((2 * HD, tile), jnp.float32), jnp.zeros((HD, tile), jnp.float32)
    both, tan = lax.fori_loop(0, 2 * blocks // SRC, add, zeros)
    attn = both[0:HD].astype(jnp.bfloat16)
    g = g_ref[...].reshape(tile, HD)
    d_ref[...] = jnp.sum(attn.astype(jnp.float32) * g.astype(jnp.float32).T, axis=0, keepdims=True)
    out_ref[:, :, 0:HD] = both[0:HD].T.astype(jnp.bfloat16).reshape(-1, SUB, HD)
    out_ref[:, :, HD:] = (both[HD:] + SCALE * tan).T.astype(jnp.bfloat16).reshape(-1, SUB, HD)


def grads_kernel(rows, z_ref, q_ref, g_ref, ka_ref, kb_ref, va_ref, vb_ref, p_ref, d_ref, dq_ref, oa_ref, ob_ref, kt_scr, k_scr, v_scr):
    blocks = ka_ref.shape[0]
    tile = p_ref.shape[1]
    step = pl.program_id(0)
    q = q_ref[...].reshape(tile, 2 * HD)[:, HD:]
    g = g_ref[...].reshape(tile, HD)
    dsum = d_ref[...]

    @pl.when(step == 0)
    def _():
        for half, ref in enumerate((ka_ref, kb_ref)):
            def turn(j, carry, half=half, ref=ref):
                kt_scr[:, key_rows(half, j, blocks, rows)] = piece(ref, j, 0, rows, slice(0, HD)).T
                return carry
            lax.fori_loop(0, blocks // SRC, turn, 0)
        k_scr[...] = jnp.zeros_like(k_scr)
        v_scr[...] = jnp.zeros_like(v_scr)

    dq = jnp.zeros((HD, tile), jnp.float32)
    for half, ref in enumerate((va_ref, vb_ref)):
        def add(j, dq, half=half, ref=ref):
            here = key_rows(half, j, blocks, rows)
            p = p_ref[here, :]
            slopes = dot(piece(ref, j, 0, rows), g, NT) - dsum
            ds = (p.astype(jnp.float32) * slopes).astype(jnp.bfloat16)
            k_scr[here, :] += dot(ds, q)
            v_scr[here, :] += dot(p, g)
            return dq + dot(kt_scr[:, here], ds)
        dq = lax.fori_loop(0, blocks // SRC, add, dq)
    dq_ref[...] = (SCALE * dq).T.astype(jnp.bfloat16).reshape(-1, SUB, HD)

    @pl.when(step == pl.num_programs(0) - 1)
    def _():
        for half, ref in enumerate((oa_ref, ob_ref)):
            def give(j, carry, half=half, ref=ref):
                here = key_rows(half, j, blocks, rows)
                group = pl.ds(j * SRC, SRC)
                ref[group, 0:rows, :] = (SCALE * k_scr[here, :]).astype(jnp.bfloat16).reshape(SRC, rows, HD)
                ref[group, rows:, :] = v_scr[here, :].astype(jnp.bfloat16).reshape(SRC, rows, HD)
                return carry
            lax.fori_loop(0, blocks // SRC, give, 0)


def whole(array):
    return pl.BlockSpec(array.shape, lambda i, s: (0,) * len(array.shape))


def kernel_call(body, name, grid, scalars, ins, outs, scratch, flops=0, bytes_accessed=4 * 2**20):
    arrays, in_specs = zip(*ins)
    shapes, out_specs = zip(*outs)
    return pl.pallas_call(
        body,
        grid_spec=pltpu.PrefetchScalarGridSpec(
            num_scalar_prefetch=1,
            grid=(grid,),
            in_specs=list(in_specs),
            out_specs=list(out_specs),
            scratch_shapes=scratch,
        ),
        out_shape=list(shapes),
        name=name,
        compiler_params=pltpu.CompilerParams(vmem_limit_bytes=52 * 2**20),
        cost_estimate=pl.CostEstimate(flops=flops, bytes_accessed=bytes_accessed, transcendentals=0),
    )(scalars, *arrays)


def specs(blocks, rows, window):
    tile = blocks * SUB
    keys = 2 * blocks * rows
    q_spec = pl.BlockSpec((blocks, SUB, 2 * HD), lambda i, s: (0, rows // SUB + i, 0))
    g_spec = pl.BlockSpec((blocks, SUB, HD), lambda i, s: (0, 2 * rows // SUB + i, 0))
    p_spec = pl.BlockSpec((keys, tile), lambda i, s: (0, i))
    d_spec = pl.BlockSpec((1, tile), lambda i, s: (0, i))
    return q_spec, g_spec, p_spec, d_spec, keys, tile, window // SUB


def attention_weights(z, recv_k, other_k, rows, window):
    q_spec, _, p_spec, _, keys, tile, grid = specs(recv_k.shape[0], rows, window)
    p_shape = jax.ShapeDtypeStruct((keys, grid * tile), jnp.bfloat16)
    return kernel_call(
        functools.partial(weights_kernel, rows), "weights", grid, z,
        [(recv_k, q_spec), (recv_k, whole(recv_k)), (other_k, whole(other_k))],
        [(p_shape, p_spec), (p_shape, p_spec)],
        [pltpu.VMEM((keys, tile), jnp.float32), pltpu.VMEM((keys, tile), jnp.float32)],
        8 * keys * grid * tile * HD, 32 * 2**20)


def attention_values(z, recv_v, other_v, probs, weights, rows, window):
    blocks = recv_v.shape[0]
    _, g_spec, p_spec, d_spec, keys, tile, grid = specs(blocks, rows, window)
    out_shape = jax.ShapeDtypeStruct((blocks, window, 2 * HD), jnp.bfloat16)
    d_shape = jax.ShapeDtypeStruct((1, grid * tile), jnp.float32)
    return kernel_call(
        functools.partial(values_kernel, rows), "values", grid, z,
        [(recv_v, g_spec), (recv_v, whole(recv_v)), (other_v, whole(other_v)), (probs, p_spec), (weights, p_spec)],
        [(out_shape, pl.BlockSpec((blocks, SUB, 2 * HD), lambda i, s: (0, i, 0))), (d_shape, d_spec)],
        [pltpu.VMEM((2 * HD, keys), jnp.bfloat16)],
        6 * keys * grid * tile * HD, 16 * 2**20)


def attention_grads(z, recv_k, other_k, recv_v, other_v, probs, dsum, rows, window):
    blocks = recv_v.shape[0]
    q_spec, g_spec, p_spec, d_spec, keys, tile, grid = specs(blocks, rows, window)
    dq_shape = jax.ShapeDtypeStruct((blocks, window, HD), jnp.bfloat16)
    shape = jax.ShapeDtypeStruct((blocks, 2 * rows, HD), jnp.bfloat16)
    return kernel_call(
        functools.partial(grads_kernel, rows), "grads", grid, z,
        [(recv_k, q_spec), (recv_v, g_spec), (recv_k, whole(recv_k)), (other_k, whole(other_k)),
         (recv_v, whole(recv_v)), (other_v, whole(other_v)), (probs, p_spec), (dsum, d_spec)],
        [(dq_shape, pl.BlockSpec((blocks, SUB, HD), lambda i, s: (0, i, 0))),
         (shape, whole(shape)), (shape, whole(shape))],
        [pltpu.VMEM((HD, keys), jnp.bfloat16), pltpu.VMEM((keys, HD), jnp.float32), pltpu.VMEM((keys, HD), jnp.float32)],
        10 * keys * grid * tile * HD, 32 * 2**20)


THIRDS = 3
SWAP = [(0, 1), (1, 0)]


def swap(array, axis):
    return lax.ppermute(array, axis, SWAP)


def plane_routes(planes):
    routes = []
    for d in range(planes):
        route = []
        for z in range(planes):
            for c in range(2):
                slot = (z + d) % planes
                route.append((z * 2 + c, (2 * c + slot // 2) * 2 + slot % 2))
        routes.append(route)
    return routes


def to_plane(pieces):
    return [lax.ppermute(a, ("z", "c"), route) for a, route in zip(pieces, plane_routes(len(pieces)))]


def from_plane(pieces):
    routes = plane_routes(len(pieces))
    return [lax.ppermute(a, ("z", "c"), [(b, a) for a, b in route]) for a, route in zip(pieces, routes)]


def over_chips(array):
    return lax.all_to_all(array, ("x", "y"), 0, 0, tiled=True)


def slot_of(z_ref, d, count):
    slot = lax.rem(z_ref[0] + d, count)
    return slot // 2, lax.rem(slot, 2)


def split_kernel(kinds, z_ref, *refs):
    outs = refs[kinds:]
    _, tokens, width = refs[0].shape
    half_rows = tokens // 2
    for d, out in enumerate(outs):
        clip, half = slot_of(z_ref, d, len(outs))
        for index, ref in enumerate(refs[:kinds]):
            start = pl.multiple_of(half * half_rows, half_rows)
            out[:, index * width:(index + 1) * width] = ref[clip, pl.ds(start, half_rows), :]


def split_slots(name, z, arrays):
    clips, tokens, width = arrays[0].shape
    shape = jax.ShapeDtypeStruct((tokens // 2, len(arrays) * width), jnp.bfloat16)
    return kernel_call(
        functools.partial(split_kernel, len(arrays)), name, 1, z,
        [(a, whole(a)) for a in arrays], [(shape, whole(shape))] * (2 * clips), [])


def join_kernel(kinds, z_ref, *refs):
    ins, outs = refs[:-kinds], refs[-kinds:]
    half_rows = ins[0].shape[0]
    width = outs[0].shape[2]
    for d, ref in enumerate(ins):
        clip, half = slot_of(z_ref, d, len(ins))
        for index, out in enumerate(outs):
            start = pl.multiple_of(half * half_rows, half_rows)
            out[clip, pl.ds(start, half_rows), :] = ref[:, index * width:(index + 1) * width]


def join_slots(name, z, pieces, kinds, clips):
    rows, width = pieces[0].shape
    shape = jax.ShapeDtypeStruct((clips, 2 * rows, width // kinds), jnp.bfloat16)
    return kernel_call(
        functools.partial(join_kernel, kinds), name, 1, z,
        [(a, whole(a)) for a in pieces], [(shape, whole(shape))] * kinds, [])


def keys_kernel(heads, z_ref, *refs):
    ins, out = refs[:-1], refs[-1]
    part = ins[0].shape[0]
    rows = part * len(ins)
    window = out.shape[1] - rows
    width = heads * HD
    for head in range(heads):
        for kind in range(4):
            source = slice(kind * width + head * HD, kind * width + (head + 1) * HD)
            lanes = slice((kind % 2) * HD, (kind % 2 + 1) * HD)
            whole_block = jnp.concatenate([ref[:, source] for ref in ins], axis=0)
            for third in range(THIRDS):
                chip = head * THIRDS + third
                if kind < 2:
                    out[chip, 0:rows, lanes] = whole_block
                else:
                    first = third * window
                    count = min(window, rows - first)
                    out[chip, rows:rows + count, lanes] = whole_block[first:first + count]
                    if count < window:
                        out[chip, rows + count:, lanes] = jnp.zeros((window - count, HD), out.dtype)
    for chip in range(heads * THIRDS, out.shape[0]):
        out[chip] = jnp.zeros(out.shape[1:], out.dtype)


def values_pack_kernel(heads, z_ref, *refs):
    ins, out = refs[:-1], refs[-1]
    rows = ins[0].shape[0] * len(ins)
    window = out.shape[1] - 2 * rows
    width = heads * HD
    for head in range(heads):
        for kind in range(3):
            source = slice(kind * width + head * HD, kind * width + (head + 1) * HD)
            whole_block = jnp.concatenate([ref[:, source] for ref in ins], axis=0)
            for third in range(THIRDS):
                chip = head * THIRDS + third
                if kind < 2:
                    out[chip, kind * rows:(kind + 1) * rows, :] = whole_block
                else:
                    first = third * window
                    count = min(window, rows - first)
                    out[chip, 2 * rows:2 * rows + count, :] = whole_block[first:first + count]
                    if count < window:
                        out[chip, 2 * rows + count:, :] = jnp.zeros((window - count, HD), out.dtype)
    for chip in range(heads * THIRDS, out.shape[0]):
        out[chip] = jnp.zeros(out.shape[1:], out.dtype)


def out_unpack_kernel(heads, z_ref, back_ref, *outs):
    part = outs[0].shape[0]
    window = back_ref.shape[1]
    rows = part * len(outs)
    width = heads * HD
    for head in range(heads):
        for kind in range(2):
            lanes = slice(kind * HD, (kind + 1) * HD)
            pieces = [
                back_ref[head * THIRDS + third, 0:min(window, rows - third * window), lanes]
                for third in range(THIRDS)
            ]
            column = jnp.concatenate(pieces, axis=0)
            for d, out in enumerate(outs):
                out[:, kind * width + head * HD:kind * width + (head + 1) * HD] = column[d * part:(d + 1) * part]


def grads_unpack_kernel(heads, z_ref, back_ref, *outs):
    part = outs[0].shape[0]
    rows = part * len(outs)
    window = back_ref.shape[1] - 2 * rows
    width = heads * HD
    for head in range(heads):
        for kind in range(3):
            chips = [head * THIRDS + third for third in range(THIRDS)]
            if kind < 2:
                column = sum(
                    back_ref[chip, kind * rows:(kind + 1) * rows, :].astype(jnp.float32) for chip in chips
                ).astype(jnp.bfloat16)
            else:
                column = jnp.concatenate([
                    back_ref[chip, 2 * rows:2 * rows + min(window, rows - third * window), :]
                    for third, chip in enumerate(chips)
                ], axis=0)
            for d, out in enumerate(outs):
                out[:, kind * width + head * HD:kind * width + (head + 1) * HD] = column[d * part:(d + 1) * part]


def merge_kernel(z_ref, own_ref, got_ref, dq_ref, out_ref):
    rows = got_ref.shape[1]
    total = own_ref[...].astype(jnp.float32) + got_ref[...].astype(jnp.float32)
    out_ref[:, 0:rows, :] = total.astype(jnp.bfloat16)
    out_ref[:, rows:, :] = dq_ref[...]


def repack(body, name, z, ins, shapes):
    shapes = [jax.ShapeDtypeStruct(s, jnp.bfloat16) for s in shapes]
    return kernel_call(body, name, 1, z, [(a, whole(a)) for a in ins], [(s, whole(s)) for s in shapes], [])


def local(queries, keys, values, queries_tan, keys_tan, values_tan, w_out, grad_out):
    w, c = lax.axis_index("w"), lax.axis_index("c")
    z = lax.axis_index("z").astype(jnp.int32).reshape(1)
    clips, tokens, features = queries.shape
    heads = features // HD
    chips = lax.axis_size(("x", "y"))
    slots = 2 * clips
    rows = slots * tokens // 2
    window = pl.cdiv(pl.cdiv(rows, THIRDS), SUB) * SUB

    far = swap(grad_out, "w")
    near = swap(grad_out, "c")
    split = split_slots("split_keys", z, (keys, keys_tan, queries_tan, queries))
    split, far = lax.optimization_barrier((split, far))
    plane = to_plane(split)
    cross = swap(far, "c")
    width = grad_out.shape[2]
    w_own, w_near, w_far, w_cross = blocks = [
        lax.dynamic_slice_in_dim(w_out, ((w ^ i) * 2 + (c ^ j)) * width, width, axis=1)
        for i in range(2) for j in range(2)
    ]
    cot = sum(
        jnp.einsum("btf,cf->btc", grad, part, preferred_element_type=jnp.float32)
        for grad, part in zip((grad_out, near, far, cross), blocks)
    ).astype(jnp.bfloat16)
    split = split_slots("split_values", z, (values, values_tan, cot))
    plane, split = lax.optimization_barrier((plane, split))
    plane_v = to_plane(split)

    packed = repack(functools.partial(keys_kernel, heads), "pack_keys", z, plane, [(chips, rows + window, 2 * HD)])[0]
    recv_k = over_chips(packed)
    recv_k, plane_v = lax.optimization_barrier((recv_k, plane_v))
    other_k = swap(recv_k, "c")
    packed = repack(functools.partial(values_pack_kernel, heads), "pack_values", z, plane_v, [(chips, 2 * rows + window, HD)])[0]
    recv_v = over_chips(packed)

    probs, weights = attention_weights(z, recv_k, other_k, rows, window)
    recv_v, probs, weights = lax.optimization_barrier((recv_v, probs, weights))
    other_v = swap(recv_v, "c")
    out, dsum = attention_values(z, recv_v, other_v, probs, weights, rows, window)
    back = over_chips(out)
    dq, own_grads, other_grads = attention_grads(z, recv_k, other_k, recv_v, other_v, probs, dsum, rows, window)
    back, dq, own_grads, other_grads = lax.optimization_barrier((back, dq, own_grads, other_grads))
    got = swap(other_grads, "c")
    merged = repack(merge_kernel, "merge", z, [own_grads, got, dq], [(chips, 2 * rows + window, HD)])[0]
    back, merged = lax.optimization_barrier((back, merged))

    shapes = [(tokens // 2, 2 * features)] * slots
    home = from_plane(repack(functools.partial(out_unpack_kernel, heads), "unpack_out", z, [back], shapes))
    grads = over_chips(merged)
    home, grads = lax.optimization_barrier((home, grads))
    attn, attn_tan = join_slots("join_out", z, home, 2, clips)
    both = jnp.concatenate([attn, attn_tan], axis=0).reshape(2 * clips * tokens, features)

    def project(part):
        return jnp.dot(both, part, preferred_element_type=jnp.float32)

    give = swap(jnp.concatenate([project(w_near), project(w_cross)], axis=1).astype(jnp.bfloat16), "c")
    give = give.astype(jnp.float32)
    got = swap((project(w_far) + give[:, width:]).astype(jnp.bfloat16), "w")
    outs = (project(w_own) + give[:, :width] + got.astype(jnp.float32)).astype(jnp.bfloat16)
    outs = outs.reshape(2, clips, tokens, -1)

    shapes = [(tokens // 2, 3 * features)] * slots
    home = from_plane(repack(functools.partial(grads_unpack_kernel, heads), "unpack_grads", z, [grads], shapes))
    grad_k, grad_v, grad_q = join_slots("join_grads", z, home, 3, clips)
    return outs[0], outs[1], grad_q, grad_k, grad_v


def solution(mesh):
    seq, tp = ("x", "y", "z"), ("w", "c")
    fine = Mesh(mesh.devices.reshape(4, 4, 4, 2, 2), seq + tp)
    split = P(None, seq, tp)
    return jax.shard_map(
        local,
        mesh=fine,
        in_specs=(split,) * 6 + (P(tp, None), split),
        out_specs=(split,) * 5,
        check_vma=False,
    )
```

time: 1220 us -> 211 us (0.17); the launches traced: 1190 us -> 210 us
  blocking collectives: 534 us -> 0 us
  waiting for transfers between devices: 347 us -> 45.1 us
  local copies, waits for them, and re-layouts: 171 us -> 6.58 us
  matrix products: 125 us -> 16.9 us
  starting transfers between devices: 0.55 us -> 87.1 us
  Pallas kernels: 0 us -> 52.2 us
  between operations: 14 us -> 1.06 us
    all_gather x2 -> x0, blocking collectives: 534 us -> none  [the longest x1 296 us: local(): lax.all_gather(lse_rows, 'seq', axis=1, tiled=True)]
    all_gather x7 -> x0, waiting for transfers between devices: 310 us -> none  [the longest x1 117 us: local(): lax.all_gather(values, 'seq', axis=1, tiled=True)]
    all_gather x6 -> x0, local copies, waits for them, and re-layouts: 147 us -> none  [the longest x1 26.5 us: local(): lax.all_gather(keys_tan, 'seq', axis=1, tiled=True)]
    dot_general x13 -> x8, matrix products: 125 us -> 16.9 us  [the longest x4 8.47 us: project(): return jnp.dot(both, part, preferred_element_type=jnp.float32)]
    ppermute x0 -> x24, starting transfers between devices: none -> 66.3 us  [the longest x8 28 us: from_plane(): lax.ppermute(a, ('z', 'c'), [(b, a) for a, b in route])]
    pallas_call x0 -> x12, Pallas kernels: none -> 52.2 us  [kernel_call(): pl.pallas_call(body, grid_spec=pltpu.PrefetchScalarGridSpec(num_scalar_pr...]
    ppermute x0 -> x24, waiting for transfers between devices: none -> 39.3 us  [the longest x8 16.7 us: from_plane(): lax.ppermute(a, ('z', 'c'), [(b, a) for a, b in route])]
    reduce_scatter x2 -> x0, waiting for transfers between devices: 36.4 us -> none  [the longest x1 36.4 us: local(): lax.psum_scatter(partial_tan.astype(jnp.bfloat16), 'tp', scatter_dimensio...]
  transfers between devices with their start and end apart: 9 -> 28, of which waited for: 5 -> 15; matrix products, arithmetic and copies ran while one was open for 25% -> 5% of each run, Pallas kernels for 0% -> 17%
where the time goes in v2:
time: 211 us; the launch traced here: 210 us
  starting transfers between devices  87.1 us (41%)
  Pallas kernels  52.2 us (25%)
  waiting for transfers between devices  45.1 us (21%)
  matrix products  16.9 us (8%)
  local copies, waits for them, and re-layouts  6.58 us (3%)
    pallas_call x12, Pallas kernels, kernel_call(): pl.pallas_call(body, grid_spec=pltpu.PrefetchScalarGridSpec(num_scalar_pr...  52.2 us
    ppermute x8, starting transfers between devices, from_plane(): lax.ppermute(a, ('z', 'c'), [(b, a) for a, b in route])  28 us
    ppermute x8, starting transfers between devices, to_plane(): lax.ppermute(a, ('z', 'c'), route)  25.8 us
    all_to_all x4, starting transfers between devices, over_chips(): return lax.all_to_all(array, ('x', 'y'), 0, 0, tiled=True)  20.9 us
    ppermute x8, waiting for transfers between devices, from_plane(): lax.ppermute(a, ('z', 'c'), [(b, a) for a, b in route])  16.7 us
    ppermute x8, waiting for transfers between devices, to_plane(): lax.ppermute(a, ('z', 'c'), route)  12.8 us
    ppermute x8, starting transfers between devices, swap(): return lax.ppermute(array, axis, SWAP)  12.5 us
    ppermute x8, waiting for transfers between devices, swap(): return lax.ppermute(array, axis, SWAP)  9.76 us
  transfers between devices with their start and end apart: 28, of which 15 were waited for; matrix products, arithmetic and copies ran while one was open for 5% of the time, Pallas kernels for 17%

profile of v2, /device:TPU:1, one launch (start us, length us, event | category | flops | bytes accessed | tf_op | source)
XLA Modules:
  0.0 209.7 jit_solution(18215334383994025089)
XLA Ops:
  14.2 8.5 %collective-permute-start.1 = (bf16[32,2560]{1,0:T(8,128)(2,1)S(1)}, bf16[32,2560]{1,0:T(8,128)(2,1)S(1)}, u32[]{:S(2)}, u32[]{:S(2)}) collective-permute-start(bf16[32,2560]{1,0:T(8,128)(2,1)S(1)} %get-tuple-element.69), channel_id=1, source_target_pairs={{0,0},{1,8},{4,1},{5,9},{8,4},{9,12},{12,5},{13,13},{2,2},{3,10},{... | collective-permute-start | bytes 491528 | tf_op jit(solution)/shard_map/ppermute | solution.py:241
  22.7 3.1 %collective-permute-start.2 = (bf16[32,2560]{1,0:T(8,128)(2,1)S(1)}, bf16[32,2560]{1,0:T(8,128)(2,1)S(1)}, u32[]{:S(2)}, u32[]{:S(2)}) collective-permute-start(bf16[32,2560]{1,0:T(8,128)(2,1)S(1)} %get-tuple-element.70), channel_id=1, source_target_pairs={{0,1},{1,9},{4,4},{5,12},{8,5},{9,13},{12,0},{13,8},{2,3},{3,11},{... | collective-permute-start | bytes 491528 | tf_op jit(solution)/shard_map/ppermute | solution.py:241
  37.0 2.6 %collective-permute-done.4.refs_3_ = bf16[32,2560]{1,0:T(8,128)(2,1)S(1)} collective-permute-done((bf16[32,2560]{1,0:T(8,128)(2,1)S(1)}, bf16[32,2560]{1,0:T(8,128)(2,1)S(1)}, u32[]{:S(2)}, u32[]{:S(2)}) %collective-permute-start.4) | collective-permute-done | bytes 163872 | tf_op jit(solution)/shard_map/ppermute | solution.py:241
  40.9 6.8 %all-to-all-start = ((bf16[16,176,256]{2,1,0:T(8,128)(2,1)}), bf16[16,176,256]{2,1,0:T(8,128)(2,1)S(1)}, u32[]{:S(2)}, u32[]{:S(2)}) async-start(bf16[16,176,256]{2,1,0:T(8,128)(2,1)} %pack_keys.1), calls=%async_computation | async-start | bytes 2883584 | tf_op jit(solution)/shard_map/all_to_all | solution.py:250
  47.7 5.1 %collective-permute-start.7 = (bf16[32,1920]{1,0:T(8,128)(2,1)S(1)}, bf16[32,1920]{1,0:T(8,128)(2,1)S(1)}, u32[]{:S(2)}, u32[]{:S(2)}) collective-permute-start(bf16[32,1920]{1,0:T(8,128)(2,1)S(1)} %get-tuple-element.82), channel_id=1, source_target_pairs={{0,0},{1,8},{4,1},{5,9},{8,4},{9,12},{12,5},{13,13},{2,2},{3,10},{... | collective-permute-start | bytes 368648 | tf_op jit(solution)/shard_map/ppermute | solution.py:241
  52.8 3.0 %collective-permute-start.8 = (bf16[32,1920]{1,0:T(8,128)(2,1)S(1)}, bf16[32,1920]{1,0:T(8,128)(2,1)S(1)}, u32[]{:S(2)}, u32[]{:S(2)}) collective-permute-start(bf16[32,1920]{1,0:T(8,128)(2,1)S(1)} %get-tuple-element.83), channel_id=1, source_target_pairs={{0,1},{1,9},{4,4},{5,12},{8,5},{9,13},{12,0},{13,8},{2,3},{3,11},{... | collective-permute-start | bytes 368648 | tf_op jit(solution)/shard_map/ppermute | solution.py:241
  55.9 3.7 %collective-permute-start.10 = (bf16[32,1920]{1,0:T(8,128)(2,1)S(1)}, bf16[32,1920]{1,0:T(8,128)(2,1)S(1)}, u32[]{:S(2)}, u32[]{:S(2)}) collective-permute-start(bf16[32,1920]{1,0:T(8,128)(2,1)S(1)} %get-tuple-element.85), channel_id=1, source_target_pairs={{0,5},{1,13},{4,0},{5,8},{8,1},{9,9},{12,4},{13,12},{2,7},{3,15},{... | collective-permute-start | bytes 368648 | tf_op jit(solution)/shard_map/ppermute | solution.py:241
  60.1 2.7 %collective-permute-done.9.refs_2_ = bf16[32,1920]{1,0:T(8,128)(2,1)S(1)} collective-permute-done((bf16[32,1920]{1,0:T(8,128)(2,1)S(1)}, bf16[32,1920]{1,0:T(8,128)(2,1)S(1)}, u32[]{:S(2)}, u32[]{:S(2)}) %collective-permute-start.9) | collective-permute-done | bytes 122912 | tf_op jit(solution)/shard_map/ppermute | solution.py:241
  62.8 4.6 %collective-permute-done.10.refs_3_ = bf16[32,1920]{1,0:T(8,128)(2,1)S(1)} collective-permute-done((bf16[32,1920]{1,0:T(8,128)(2,1)S(1)}, bf16[32,1920]{1,0:T(8,128)(2,1)S(1)}, u32[]{:S(2)}, u32[]{:S(2)}) %collective-permute-start.10) | collective-permute-done | bytes 122912 | tf_op jit(solution)/shard_map/ppermute | solution.py:241
  72.4 3.7 %all-to-all-start.1 = ((bf16[16,304,128]{2,1,0:T(8,128)(2,1)}), bf16[16,304,128]{2,1,0:T(8,128)(2,1)S(1)}, u32[]{:S(2)}, u32[]{:S(2)}) async-start(bf16[16,304,128]{2,1,0:T(8,128)(2,1)} %pack_values.1), calls=%async_computation.1 | async-start | bytes 2490368 | tf_op jit(solution)/shard_map/all_to_all | solution.py:250
  76.1 16.1 %weights.1 = (bf16[4096,768]{1,0:T(8,128)(2,1)}, bf16[4096,768]{1,0:T(8,128)(2,1)}) custom-call(s32[1]{0:T(128)} %bitcast.z_ref, bf16[16,176,256]{2,1,0:T(8,128)(2,1)S(1)} %all-to-all-done.q_ref.ka_ref, bf16[16,176,256]{2,1,0:T(8,128)(2,1)S(1)} %all-to-all-done.q_ref.ka_ref, bf16[16,176,256]{2,1,0:T(8,128)(2,1)} %collective-permute-done.11.kb_ref), custom_call_target="tpu_custom_call" | custom-call | flops 3221225472 | bytes 33554432 | tf_op jit(solution)/shard_map/weights/pallas_call | solution.py:155
  92.2 3.9 %all-to-all-done.1.g_ref.va_ref = bf16[16,304,128]{2,1,0:T(8,128)(2,1)S(1)} async-done(((bf16[16,304,128]{2,1,0:T(8,128)(2,1)}), bf16[16,304,128]{2,1,0:T(8,128)(2,1)S(1)}, u32[]{:S(2)}, u32[]{:S(2)}) %all-to-all-start.1) | async-done | bytes 1245216 | tf_op jit(solution)/shard_map/all_to_all | solution.py:250
  101.0 12.1 %values.1 = (bf16[16,48,256]{2,1,0:T(8,128)(2,1)}, f32[1,768]{1,0:T(1,128)S(1)}) custom-call(s32[1]{0:T(128)} %bitcast.z_ref, bf16[16,304,128]{2,1,0:T(8,128)(2,1)S(1)} %all-to-all-done.1.g_ref.va_ref, bf16[16,304,128]{2,1,0:T(8,128)(2,1)S(1)} %all-to-all-done.1.g_ref.va_ref, bf16[16,304,128]{2,1,0:T(8,128)(2,1)} %copy-done.8, ...), custom_call_target="tpu_custom_call" | custom-call | flops 2415919104 | bytes 16777216 | tf_op jit(solution)/shard_map/values/pallas_call | solution.py:155
  113.1 3.6 %all-to-all-start.2 = ((bf16[16,48,256]{2,1,0:T(8,128)(2,1)}), bf16[16,48,256]{2,1,0:T(8,128)(2,1)S(1)}, u32[]{:S(2)}, u32[]{:S(2)}) async-start(bf16[16,48,256]{2,1,0:T(8,128)(2,1)} %get-tuple-element.96), calls=%async_computation.2 | async-start | bytes 786432 | tf_op jit(solution)/shard_map/all_to_all | solution.py:250
  116.6 17.8 %grads.1 = (bf16[16,48,128]{2,1,0:T(8,128)(2,1)S(1)}, bf16[16,256,128]{2,1,0:T(8,128)(2,1)S(1)}, bf16[16,256,128]{2,1,0:T(8,128)(2,1)}) custom-call(s32[1]{0:T(128)} %bitcast.z_ref, bf16[16,176,256]{2,1,0:T(8,128)(2,1)} %copy-done.1, bf16[16,304,128]{2,1,0:T(8,128)(2,1)} %copy-done, bf16[16,176,256]{2,1,0:T(8,128)(2,1)} %copy-done.1, ...), custom_call_target="tpu_custom_call" | custom-call | flops 4026531840 | bytes 33554432 | tf_op jit(solution)/shard_map/grads/pallas_call | solution.py:155
  140.9 6.8 %all-to-all-start.3 = ((bf16[16,304,128]{2,1,0:T(8,128)(2,1)}), bf16[16,304,128]{2,1,0:T(8,128)(2,1)S(1)}, u32[]{:S(2)}, u32[]{:S(2)}) async-start(bf16[16,304,128]{2,1,0:T(8,128)(2,1)} %merge.1), calls=%async_computation.3 | async-start | bytes 2490368 | tf_op jit(solution)/shard_map/all_to_all | solution.py:250
  147.8 3.7 %collective-permute-start.14 = (bf16[32,1280]{1,0:T(8,128)(2,1)S(1)}, bf16[32,1280]{1,0:T(8,128)(2,1)S(1)}, u32[]{:S(2)}, u32[]{:S(2)}) collective-permute-start(bf16[32,1280]{1,0:T(8,128)(2,1)S(1)} %get-tuple-element.106), channel_id=1, source_target_pairs={{0,0},{8,1},{1,4},{9,5},{4,8},{12,9},{5,12},{13,13},{2,2},{10,3},{... | collective-permute-start | bytes 245768 | tf_op jit(solution)/shard_map/ppermute | solution.py:246
  153.5 7.4 %collective-permute-start.16 = (bf16[32,1280]{1,0:T(8,128)(2,1)S(1)}, bf16[32,1280]{1,0:T(8,128)(2,1)S(1)}, u32[]{:S(2)}, u32[]{:S(2)}) collective-permute-start(bf16[32,1280]{1,0:T(8,128)(2,1)S(1)} %get-tuple-element.108), channel_id=1, source_target_pairs={{4,0},{12,1},{5,4},{13,5},{0,8},{8,9},{1,12},{9,13},{6,2},{14,3},{... | collective-permute-start | bytes 245768 | tf_op jit(solution)/shard_map/ppermute | solution.py:246
  162.9 3.6 %collective-permute-done.16.refs_2_ = bf16[32,1280]{1,0:T(8,128)(2,1)S(1)} collective-permute-done((bf16[32,1280]{1,0:T(8,128)(2,1)S(1)}, bf16[32,1280]{1,0:T(8,128)(2,1)S(1)}, u32[]{:S(2)}, u32[]{:S(2)}) %collective-permute-start.16) | collective-permute-done | bytes 81952 | tf_op jit(solution)/shard_map/ppermute | solution.py:246
  173.3 2.7 %collective-permute-done.18 = bf16[256,2560]{1,0:T(8,128)(2,1)S(1)} collective-permute-done((bf16[256,2560]{1,0:T(8,128)(2,1)S(1)}, bf16[256,2560]{1,0:T(8,128)(2,1)S(1)}, u32[]{:S(2)}, u32[]{:S(2)}) %collective-permute-start.18) | collective-permute-done | bytes 1310752 | tf_op jit(solution)/shard_map/ppermute | solution.py:225
  178.4 2.8 %collective-permute-start.19 = (bf16[256,1280]{1,0:T(8,128)(2,1)S(1)}, bf16[256,1280]{1,0:T(8,128)(2,1)S(1)}, u32[]{:S(2)}, u32[]{:S(2)}) collective-permute-start(bf16[256,1280]{1,0:T(8,128)(2,1)S(1)} %fusion.18), channel_id=1, source_target_pairs={{0,2},{2,0},{1,3},{3,1},{4,6},{6,4},{5,7},{7,5},{8,10},{10,8},{9,1... | collective-permute-start | bytes 1966088 | tf_op jit(solution)/shard_map/ppermute | solution.py:225
  185.9 6.5 %collective-permute-start.22 = (bf16[32,1920]{1,0:T(8,128)(2,1)S(1)}, bf16[32,1920]{1,0:T(8,128)(2,1)S(1)}, u32[]{:S(2)}, u32[]{:S(2)}) collective-permute-start(bf16[32,1920]{1,0:T(8,128)(2,1)S(1)} %get-tuple-element.120), channel_id=1, source_target_pairs={{4,0},{12,1},{5,4},{13,5},{0,8},{8,9},{1,12},{9,13},{6,2},{14,3},{... | collective-permute-start | bytes 368648 | tf_op jit(solution)/shard_map/ppermute | solution.py:246
  196.4 8.1 %collective-permute-done.20.refs_0_ = bf16[32,1920]{1,0:T(8,128)(2,1)S(1)} collective-permute-done((bf16[32,1920]{1,0:T(8,128)(2,1)S(1)}, bf16[32,1920]{1,0:T(8,128)(2,1)S(1)}, u32[]{:S(2)}, u32[]{:S(2)}) %collective-permute-start.20) | collective-permute-done | bytes 122912 | tf_op jit(solution)/shard_map/ppermute | solution.py:246
  204.6 3.1 %collective-permute-done.22.refs_2_ = bf16[32,1920]{1,0:T(8,128)(2,1)S(1)} collective-permute-done((bf16[32,1920]{1,0:T(8,128)(2,1)S(1)}, bf16[32,1920]{1,0:T(8,128)(2,1)S(1)}, u32[]{:S(2)}, u32[]{:S(2)}) %collective-permute-start.22) | collective-permute-done | bytes 122912 | tf_op jit(solution)/shard_map/ppermute | solution.py:246
  (77 shorter events, 66.5 us)
Async XLA Ops:
  0.6 9.2 %collective-permute-start = (bf16[2,64,1280]{2,1,0:T(8,128)(2,1)}, bf16[2,64,1280]{2,1,0:T(8,128)(2,1)S(1)}, u32[]{:S(2)}, u32[]{:S(2)}) collective-permute-start(bf16[2,64,1280]{2,1,0:T(8,128)(2,1)} %param.15), channel_id=1, source_target_pairs={{0,2},{2,0},{1,3},{3,1},{4,6},{6,4},{5,7},{7,5},{8,10},{10,8},{9,1... | collective-permute-start | bytes 983048 | tf_op jit(solution)/shard_map/ppermute | solution.py:225
  3.2 29.1 %collective-permute-start.5 = (bf16[2,64,1280]{2,1,0:T(8,128)(2,1)}, bf16[2,64,1280]{2,1,0:T(8,128)(2,1)S(1)}, u32[]{:S(2)}, u32[]{:S(2)}) collective-permute-start(bf16[2,64,1280]{2,1,0:T(8,128)(2,1)} %param.15), channel_id=1, source_target_pairs={{0,1},{1,0},{2,3},{3,2},{4,5},{5,4},{6,7},{7,6},{8,9},{9,8},{10,11... | collective-permute-start | bytes 983048 | tf_op jit(solution)/shard_map/ppermute | solution.py:225
  9.9 18.1 %collective-permute-start.6 = (bf16[2,64,1280]{2,1,0:T(8,128)(2,1)S(1)}, bf16[2,64,1280]{2,1,0:T(8,128)(2,1)S(1)}, u32[]{:S(2)}, u32[]{:S(2)}) collective-permute-start(bf16[2,64,1280]{2,1,0:T(8,128)(2,1)S(1)} %collective-permute-done), channel_id=1, source_target_pairs={{0,1},{1,0},{2,3},{3,2},{4,5},{5,4},{6,7},{7,6},{8,9},{9,8},{10,11... | collective-permute-start | bytes 983048 | tf_op jit(solution)/shard_map/ppermute | solution.py:225
  14.2 20.4 %collective-permute-start.1 = (bf16[32,2560]{1,0:T(8,128)(2,1)S(1)}, bf16[32,2560]{1,0:T(8,128)(2,1)S(1)}, u32[]{:S(2)}, u32[]{:S(2)}) collective-permute-start(bf16[32,2560]{1,0:T(8,128)(2,1)S(1)} %get-tuple-element.69), channel_id=1, source_target_pairs={{0,0},{1,8},{4,1},{5,9},{8,4},{9,12},{12,5},{13,13},{2,2},{3,10},{... | collective-permute-start | bytes 491528 | tf_op jit(solution)/shard_map/ppermute | solution.py:241
  22.7 11.9 %collective-permute-start.2 = (bf16[32,2560]{1,0:T(8,128)(2,1)S(1)}, bf16[32,2560]{1,0:T(8,128)(2,1)S(1)}, u32[]{:S(2)}, u32[]{:S(2)}) collective-permute-start(bf16[32,2560]{1,0:T(8,128)(2,1)S(1)} %get-tuple-element.70), channel_id=1, source_target_pairs={{0,1},{1,9},{4,4},{5,12},{8,5},{9,13},{12,0},{13,8},{2,3},{3,11},{... | collective-permute-start | bytes 491528 | tf_op jit(solution)/shard_map/ppermute | solution.py:241
  25.8 11.1 %collective-permute-start.3 = (bf16[32,2560]{1,0:T(8,128)(2,1)S(1)}, bf16[32,2560]{1,0:T(8,128)(2,1)S(1)}, u32[]{:S(2)}, u32[]{:S(2)}) collective-permute-start(bf16[32,2560]{1,0:T(8,128)(2,1)S(1)} %get-tuple-element.71), channel_id=1, source_target_pairs={{0,4},{1,12},{4,5},{5,13},{8,0},{9,8},{12,1},{13,9},{2,6},{3,14},{... | collective-permute-start | bytes 491528 | tf_op jit(solution)/shard_map/ppermute | solution.py:241
  28.0 11.6 %collective-permute-start.4 = (bf16[32,2560]{1,0:T(8,128)(2,1)S(1)}, bf16[32,2560]{1,0:T(8,128)(2,1)S(1)}, u32[]{:S(2)}, u32[]{:S(2)}) collective-permute-start(bf16[32,2560]{1,0:T(8,128)(2,1)S(1)} %get-tuple-element.72), channel_id=1, source_target_pairs={{0,5},{1,13},{4,0},{5,8},{8,1},{9,9},{12,4},{13,12},{2,7},{3,15},{... | collective-permute-start | bytes 491528 | tf_op jit(solution)/shard_map/ppermute | solution.py:241
  40.9 28.4 %all-to-all-start = ((bf16[16,176,256]{2,1,0:T(8,128)(2,1)}), bf16[16,176,256]{2,1,0:T(8,128)(2,1)S(1)}, u32[]{:S(2)}, u32[]{:S(2)}) async-start(bf16[16,176,256]{2,1,0:T(8,128)(2,1)} %pack_keys.1), calls=%async_computation | async-start | bytes 2883584 | tf_op jit(solution)/shard_map/all_to_all | solution.py:250
  47.7 11.9 %collective-permute-start.7 = (bf16[32,1920]{1,0:T(8,128)(2,1)S(1)}, bf16[32,1920]{1,0:T(8,128)(2,1)S(1)}, u32[]{:S(2)}, u32[]{:S(2)}) collective-permute-start(bf16[32,1920]{1,0:T(8,128)(2,1)S(1)} %get-tuple-element.82), channel_id=1, source_target_pairs={{0,0},{1,8},{4,1},{5,9},{8,4},{9,12},{12,5},{13,13},{2,2},{3,10},{... | collective-permute-start | bytes 368648 | tf_op jit(solution)/shard_map/ppermute | solution.py:241
  52.8 7.3 %collective-permute-start.8 = (bf16[32,1920]{1,0:T(8,128)(2,1)S(1)}, bf16[32,1920]{1,0:T(8,128)(2,1)S(1)}, u32[]{:S(2)}, u32[]{:S(2)}) collective-permute-start(bf16[32,1920]{1,0:T(8,128)(2,1)S(1)} %get-tuple-element.83), channel_id=1, source_target_pairs={{0,1},{1,9},{4,4},{5,12},{8,5},{9,13},{12,0},{13,8},{2,3},{3,11},{... | collective-permute-start | bytes 368648 | tf_op jit(solution)/shard_map/ppermute | solution.py:241
  55.8 7.0 %collective-permute-start.9 = (bf16[32,1920]{1,0:T(8,128)(2,1)S(1)}, bf16[32,1920]{1,0:T(8,128)(2,1)S(1)}, u32[]{:S(2)}, u32[]{:S(2)}) collective-permute-start(bf16[32,1920]{1,0:T(8,128)(2,1)S(1)} %get-tuple-element.84), channel_id=1, source_target_pairs={{0,4},{1,12},{4,5},{5,13},{8,0},{9,8},{12,1},{13,9},{2,6},{3,14},{... | collective-permute-start | bytes 368648 | tf_op jit(solution)/shard_map/ppermute | solution.py:241
  55.9 11.4 %collective-permute-start.10 = (bf16[32,1920]{1,0:T(8,128)(2,1)S(1)}, bf16[32,1920]{1,0:T(8,128)(2,1)S(1)}, u32[]{:S(2)}, u32[]{:S(2)}) collective-permute-start(bf16[32,1920]{1,0:T(8,128)(2,1)S(1)} %get-tuple-element.85), channel_id=1, source_target_pairs={{0,5},{1,13},{4,0},{5,8},{8,1},{9,9},{12,4},{13,12},{2,7},{3,15},{... | collective-permute-start | bytes 368648 | tf_op jit(solution)/shard_map/ppermute | solution.py:241
  72.4 23.7 %all-to-all-start.1 = ((bf16[16,304,128]{2,1,0:T(8,128)(2,1)}), bf16[16,304,128]{2,1,0:T(8,128)(2,1)S(1)}, u32[]{:S(2)}, u32[]{:S(2)}) async-start(bf16[16,304,128]{2,1,0:T(8,128)(2,1)} %pack_values.1), calls=%async_computation.1 | async-start | bytes 2490368 | tf_op jit(solution)/shard_map/all_to_all | solution.py:250
  113.1 21.4 %all-to-all-start.2 = ((bf16[16,48,256]{2,1,0:T(8,128)(2,1)}), bf16[16,48,256]{2,1,0:T(8,128)(2,1)S(1)}, u32[]{:S(2)}, u32[]{:S(2)}) async-start(bf16[16,48,256]{2,1,0:T(8,128)(2,1)} %get-tuple-element.96), calls=%async_computation.2 | async-start | bytes 786432 | tf_op jit(solution)/shard_map/all_to_all | solution.py:250
  140.9 27.4 %all-to-all-start.3 = ((bf16[16,304,128]{2,1,0:T(8,128)(2,1)}), bf16[16,304,128]{2,1,0:T(8,128)(2,1)S(1)}, u32[]{:S(2)}, u32[]{:S(2)}) async-start(bf16[16,304,128]{2,1,0:T(8,128)(2,1)} %merge.1), calls=%async_computation.3 | async-start | bytes 2490368 | tf_op jit(solution)/shard_map/all_to_all | solution.py:250
  147.8 15.0 %collective-permute-start.14 = (bf16[32,1280]{1,0:T(8,128)(2,1)S(1)}, bf16[32,1280]{1,0:T(8,128)(2,1)S(1)}, u32[]{:S(2)}, u32[]{:S(2)}) collective-permute-start(bf16[32,1280]{1,0:T(8,128)(2,1)S(1)} %get-tuple-element.106), channel_id=1, source_target_pairs={{0,0},{8,1},{1,4},{9,5},{4,8},{12,9},{5,12},{13,13},{2,2},{10,3},{... | collective-permute-start | bytes 245768 | tf_op jit(solution)/shard_map/ppermute | solution.py:246
  151.6 11.3 %collective-permute-start.15 = (bf16[32,1280]{1,0:T(8,128)(2,1)S(1)}, bf16[32,1280]{1,0:T(8,128)(2,1)S(1)}, u32[]{:S(2)}, u32[]{:S(2)}) collective-permute-start(bf16[32,1280]{1,0:T(8,128)(2,1)S(1)} %get-tuple-element.107), channel_id=1, source_target_pairs={{1,0},{9,1},{4,4},{12,5},{5,8},{13,9},{0,12},{8,13},{3,2},{11,3},{... | collective-permute-start | bytes 245768 | tf_op jit(solution)/shard_map/ppermute | solution.py:246
  153.5 13.0 %collective-permute-start.16 = (bf16[32,1280]{1,0:T(8,128)(2,1)S(1)}, bf16[32,1280]{1,0:T(8,128)(2,1)S(1)}, u32[]{:S(2)}, u32[]{:S(2)}) collective-permute-start(bf16[32,1280]{1,0:T(8,128)(2,1)S(1)} %get-tuple-element.108), channel_id=1, source_target_pairs={{4,0},{12,1},{5,4},{13,5},{0,8},{8,9},{1,12},{9,13},{6,2},{14,3},{... | collective-permute-start | bytes 245768 | tf_op jit(solution)/shard_map/ppermute | solution.py:246
  160.9 7.4 %collective-permute-start.17 = (bf16[32,1280]{1,0:T(8,128)(2,1)S(1)}, bf16[32,1280]{1,0:T(8,128)(2,1)S(1)}, u32[]{:S(2)}, u32[]{:S(2)}) collective-permute-start(bf16[32,1280]{1,0:T(8,128)(2,1)S(1)} %get-tuple-element.109), channel_id=1, source_target_pairs={{5,0},{13,1},{0,4},{8,5},{1,8},{9,9},{4,12},{12,13},{7,2},{15,3},{... | collective-permute-start | bytes 245768 | tf_op jit(solution)/shard_map/ppermute | solution.py:246
  178.4 30.2 %collective-permute-start.19 = (bf16[256,1280]{1,0:T(8,128)(2,1)S(1)}, bf16[256,1280]{1,0:T(8,128)(2,1)S(1)}, u32[]{:S(2)}, u32[]{:S(2)}) collective-permute-start(bf16[256,1280]{1,0:T(8,128)(2,1)S(1)} %fusion.18), channel_id=1, source_target_pairs={{0,2},{2,0},{1,3},{3,1},{4,6},{6,4},{5,7},{7,5},{8,10},{10,8},{9,1... | collective-permute-start | bytes 1966088 | tf_op jit(solution)/shard_map/ppermute | solution.py:225
  181.3 23.3 %collective-permute-start.20 = (bf16[32,1920]{1,0:T(8,128)(2,1)S(1)}, bf16[32,1920]{1,0:T(8,128)(2,1)S(1)}, u32[]{:S(2)}, u32[]{:S(2)}) collective-permute-start(bf16[32,1920]{1,0:T(8,128)(2,1)S(1)} %get-tuple-element.118), channel_id=1, source_target_pairs={{0,0},{8,1},{1,4},{9,5},{4,8},{12,9},{5,12},{13,13},{2,2},{10,3},{... | collective-permute-start | bytes 368648 | tf_op jit(solution)/shard_map/ppermute | solution.py:246
  183.9 20.6 %collective-permute-start.21 = (bf16[32,1920]{1,0:T(8,128)(2,1)S(1)}, bf16[32,1920]{1,0:T(8,128)(2,1)S(1)}, u32[]{:S(2)}, u32[]{:S(2)}) collective-permute-start(bf16[32,1920]{1,0:T(8,128)(2,1)S(1)} %get-tuple-element.119), channel_id=1, source_target_pairs={{1,0},{9,1},{4,4},{12,5},{5,8},{13,9},{0,12},{8,13},{3,2},{11,3},{... | collective-permute-start | bytes 368648 | tf_op jit(solution)/shard_map/ppermute | solution.py:246
  185.9 21.8 %collective-permute-start.22 = (bf16[32,1920]{1,0:T(8,128)(2,1)S(1)}, bf16[32,1920]{1,0:T(8,128)(2,1)S(1)}, u32[]{:S(2)}, u32[]{:S(2)}) collective-permute-start(bf16[32,1920]{1,0:T(8,128)(2,1)S(1)} %get-tuple-element.120), channel_id=1, source_target_pairs={{4,0},{12,1},{5,4},{13,5},{0,8},{8,9},{1,12},{9,13},{6,2},{14,3},{... | collective-permute-start | bytes 368648 | tf_op jit(solution)/shard_map/ppermute | solution.py:246
  192.4 15.3 %collective-permute-start.23 = (bf16[32,1920]{1,0:T(8,128)(2,1)S(1)}, bf16[32,1920]{1,0:T(8,128)(2,1)S(1)}, u32[]{:S(2)}, u32[]{:S(2)}) collective-permute-start(bf16[32,1920]{1,0:T(8,128)(2,1)S(1)} %get-tuple-element.121), channel_id=1, source_target_pairs={{5,0},{13,1},{0,4},{8,5},{1,8},{9,9},{4,12},{12,13},{7,2},{15,3},{... | collective-permute-start | bytes 368648 | tf_op jit(solution)/shard_map/ppermute | solution.py:246
  (14 other events, 50.5 us)

commit v3 on v2

v3 whole, which is shorter than its diff:
```python
import functools

import jax
import jax.numpy as jnp
from jax import lax
from jax.experimental import pallas as pl
from jax.experimental.pallas import tpu as pltpu
from jax.sharding import Mesh, PartitionSpec as P

HD = 128
SCALE = HD ** (-0.5)
LOG2E = 1.4426950408889634
SUB = 16
W_GROUP, W_UNROLL = 4, 4
V_GROUP, V_UNROLL = 8, True
G_GROUP, G_UNROLL = 8, True
VMEM_LIMIT = 52 * 2**20
NT = (((1,), (1,)), ((), ()))
NN = (((1,), (0,)), ((), ()))


def dot(a, b, dims=NN):
    return lax.dot_general(a, b, dims, preferred_element_type=jnp.float32)


def piece(ref, j, group, first, count, lanes=slice(None)):
    block = ref[pl.ds(j * group, group), first:first + count, lanes]
    return block.reshape(group * count, block.shape[-1])


def key_rows(half, j, group, blocks, rows):
    start = (half * blocks + j * group) * rows
    return pl.ds(pl.multiple_of(start, group * rows), group * rows)


def weights_kernel(rows, z_ref, q_ref, ka_ref, kb_ref, p_ref, w_ref, s_scr, t_scr):
    blocks = ka_ref.shape[0]
    tile = p_ref.shape[1]
    qtq = q_ref[...].reshape(tile, 2 * HD)
    q = qtq[:, HD:]

    top = jnp.full((1, tile), -jnp.inf, jnp.float32)
    for half, ref in enumerate((ka_ref, kb_ref)):
        def scores(j, top, half=half, ref=ref):
            here = key_rows(half, j, W_GROUP, blocks, rows)
            both = piece(ref, j, W_GROUP, 0, rows)
            s = dot(both[:, :HD], q, NT)
            s_scr[here, :] = s
            t_scr[here, :] = dot(both, qtq, NT)
            return jnp.maximum(top, jnp.max(s, axis=0, keepdims=True))
        top = lax.fori_loop(0, blocks // W_GROUP, scores, top, unroll=W_UNROLL)

    zero = jnp.zeros((1, tile), jnp.float32)

    def sums(j, carry):
        total, slope = carry
        here = key_rows(0, j, W_GROUP, blocks, rows)
        e = jnp.exp2((s_scr[here, :] - top) * (SCALE * LOG2E))
        s_scr[here, :] = e
        total += jnp.sum(e, axis=0, keepdims=True)
        slope += jnp.sum(e * t_scr[here, :], axis=0, keepdims=True)
        return total, slope

    total, slope = lax.fori_loop(0, 2 * blocks // W_GROUP, sums, (zero, zero), unroll=W_UNROLL)
    inv = 1.0 / total
    slope = slope * inv

    def store(j, carry):
        here = key_rows(0, j, W_GROUP, blocks, rows)
        p = s_scr[here, :] * inv
        p_ref[here, :] = p.astype(jnp.bfloat16)
        w_ref[here, :] = (p * (t_scr[here, :] - slope)).astype(jnp.bfloat16)
        return carry

    lax.fori_loop(0, 2 * blocks // W_GROUP, store, 0, unroll=W_UNROLL)


def values_kernel(rows, z_ref, g_ref, va_ref, vb_ref, p_ref, w_ref, out_ref, d_ref, vt_scr):
    blocks = va_ref.shape[0]
    tile = p_ref.shape[1]

    @pl.when(pl.program_id(0) == 0)
    def _():
        for half, ref in enumerate((va_ref, vb_ref)):
            def turn(j, carry, half=half, ref=ref):
                here = key_rows(half, j, V_GROUP, blocks, rows)
                vt_scr[0:HD, here] = piece(ref, j, V_GROUP, 0, rows).T
                vt_scr[HD:, here] = piece(ref, j, V_GROUP, rows, rows).T
                return carry
            lax.fori_loop(0, blocks // V_GROUP, turn, 0, unroll=V_UNROLL)

    def add(j, carry):
        both, tan = carry
        here = key_rows(0, j, V_GROUP, blocks, rows)
        both += dot(vt_scr[:, here], p_ref[here, :])
        tan += dot(vt_scr[0:HD, here], w_ref[here, :])
        return both, tan

    zeros = jnp.zeros((2 * HD, tile), jnp.float32), jnp.zeros((HD, tile), jnp.float32)
    both, tan = lax.fori_loop(0, 2 * blocks // V_GROUP, add, zeros, unroll=V_UNROLL)
    attn = both[0:HD].astype(jnp.bfloat16)
    g = g_ref[...].reshape(tile, HD)
    d_ref[...] = jnp.sum(attn.astype(jnp.float32) * g.astype(jnp.float32).T, axis=0, keepdims=True)
    out_ref[:, :, 0:HD] = both[0:HD].T.astype(jnp.bfloat16).reshape(-1, SUB, HD)
    out_ref[:, :, HD:] = (both[HD:] + SCALE * tan).T.astype(jnp.bfloat16).reshape(-1, SUB, HD)


def grads_kernel(rows, z_ref, q_ref, g_ref, ka_ref, kb_ref, va_ref, vb_ref, p_ref, d_ref, dq_ref, oa_ref, ob_ref, kt_scr, k_scr, v_scr):
    blocks = ka_ref.shape[0]
    tile = p_ref.shape[1]
    step = pl.program_id(0)
    q = q_ref[...].reshape(tile, 2 * HD)[:, HD:]
    g = g_ref[...].reshape(tile, HD)
    dsum = d_ref[...]

    @pl.when(step == 0)
    def _():
        for half, ref in enumerate((ka_ref, kb_ref)):
            def turn(j, carry, half=half, ref=ref):
                kt_scr[:, key_rows(half, j, G_GROUP, blocks, rows)] = piece(ref, j, G_GROUP, 0, rows, slice(0, HD)).T
                return carry
            lax.fori_loop(0, blocks // G_GROUP, turn, 0, unroll=G_UNROLL)
        k_scr[...] = jnp.zeros_like(k_scr)
        v_scr[...] = jnp.zeros_like(v_scr)

    dq = jnp.zeros((HD, tile), jnp.float32)
    for half, ref in enumerate((va_ref, vb_ref)):
        def add(j, dq, half=half, ref=ref):
            here = key_rows(half, j, G_GROUP, blocks, rows)
            p = p_ref[here, :]
            slopes = dot(piece(ref, j, G_GROUP, 0, rows), g, NT) - dsum
            ds = (p.astype(jnp.float32) * slopes).astype(jnp.bfloat16)
            k_scr[here, :] += dot(ds, q)
            v_scr[here, :] += dot(p, g)
            return dq + dot(kt_scr[:, here], ds)
        dq = lax.fori_loop(0, blocks // G_GROUP, add, dq, unroll=G_UNROLL)
    dq_ref[...] = (SCALE * dq).T.astype(jnp.bfloat16).reshape(-1, SUB, HD)

    @pl.when(step == pl.num_programs(0) - 1)
    def _():
        for half, ref in enumerate((oa_ref, ob_ref)):
            def give(j, carry, half=half, ref=ref):
                here = key_rows(half, j, G_GROUP, blocks, rows)
                group = pl.ds(j * G_GROUP, G_GROUP)
                ref[group, 0:rows, :] = (SCALE * k_scr[here, :]).astype(jnp.bfloat16).reshape(G_GROUP, rows, HD)
                ref[group, rows:, :] = v_scr[here, :].astype(jnp.bfloat16).reshape(G_GROUP, rows, HD)
                return carry
            lax.fori_loop(0, blocks // G_GROUP, give, 0, unroll=G_UNROLL)


def whole(array):
    return pl.BlockSpec(array.shape, lambda i, s: (0,) * len(array.shape))


def kernel_call(body, name, grid, scalars, ins, outs, scratch, flops=0, bytes_accessed=4 * 2**20, limit=VMEM_LIMIT):
    arrays, in_specs = zip(*ins)
    shapes, out_specs = zip(*outs)
    return pl.pallas_call(
        body,
        grid_spec=pltpu.PrefetchScalarGridSpec(
            num_scalar_prefetch=1,
            grid=(grid,),
            in_specs=list(in_specs),
            out_specs=list(out_specs),
            scratch_shapes=scratch,
        ),
        out_shape=list(shapes),
        name=name,
        compiler_params=pltpu.CompilerParams(vmem_limit_bytes=limit),
        cost_estimate=pl.CostEstimate(flops=flops, bytes_accessed=bytes_accessed, transcendentals=0),
    )(scalars, *arrays)


def specs(blocks, rows, window):
    tile = blocks * SUB
    keys = 2 * blocks * rows
    q_spec = pl.BlockSpec((blocks, SUB, 2 * HD), lambda i, s: (0, rows // SUB + i, 0))
    g_spec = pl.BlockSpec((blocks, SUB, HD), lambda i, s: (0, 2 * rows // SUB + i, 0))
    p_spec = pl.BlockSpec((keys, tile), lambda i, s: (0, i))
    d_spec = pl.BlockSpec((1, tile), lambda i, s: (0, i))
    return q_spec, g_spec, p_spec, d_spec, keys, tile, window // SUB


def attention_weights(z, recv_k, other_k, rows, window):
    q_spec, _, p_spec, _, keys, tile, grid = specs(recv_k.shape[0], rows, window)
    p_shape = jax.ShapeDtypeStruct((keys, grid * tile), jnp.bfloat16)
    return kernel_call(
        functools.partial(weights_kernel, rows), "weights", grid, z,
        [(recv_k, q_spec), (recv_k, whole(recv_k)), (other_k, whole(other_k))],
        [(p_shape, p_spec), (p_shape, p_spec)],
        [pltpu.VMEM((keys, tile), jnp.float32), pltpu.VMEM((keys, tile), jnp.float32)],
        8 * keys * grid * tile * HD, 32 * 2**20)


def attention_values(z, recv_v, other_v, probs, weights, rows, window):
    blocks = recv_v.shape[0]
    _, g_spec, p_spec, d_spec, keys, tile, grid = specs(blocks, rows, window)
    out_shape = jax.ShapeDtypeStruct((blocks, window, 2 * HD), jnp.bfloat16)
    d_shape = jax.ShapeDtypeStruct((1, grid * tile), jnp.float32)
    return kernel_call(
        functools.partial(values_kernel, rows), "values", grid, z,
        [(recv_v, g_spec), (recv_v, whole(recv_v)), (other_v, whole(other_v)), (probs, p_spec), (weights, p_spec)],
        [(out_shape, pl.BlockSpec((blocks, SUB, 2 * HD), lambda i, s: (0, i, 0))), (d_shape, d_spec)],
        [pltpu.VMEM((2 * HD, keys), jnp.bfloat16)],
        6 * keys * grid * tile * HD, 16 * 2**20)


def attention_grads(z, recv_k, other_k, recv_v, other_v, probs, dsum, rows, window):
    blocks = recv_v.shape[0]
    q_spec, g_spec, p_spec, d_spec, keys, tile, grid = specs(blocks, rows, window)
    dq_shape = jax.ShapeDtypeStruct((blocks, window, HD), jnp.bfloat16)
    shape = jax.ShapeDtypeStruct((blocks, 2 * rows, HD), jnp.bfloat16)
    return kernel_call(
        functools.partial(grads_kernel, rows), "grads", grid, z,
        [(recv_k, q_spec), (recv_v, g_spec), (recv_k, whole(recv_k)), (other_k, whole(other_k)),
         (recv_v, whole(recv_v)), (other_v, whole(other_v)), (probs, p_spec), (dsum, d_spec)],
        [(dq_shape, pl.BlockSpec((blocks, SUB, HD), lambda i, s: (0, i, 0))),
         (shape, whole(shape)), (shape, whole(shape))],
        [pltpu.VMEM((HD, keys), jnp.bfloat16), pltpu.VMEM((keys, HD), jnp.float32), pltpu.VMEM((keys, HD), jnp.float32)],
        10 * keys * grid * tile * HD, 32 * 2**20)


THIRDS = 3
SWAP = [(0, 1), (1, 0)]


def swap(array, axis):
    return lax.ppermute(array, axis, SWAP)


def along_z(pieces):
    count = len(pieces)
    routes = [[(i, (i + k) % count) for i in range(count)] for k in range(count)]
    return [pieces[0]] + [lax.ppermute(a, "z", route) for a, route in zip(pieces[1:], routes[1:])]


def over_chips(array):
    return lax.all_to_all(array, ("x", "y"), 0, 0, tiled=True)


def plane_at(place_ref, shift, count):
    return lax.rem(place_ref[0] + shift + count, count)


def split_kernel(place_ref, *refs):
    count = 4
    ins, outs = refs[:-count], refs[-count:]
    kinds = len(ins) // 2
    clips, tokens, width = ins[0].shape
    rows = tokens // 2
    core = place_ref[1]
    start = pl.multiple_of(core * rows, rows)
    for k, out in enumerate(outs):
        slot = plane_at(place_ref, k, count)
        part, clip = slot // clips, lax.rem(slot, clips)

        for mine, group in ((True, ins[:kinds]), (False, ins[kinds:])):
            @pl.when((part == core) == mine)
            def _(out=out, group=group, clip=clip):
                for index, ref in enumerate(group):
                    out[:, index * width:(index + 1) * width] = ref[clip, pl.ds(start, rows), :]


def keep_kernel(c_ref, *refs):
    out = refs[-1]
    kinds = len(refs) // 2
    clips, tokens, width = refs[0].shape
    rows = tokens // 2
    core = c_ref[0]
    start = pl.multiple_of(core * rows, rows)
    for part, group in ((core, refs[:kinds]), (1 - core, refs[kinds:2 * kinds])):
        for clip in range(clips):
            for index, ref in enumerate(group):
                out[part * clips + clip, :, index * width:(index + 1) * width] = ref[clip, pl.ds(start, rows), :]


def home_kernel(c_ref, back_ref, got_ref, *outs):
    clips, tokens, width = outs[0].shape
    rows = tokens // 2
    core = c_ref[0]
    for clip in range(clips):
        for index, out in enumerate(outs):
            lanes = slice(index * width, (index + 1) * width)
            out[clip, pl.ds(pl.multiple_of(core * rows, rows), rows), :] = back_ref[core * clips + clip, :, lanes]
            out[clip, pl.ds(pl.multiple_of((1 - core) * rows, rows), rows), :] = got_ref[core * clips + clip, :, lanes]


def keys_kernel(heads, z_ref, *refs):
    plane_ref, out = refs
    rows = plane_ref.shape[0]
    window = out.shape[1] - rows
    width = heads * HD
    for head in range(heads):
        for kind in range(4):
            source = slice(kind * width + head * HD, kind * width + (head + 1) * HD)
            lanes = slice((kind % 2) * HD, (kind % 2 + 1) * HD)
            whole_block = plane_ref[:, source]
            for third in range(THIRDS):
                chip = head * THIRDS + third
                if kind < 2:
                    out[chip, 0:rows, lanes] = whole_block
                else:
                    first = third * window
                    count = min(window, rows - first)
                    out[chip, rows:rows + count, lanes] = whole_block[first:first + count]
                    if count < window:
                        out[chip, rows + count:, lanes] = jnp.zeros((window - count, HD), out.dtype)
    for chip in range(heads * THIRDS, out.shape[0]):
        out[chip] = jnp.zeros(out.shape[1:], out.dtype)


def values_pack_kernel(heads, place_ref, *refs):
    ins, out, scr = refs[:-2], refs[-2], refs[-1]
    part = ins[0].shape[0]
    rows = part * len(ins)
    for k, ref in enumerate(ins):
        scr[pl.ds(pl.multiple_of(plane_at(place_ref, -k, len(ins)) * part, part), part), :] = ref[...]
    window = out.shape[1] - 2 * rows
    width = heads * HD
    for head in range(heads):
        for kind in range(3):
            source = slice(kind * width + head * HD, kind * width + (head + 1) * HD)
            whole_block = scr[:, source]
            for third in range(THIRDS):
                chip = head * THIRDS + third
                if kind < 2:
                    out[chip, kind * rows:(kind + 1) * rows, :] = whole_block
                else:
                    first = third * window
                    count = min(window, rows - first)
                    out[chip, 2 * rows:2 * rows + count, :] = whole_block[first:first + count]
                    if count < window:
                        out[chip, 2 * rows + count:, :] = jnp.zeros((window - count, HD), out.dtype)
    for chip in range(heads * THIRDS, out.shape[0]):
        out[chip] = jnp.zeros(out.shape[1:], out.dtype)


def out_unpack_kernel(heads, place_ref, back_ref, *refs):
    outs, scr = refs[:-1], refs[-1]
    part = outs[0].shape[0]
    window = back_ref.shape[1]
    rows = part * len(outs)
    width = heads * HD
    for head in range(heads):
        for kind in range(2):
            lanes = slice(kind * HD, (kind + 1) * HD)
            pieces = [
                back_ref[head * THIRDS + third, 0:min(window, rows - third * window), lanes]
                for third in range(THIRDS)
            ]
            scr[:, kind * width + head * HD:kind * width + (head + 1) * HD] = jnp.concatenate(pieces, axis=0)
    for k, out in enumerate(outs):
        out[...] = scr[pl.ds(pl.multiple_of(plane_at(place_ref, k, len(outs)) * part, part), part), :]


def join_out_kernel(place_ref, *refs):
    ins, own_ref, other_ref = refs[:-2], refs[-2], refs[-1]
    rows, width = ins[0].shape
    clips, width = len(ins) // 2, width // 2
    for k, ref in enumerate(ins):
        slot = plane_at(place_ref, -k, len(ins))
        part, clip = slot // clips, lax.rem(slot, clips)
        for mine, out in ((True, own_ref), (False, other_ref)):
            @pl.when((part == place_ref[1]) == mine)
            def _(ref=ref, out=out, clip=clip):
                for kind in range(2):
                    first = pl.multiple_of((kind * clips + clip) * rows, rows)
                    out[pl.ds(first, rows), :] = ref[:, kind * width:(kind + 1) * width]


def home_out_kernel(c_ref, keep_ref, got_ref, *outs):
    clips, tokens, width = outs[0].shape
    rows = tokens // 2
    core = c_ref[0]
    for ref, half in ((keep_ref, core), (got_ref, 1 - core)):
        for kind, out in enumerate(outs):
            for clip in range(clips):
                first = (kind * clips + clip) * rows
                lanes = pl.ds(pl.multiple_of(core * width, HD), width)
                out[clip, pl.ds(pl.multiple_of(half * rows, rows), rows), :] = ref[first:first + rows, lanes]


def grads_unpack_kernel(heads, z_ref, back_ref, out_ref):
    part = out_ref.shape[1]
    rows = part * out_ref.shape[0]
    window = back_ref.shape[1] - 2 * rows
    width = heads * HD
    for head in range(heads):
        for kind in range(3):
            chips = [head * THIRDS + third for third in range(THIRDS)]
            if kind < 2:
                column = sum(
                    back_ref[chip, kind * rows:(kind + 1) * rows, :].astype(jnp.float32) for chip in chips
                ).astype(jnp.bfloat16)
            else:
                column = jnp.concatenate([
                    back_ref[chip, 2 * rows:2 * rows + min(window, rows - third * window), :]
                    for third, chip in enumerate(chips)
                ], axis=0)
            for d in range(out_ref.shape[0]):
                lanes = slice(kind * width + head * HD, kind * width + (head + 1) * HD)
                out_ref[d, :, lanes] = column[d * part:(d + 1) * part]


def merge_kernel(z_ref, own_ref, got_ref, dq_ref, out_ref):
    rows = got_ref.shape[1]
    total = own_ref[...].astype(jnp.float32) + got_ref[...].astype(jnp.float32)
    out_ref[:, 0:rows, :] = total.astype(jnp.bfloat16)
    out_ref[:, rows:, :] = dq_ref[...]


def repack(body, name, z, ins, shapes, scratch=(), limit=VMEM_LIMIT):
    shapes = [jax.ShapeDtypeStruct(s, jnp.bfloat16) for s in shapes]
    return kernel_call(body, name, 1, z, [(a, whole(a)) for a in ins], [(s, whole(s)) for s in shapes], list(scratch), limit=limit)


def over_planes(array):
    return lax.all_to_all(array, "z", 0, 0, tiled=True)


def local(queries, keys, values, queries_tan, keys_tan, values_tan, w_out, grad_out):
    w, c = lax.axis_index("w"), lax.axis_index("c")
    z = lax.axis_index("z").astype(jnp.int32).reshape(1)
    core = c.astype(jnp.int32).reshape(1)
    place = jnp.concatenate([z, core])
    clips, tokens, features = queries.shape
    heads = features // HD
    chips = lax.axis_size(("x", "y"))
    slots = 2 * clips
    rows = slots * tokens // 2
    window = pl.cdiv(pl.cdiv(rows, THIRDS), SUB) * SUB

    w_other = swap(w_out, "c")

    far = swap(grad_out, "w")
    near = swap(grad_out, "c")
    kinds = (keys, keys_tan, queries_tan, queries)
    got = tuple(swap(kind, "c") for kind in kinds)
    got_values = tuple(swap(kind, "c") for kind in (values, values_tan))
    kept = repack(keep_kernel, "keep_keys", core, kinds + got, [(slots, tokens // 2, len(kinds) * features)],
                  limit=60 * 2**20)[0]
    kept, far = lax.optimization_barrier((kept, far))
    plane = over_planes(kept).reshape(rows, -1)
    cross = swap(far, "c")
    width = grad_out.shape[2]
    blocks = [
        lax.dynamic_slice_in_dim(w_out, ((w ^ i) * 2 + (c ^ j)) * width, width, axis=1)
        for i in range(2) for j in range(2)
    ]
    cot = sum(
        jnp.einsum("btf,cf->btc", grad, part, preferred_element_type=jnp.float32)
        for grad, part in zip((grad_out, near, far, cross), blocks)
    ).astype(jnp.bfloat16)
    kinds = (values, values_tan, cot)
    got = got_values + (swap(cot, "c"),)
    shape = (tokens // 2, len(kinds) * features)
    split = repack(split_kernel, "split_values", place, kinds + got, [shape] * slots)
    plane, split = lax.optimization_barrier((plane, split))
    plane_v = along_z(split)

    packed = repack(functools.partial(keys_kernel, heads), "pack_keys", z, [plane], [(chips, rows + window, 2 * HD)])[0]
    recv_k = over_chips(packed)
    recv_k, plane_v = lax.optimization_barrier((recv_k, plane_v))
    other_k = swap(recv_k, "c")
    packed = repack(functools.partial(values_pack_kernel, heads), "pack_values", place, plane_v, [(chips, 2 * rows + window, HD)],
                    [pltpu.VMEM((rows, 3 * features), jnp.bfloat16)])[0]
    recv_v = over_chips(packed)

    probs, weights = attention_weights(z, recv_k, other_k, rows, window)
    recv_v, probs, weights = lax.optimization_barrier((recv_v, probs, weights))
    other_v = swap(recv_v, "c")
    out, dsum = attention_values(z, recv_v, other_v, probs, weights, rows, window)
    back = over_chips(out)
    dq, own_grads, other_grads = attention_grads(z, recv_k, other_k, recv_v, other_v, probs, dsum, rows, window)
    back, dq, own_grads, other_grads = lax.optimization_barrier((back, dq, own_grads, other_grads))
    got = swap(other_grads, "c")
    merged = repack(merge_kernel, "merge", z, [own_grads, got, dq], [(chips, 2 * rows + window, HD)])[0]
    back, merged = lax.optimization_barrier((back, merged))
    grads = over_chips(merged)

    shape = (tokens // 2, 2 * features)
    home = along_z(repack(functools.partial(out_unpack_kernel, heads), "unpack_out", place, [back], [shape] * slots,
                          [pltpu.VMEM((rows, 2 * features), jnp.bfloat16)]))
    home, grads = lax.optimization_barrier((home, grads))
    own, other = repack(join_out_kernel, "join_out", place, home, [(slots * tokens // 2, features)] * 2)

    def project(chip):
        parts = [
            jnp.dot(rows_of, lax.dynamic_slice_in_dim(weight, chip * 2 * width, 2 * width, axis=1),
                    preferred_element_type=jnp.float32)
            for rows_of, weight in ((own, w_out), (other, w_other))
        ]
        return parts[0] + parts[1]

    got = swap(project(1 - w).astype(jnp.bfloat16), "w")
    total = (project(w) + got.astype(jnp.float32)).astype(jnp.bfloat16)
    outs = repack(home_out_kernel, "home_out", core, [total, swap(total, "c")], [(clips, tokens, width)] * 2)

    shape = (slots, tokens // 2, 3 * features)
    back = over_planes(repack(functools.partial(grads_unpack_kernel, heads), "unpack_grads", z, [grads], [shape])[0])
    grad_k, grad_v, grad_q = repack(home_kernel, "home_grads", core, [back, swap(back, "c")], [queries.shape] * 3)
    return outs[0], outs[1], grad_q, grad_k, grad_v


def solution(mesh):
    seq, tp = ("x", "y", "z"), ("w", "c")
    fine = Mesh(mesh.devices.reshape(4, 4, 4, 2, 2), seq + tp)
    split = P(None, seq, tp)
    return jax.shard_map(
        local,
        mesh=fine,
        in_specs=(split,) * 6 + (P(tp, None), split),
        out_specs=(split,) * 5,
        check_vma=False,
    )
```

time: 211 us -> 192 us (0.910)
  starting transfers between devices: 87.1 us -> 75.9 us
  Pallas kernels: 52.2 us -> 45.9 us
  local copies, waits for them, and re-layouts: 6.58 us -> 2.82 us
    ppermute x16 -> x6, starting transfers between devices: 53.8 us -> 15.6 us  [along_z(): lax.ppermute(a, 'z', route)]
    ppermute x8 -> x17, starting transfers between devices: 12.5 us -> 27.8 us  [swap(): return lax.ppermute(array, axis, SWAP)]
    ppermute x16 -> x6, waiting for transfers between devices: 29.5 us -> 16.1 us  [along_z(): lax.ppermute(a, 'z', route)]
    all_to_all x0 -> x2, starting transfers between devices: none -> 11.5 us  [over_planes(): return lax.all_to_all(array, 'z', 0, 0, tiled=True)]
    ppermute x8 -> x17, waiting for transfers between devices: 9.76 us -> 16.3 us  [swap(): return lax.ppermute(array, axis, SWAP)]
    pallas_call x12 -> x13, Pallas kernels: 52.2 us -> 45.9 us  [kernel_call(): pl.pallas_call(body, grid_spec=pltpu.PrefetchScalarGridSpec(num_scalar_pr...]
    all_to_all x0 -> x2, waiting for transfers between devices: none -> 5.25 us  [over_planes(): return lax.all_to_all(array, 'z', 0, 0, tiled=True)]
    all_to_all x4, waiting for transfers between devices: 5.87 us -> 9.36 us  [over_chips(): return lax.all_to_all(array, ('x', 'y'), 0, 0, tiled=True)]
  transfers between devices with their start and end apart: 28 -> 29, of which waited for: 15 -> 16; matrix products, arithmetic and copies ran while one was open for 5% -> 8% of each run, Pallas kernels for 17% -> 23%
where the time goes in v3:
time: 192 us
  starting transfers between devices  75.9 us (40%)
  waiting for transfers between devices  47.1 us (25%)
  Pallas kernels  45.9 us (24%)
  matrix products  18.8 us (10%)
  local copies, waits for them, and re-layouts  2.82 us (1%)
    pallas_call x13, Pallas kernels, kernel_call(): pl.pallas_call(body, grid_spec=pltpu.PrefetchScalarGridSpec(num_scalar_pr...  45.9 us
    ppermute x17, starting transfers between devices, swap(): return lax.ppermute(array, axis, SWAP)  27.8 us
    all_to_all x4, starting transfers between devices, over_chips(): return lax.all_to_all(array, ('x', 'y'), 0, 0, tiled=True)  21.1 us
    ppermute x17, waiting for transfers between devices, swap(): return lax.ppermute(array, axis, SWAP)  16.3 us
    ppermute x6, waiting for transfers between devices, along_z(): lax.ppermute(a, 'z', route)  16.1 us
    ppermute x6, starting transfers between devices, along_z(): lax.ppermute(a, 'z', route)  15.6 us
    all_to_all x2, starting transfers between devices, over_planes(): return lax.all_to_all(array, 'z', 0, 0, tiled=True)  11.5 us
    dot_general x4, matrix products, project(): jnp.dot(rows_of, lax.dynamic_slice_in_dim(weight, chip * 2 * width, 2 * w...  10.4 us
  transfers between devices with their start and end apart: 29, of which 16 were waited for; matrix products, arithmetic and copies ran while one was open for 8% of the time, Pallas kernels for 23%

profile of v3, /device:TPU:1, one launch (start us, length us, event | category | flops | bytes accessed | tf_op | source)
XLA Modules:
  0.0 191.5 jit_solution(16623898303532219323)
XLA Ops:
  12.1 8.0 %all-to-all-start = ((bf16[4,32,2560]{2,1,0:T(8,128)(2,1)}), bf16[4,32,2560]{2,1,0:T(8,128)(2,1)S(1)}, u32[]{:S(2)}, u32[]{:S(2)}) async-start(bf16[4,32,2560]{2,1,0:T(8,128)(2,1)} %keep_keys.1), calls=%async_computation | async-start | bytes 1310720 | tf_op jit(solution)/shard_map/all_to_all | solution.py:418
  30.7 5.2 %all-to-all-done = bf16[4,32,2560]{2,1,0:T(8,128)(2,1)S(1)} async-done(((bf16[4,32,2560]{2,1,0:T(8,128)(2,1)}), bf16[4,32,2560]{2,1,0:T(8,128)(2,1)S(1)}, u32[]{:S(2)}, u32[]{:S(2)}) %all-to-all-start) | async-done | bytes 655392 | tf_op jit(solution)/shard_map/all_to_all | solution.py:418
  37.3 6.8 %all-to-all-start.1 = ((bf16[16,176,256]{2,1,0:T(8,128)(2,1)}), bf16[16,176,256]{2,1,0:T(8,128)(2,1)S(1)}, u32[]{:S(2)}, u32[]{:S(2)}) async-start(bf16[16,176,256]{2,1,0:T(8,128)(2,1)} %pack_keys.1), calls=%async_computation.1 | async-start | bytes 2883584 | tf_op jit(solution)/shard_map/all_to_all | solution.py:238
  46.3 3.9 %collective-permute-start.10 = (bf16[32,1920]{1,0:T(8,128)(2,1)}, bf16[32,1920]{1,0:T(8,128)(2,1)S(1)}, u32[]{:S(2)}, u32[]{:S(2)}) collective-permute-start(bf16[32,1920]{1,0:T(8,128)(2,1)} %copy-done.4), channel_id=1, source_target_pairs={{0,4},{4,8},{8,12},{12,0},{1,5},{5,9},{9,13},{13,1},{2,6},{6,10},{... | collective-permute-start | bytes 368648 | tf_op jit(solution)/shard_map/ppermute | solution.py:234
  53.5 2.9 %collective-permute-done.10.refs_1_ = bf16[32,1920]{1,0:T(8,128)(2,1)S(1)} collective-permute-done((bf16[32,1920]{1,0:T(8,128)(2,1)}, bf16[32,1920]{1,0:T(8,128)(2,1)S(1)}, u32[]{:S(2)}, u32[]{:S(2)}) %collective-permute-start.10) | collective-permute-done | bytes 122912 | tf_op jit(solution)/shard_map/ppermute | solution.py:234
  56.4 4.7 %collective-permute-done.11.refs_2_ = bf16[32,1920]{1,0:T(8,128)(2,1)S(1)} collective-permute-done((bf16[32,1920]{1,0:T(8,128)(2,1)S(1)}, bf16[32,1920]{1,0:T(8,128)(2,1)S(1)}, u32[]{:S(2)}, u32[]{:S(2)}) %collective-permute-start.11) | collective-permute-done | bytes 122912 | tf_op jit(solution)/shard_map/ppermute | solution.py:234
  63.0 4.0 %collective-permute-start.13 = (bf16[16,176,256]{2,1,0:T(8,128)(2,1)S(1)}, bf16[16,176,256]{2,1,0:T(8,128)(2,1)}, u32[]{:S(2)}, u32[]{:S(2)}) collective-permute-start(bf16[16,176,256]{2,1,0:T(8,128)(2,1)S(1)} %all-to-all-done.1.q_ref.ka_ref), channel_id=1, source_target_pairs={{0,1},{1,0},{2,3},{3,2},{4,5},{5,4},{6,7},{7,6},{8,9},{9,8},{10,11... | collective-permute-start | bytes 4325384 | tf_op jit(solution)/shard_map/ppermute | solution.py:228
  68.9 3.9 %all-to-all-start.2 = ((bf16[16,304,128]{2,1,0:T(8,128)(2,1)}), bf16[16,304,128]{2,1,0:T(8,128)(2,1)S(1)}, u32[]{:S(2)}, u32[]{:S(2)}) async-start(bf16[16,304,128]{2,1,0:T(8,128)(2,1)} %pack_values.1), calls=%async_computation.2 | async-start | bytes 2490368 | tf_op jit(solution)/shard_map/all_to_all | solution.py:238
  72.8 12.9 %weights.1 = (bf16[4096,768]{1,0:T(8,128)(2,1)}, bf16[4096,768]{1,0:T(8,128)(2,1)}) custom-call(s32[1]{0:T(128)} %bitcast.1.z_ref, bf16[16,176,256]{2,1,0:T(8,128)(2,1)S(1)} %all-to-all-done.1.q_ref.ka_ref, bf16[16,176,256]{2,1,0:T(8,128)(2,1)S(1)} %all-to-all-done.1.q_ref.ka_ref, bf16[16,176,256]{2,1,0:T(8,128)(2,1)} %collective-permute-done.13.kb_ref), custom_call_target="tpu_custom_call" | custom-call | flops 3221225472 | bytes 33554432 | tf_op jit(solution)/shard_map/weights/pallas_call | solution.py:158
  85.7 7.3 %all-to-all-done.2.g_ref.va_ref = bf16[16,304,128]{2,1,0:T(8,128)(2,1)S(1)} async-done(((bf16[16,304,128]{2,1,0:T(8,128)(2,1)}), bf16[16,304,128]{2,1,0:T(8,128)(2,1)S(1)}, u32[]{:S(2)}, u32[]{:S(2)}) %all-to-all-start.2) | async-done | bytes 1245216 | tf_op jit(solution)/shard_map/all_to_all | solution.py:238
  97.9 8.3 %values.1 = (bf16[16,48,256]{2,1,0:T(8,128)(2,1)}, f32[1,768]{1,0:T(1,128)S(1)}) custom-call(s32[1]{0:T(128)} %bitcast.1.z_ref, bf16[16,304,128]{2,1,0:T(8,128)(2,1)S(1)} %all-to-all-done.2.g_ref.va_ref, bf16[16,304,128]{2,1,0:T(8,128)(2,1)S(1)} %all-to-all-done.2.g_ref.va_ref, bf16[16,304,128]{2,1,0:T(8,128)(2,1)} %copy-done.5, ...), custom_call_target="tpu_custom_call" | custom-call | flops 2415919104 | bytes 16777216 | tf_op jit(solution)/shard_map/values/pallas_call | solution.py:158
  106.2 3.6 %all-to-all-start.3 = ((bf16[16,48,256]{2,1,0:T(8,128)(2,1)}), bf16[16,48,256]{2,1,0:T(8,128)(2,1)S(1)}, u32[]{:S(2)}, u32[]{:S(2)}) async-start(bf16[16,48,256]{2,1,0:T(8,128)(2,1)} %get-tuple-element.74), calls=%async_computation.3 | async-start | bytes 786432 | tf_op jit(solution)/shard_map/all_to_all | solution.py:238
  109.8 12.1 %grads.1 = (bf16[16,48,128]{2,1,0:T(8,128)(2,1)S(1)}, bf16[16,256,128]{2,1,0:T(8,128)(2,1)S(1)}, bf16[16,256,128]{2,1,0:T(8,128)(2,1)}) custom-call(s32[1]{0:T(128)} %bitcast.1.z_ref, bf16[16,176,256]{2,1,0:T(8,128)(2,1)} %copy-done.1, bf16[16,304,128]{2,1,0:T(8,128)(2,1)} %copy-done, bf16[16,176,256]{2,1,0:T(8,128)(2,1)} %copy-done.1, ...), custom_call_target="tpu_custom_call" | custom-call | flops 4026531840 | bytes 33554432 | tf_op jit(solution)/shard_map/grads/pallas_call | solution.py:158
  128.3 6.9 %all-to-all-start.4 = ((bf16[16,304,128]{2,1,0:T(8,128)(2,1)}), bf16[16,304,128]{2,1,0:T(8,128)(2,1)S(1)}, u32[]{:S(2)}, u32[]{:S(2)}) async-start(bf16[16,304,128]{2,1,0:T(8,128)(2,1)} %merge.1), calls=%async_computation.4 | async-start | bytes 2490368 | tf_op jit(solution)/shard_map/all_to_all | solution.py:238
  135.8 5.0 %collective-permute-start.16 = (bf16[32,1280]{1,0:T(8,128)(2,1)S(1)}, bf16[32,1280]{1,0:T(8,128)(2,1)S(1)}, u32[]{:S(2)}, u32[]{:S(2)}) collective-permute-start(bf16[32,1280]{1,0:T(8,128)(2,1)S(1)} %get-tuple-element.85), channel_id=1, source_target_pairs={{0,4},{4,8},{8,12},{12,0},{1,5},{5,9},{9,13},{13,1},{2,6},{6,10},{... | collective-permute-start | bytes 245768 | tf_op jit(solution)/shard_map/ppermute | solution.py:234
  144.5 3.5 %collective-permute-done.17.refs_2_ = bf16[32,1280]{1,0:T(8,128)(2,1)S(1)} collective-permute-done((bf16[32,1280]{1,0:T(8,128)(2,1)S(1)}, bf16[32,1280]{1,0:T(8,128)(2,1)S(1)}, u32[]{:S(2)}, u32[]{:S(2)}) %collective-permute-start.17) | collective-permute-done | bytes 81952 | tf_op jit(solution)/shard_map/ppermute | solution.py:234
  148.1 4.7 %collective-permute-done.18.refs_3_ = bf16[32,1280]{1,0:T(8,128)(2,1)S(1)} collective-permute-done((bf16[32,1280]{1,0:T(8,128)(2,1)S(1)}, bf16[32,1280]{1,0:T(8,128)(2,1)S(1)}, u32[]{:S(2)}, u32[]{:S(2)}) %collective-permute-start.18) | collective-permute-done | bytes 81952 | tf_op jit(solution)/shard_map/ppermute | solution.py:234
  153.5 2.6 %fusion.4 = f32[128,2560]{1,0:T(8,128)S(1)} fusion(bf16[128,640]{1,0:T(8,128)(2,1)S(1)} %get-tuple-element.93, bf16[640,5120]{1,0:T(8,128)(2,1)} %param.14, s32[]{:T(128)S(6)} %select_n.25), kind=kOutput, calls=%fused_computation.6 | convolution fusion | flops 419430400 | bytes 4751364 | tf_op jit(solution)/shard_map/dot_general | solution.py:489
  156.2 2.6 %fusion.1 = bf16[128,2560]{1,0:T(8,128)(2,1)S(1)} fusion(f32[128,2560]{1,0:T(8,128)S(1)} %fusion.4, bf16[128,640]{1,0:T(8,128)(2,1)S(1)} %get-tuple-element.94, bf16[640,5120]{1,0:T(8,128)(2,1)} %collective-permute-done.19, s32[]{:T(128)S(6)} %select_n.25), kind=kOutput, calls=%fused_computation.3 | convolution fusion | flops 420085760 | bytes 5406724 | tf_op jit(solution)/shard_map/dot_general | solution.py:489
  158.8 3.8 %collective-permute-start.20 = (bf16[128,2560]{1,0:T(8,128)(2,1)S(1)}, bf16[128,2560]{1,0:T(8,128)(2,1)S(1)}, u32[]{:S(2)}, u32[]{:S(2)}) collective-permute-start(bf16[128,2560]{1,0:T(8,128)(2,1)S(1)} %fusion.1), channel_id=1, source_target_pairs={{0,2},{2,0},{1,3},{3,1},{4,6},{6,4},{5,7},{7,5},{8,10},{10,8},{9,1... | collective-permute-start | bytes 1966088 | tf_op jit(solution)/shard_map/ppermute | solution.py:228
  163.5 3.5 %all-to-all-start.5 = ((bf16[4,32,1920]{2,1,0:T(8,128)(2,1)}), bf16[4,32,1920]{2,1,0:T(8,128)(2,1)S(1)}, u32[]{:S(2)}, u32[]{:S(2)}) async-start(bf16[4,32,1920]{2,1,0:T(8,128)(2,1)} %unpack_grads.1), calls=%async_computation.5 | async-start | bytes 983040 | tf_op jit(solution)/shard_map/all_to_all | solution.py:418
  169.5 7.4 %collective-permute-done.20 = bf16[128,2560]{1,0:T(8,128)(2,1)S(1)} collective-permute-done((bf16[128,2560]{1,0:T(8,128)(2,1)S(1)}, bf16[128,2560]{1,0:T(8,128)(2,1)S(1)}, u32[]{:S(2)}, u32[]{:S(2)}) %collective-permute-start.20) | collective-permute-done | bytes 655392 | tf_op jit(solution)/shard_map/ppermute | solution.py:228
  176.9 2.6 %fusion.2.keep_ref = bf16[128,2560]{1,0:T(8,128)(2,1)S(1)} fusion(f32[128,2560]{1,0:T(8,128)S(1)} %fusion.7, bf16[128,640]{1,0:T(8,128)(2,1)S(1)} %get-tuple-element.94, bf16[640,5120]{1,0:T(8,128)(2,1)} %collective-permute-done.19, s32[]{:T(128)S(6)} %select_n.24, bf16[128,2560]{1,0:T(8,128)(2,1)S(1)} %collective-permute-done.20), kind=kOutput, calls=%fused_computation.4 | convolution fusion | flops 420741120 | bytes 6062084 | tf_op jit(solution)/shard_map/dot_general | solution.py:489
  179.5 7.3 %collective-permute-start.21 = (bf16[128,2560]{1,0:T(8,128)(2,1)S(1)}, bf16[128,2560]{1,0:T(8,128)(2,1)S(1)}, u32[]{:S(2)}, u32[]{:S(2)}) collective-permute-start(bf16[128,2560]{1,0:T(8,128)(2,1)S(1)} %fusion.2.keep_ref), channel_id=1, source_target_pairs={{0,1},{1,0},{2,3},{3,2},{4,5},{5,4},{6,7},{7,6},{8,9},{9,8},{10,11... | collective-permute-start | bytes 1966088 | tf_op jit(solution)/shard_map/ppermute | solution.py:228
  (80 shorter events, 57.2 us)
Async XLA Ops:
  0.6 9.2 %collective-permute-start.4 = (bf16[2,64,1280]{2,1,0:T(8,128)(2,1)}, bf16[2,64,1280]{2,1,0:T(8,128)(2,1)S(1)}, u32[]{:S(2)}, u32[]{:S(2)}) collective-permute-start(bf16[2,64,1280]{2,1,0:T(8,128)(2,1)} %param.15), channel_id=1, source_target_pairs={{0,2},{2,0},{1,3},{3,1},{4,6},{6,4},{5,7},{7,5},{8,10},{10,8},{9,1... | collective-permute-start | bytes 983048 | tf_op jit(solution)/shard_map/ppermute | solution.py:228
  5.4 21.0 %collective-permute-start.5 = (bf16[2,64,1280]{2,1,0:T(8,128)(2,1)}, bf16[2,64,1280]{2,1,0:T(8,128)(2,1)S(1)}, u32[]{:S(2)}, u32[]{:S(2)}) collective-permute-start(bf16[2,64,1280]{2,1,0:T(8,128)(2,1)} %param.15), channel_id=1, source_target_pairs={{0,1},{1,0},{2,3},{3,2},{4,5},{5,4},{6,7},{7,6},{8,9},{9,8},{10,11... | collective-permute-start | bytes 983048 | tf_op jit(solution)/shard_map/ppermute | solution.py:228
  5.8 23.2 %collective-permute-start.7 = (bf16[2,64,640]{2,1,0:T(8,128)(2,1)}, bf16[2,64,640]{2,1,0:T(8,128)(2,1)S(1)}, u32[]{:S(2)}, u32[]{:S(2)}) collective-permute-start(bf16[2,64,640]{2,1,0:T(8,128)(2,1)} %refs_0_.3), channel_id=1, source_target_pairs={{0,1},{1,0},{2,3},{3,2},{4,5},{5,4},{6,7},{7,6},{8,9},{9,8},{10,11... | collective-permute-start | bytes 491528 | tf_op jit(solution)/shard_map/ppermute | solution.py:228
  6.0 23.0 %collective-permute-start.8 = (bf16[2,64,640]{2,1,0:T(8,128)(2,1)}, bf16[2,64,640]{2,1,0:T(8,128)(2,1)S(1)}, u32[]{:S(2)}, u32[]{:S(2)}) collective-permute-start(bf16[2,64,640]{2,1,0:T(8,128)(2,1)} %refs_1_.3), channel_id=1, source_target_pairs={{0,1},{1,0},{2,3},{3,2},{4,5},{5,4},{6,7},{7,6},{8,9},{9,8},{10,11... | collective-permute-start | bytes 491528 | tf_op jit(solution)/shard_map/ppermute | solution.py:228
  9.9 14.4 %collective-permute-start.6 = (bf16[2,64,1280]{2,1,0:T(8,128)(2,1)S(1)}, bf16[2,64,1280]{2,1,0:T(8,128)(2,1)S(1)}, u32[]{:S(2)}, u32[]{:S(2)}) collective-permute-start(bf16[2,64,1280]{2,1,0:T(8,128)(2,1)S(1)} %collective-permute-done.4), channel_id=1, source_target_pairs={{0,1},{1,0},{2,3},{3,2},{4,5},{5,4},{6,7},{7,6},{8,9},{9,8},{10,11... | collective-permute-start | bytes 983048 | tf_op jit(solution)/shard_map/ppermute | solution.py:228
  12.1 23.9 %all-to-all-start = ((bf16[4,32,2560]{2,1,0:T(8,128)(2,1)}), bf16[4,32,2560]{2,1,0:T(8,128)(2,1)S(1)}, u32[]{:S(2)}, u32[]{:S(2)}) async-start(bf16[4,32,2560]{2,1,0:T(8,128)(2,1)} %keep_keys.1), calls=%async_computation | async-start | bytes 1310720 | tf_op jit(solution)/shard_map/all_to_all | solution.py:418
  37.3 25.7 %all-to-all-start.1 = ((bf16[16,176,256]{2,1,0:T(8,128)(2,1)}), bf16[16,176,256]{2,1,0:T(8,128)(2,1)S(1)}, u32[]{:S(2)}, u32[]{:S(2)}) async-start(bf16[16,176,256]{2,1,0:T(8,128)(2,1)} %pack_keys.1), calls=%async_computation.1 | async-start | bytes 2883584 | tf_op jit(solution)/shard_map/all_to_all | solution.py:238
  44.1 112.1 %collective-permute-start.19 = (bf16[640,5120]{1,0:T(8,128)(2,1)}, bf16[640,5120]{1,0:T(8,128)(2,1)}, u32[]{:S(2)}, u32[]{:S(2)}) collective-permute-start(bf16[640,5120]{1,0:T(8,128)(2,1)} %param.14), channel_id=1, source_target_pairs={{0,1},{1,0},{2,3},{3,2},{4,5},{5,4},{6,7},{7,6},{8,9},{9,8},{10,11... | collective-permute-start | bytes 19660808 | tf_op jit(solution)/shard_map/ppermute | solution.py:228
  46.3 10.1 %collective-permute-start.10 = (bf16[32,1920]{1,0:T(8,128)(2,1)}, bf16[32,1920]{1,0:T(8,128)(2,1)S(1)}, u32[]{:S(2)}, u32[]{:S(2)}) collective-permute-start(bf16[32,1920]{1,0:T(8,128)(2,1)} %copy-done.4), channel_id=1, source_target_pairs={{0,4},{4,8},{8,12},{12,0},{1,5},{5,9},{9,13},{13,1},{2,6},{6,10},{... | collective-permute-start | bytes 368648 | tf_op jit(solution)/shard_map/ppermute | solution.py:234
  50.2 10.8 %collective-permute-start.11 = (bf16[32,1920]{1,0:T(8,128)(2,1)S(1)}, bf16[32,1920]{1,0:T(8,128)(2,1)S(1)}, u32[]{:S(2)}, u32[]{:S(2)}) collective-permute-start(bf16[32,1920]{1,0:T(8,128)(2,1)S(1)} %get-tuple-element.62), channel_id=1, source_target_pairs={{0,8},{4,12},{8,0},{12,4},{1,9},{5,13},{9,1},{13,5},{2,10},{6,14},... | collective-permute-start | bytes 368648 | tf_op jit(solution)/shard_map/ppermute | solution.py:234
  51.8 9.2 %collective-permute-start.12 = (bf16[32,1920]{1,0:T(8,128)(2,1)S(1)}, bf16[32,1920]{1,0:T(8,128)(2,1)S(1)}, u32[]{:S(2)}, u32[]{:S(2)}) collective-permute-start(bf16[32,1920]{1,0:T(8,128)(2,1)S(1)} %get-tuple-element.63), channel_id=1, source_target_pairs={{0,12},{4,0},{8,4},{12,8},{1,13},{5,1},{9,5},{13,9},{2,14},{6,2},{... | collective-permute-start | bytes 368648 | tf_op jit(solution)/shard_map/ppermute | solution.py:234
  63.0 9.7 %collective-permute-start.13 = (bf16[16,176,256]{2,1,0:T(8,128)(2,1)S(1)}, bf16[16,176,256]{2,1,0:T(8,128)(2,1)}, u32[]{:S(2)}, u32[]{:S(2)}) collective-permute-start(bf16[16,176,256]{2,1,0:T(8,128)(2,1)S(1)} %all-to-all-done.1.q_ref.ka_ref), channel_id=1, source_target_pairs={{0,1},{1,0},{2,3},{3,2},{4,5},{5,4},{6,7},{7,6},{8,9},{9,8},{10,11... | collective-permute-start | bytes 4325384 | tf_op jit(solution)/shard_map/ppermute | solution.py:228
  68.9 24.1 %all-to-all-start.2 = ((bf16[16,304,128]{2,1,0:T(8,128)(2,1)}), bf16[16,304,128]{2,1,0:T(8,128)(2,1)S(1)}, u32[]{:S(2)}, u32[]{:S(2)}) async-start(bf16[16,304,128]{2,1,0:T(8,128)(2,1)} %pack_values.1), calls=%async_computation.2 | async-start | bytes 2490368 | tf_op jit(solution)/shard_map/all_to_all | solution.py:238
  93.0 3.8 %collective-permute-start.14 = (bf16[16,304,128]{2,1,0:T(8,128)(2,1)S(1)}, bf16[16,304,128]{2,1,0:T(8,128)(2,1)S(1)}, u32[]{:S(2)}, u32[]{:S(2)}) collective-permute-start(bf16[16,304,128]{2,1,0:T(8,128)(2,1)S(1)} %all-to-all-done.2.g_ref.va_ref), channel_id=1, source_target_pairs={{0,1},{1,0},{2,3},{3,2},{4,5},{5,4},{6,7},{7,6},{8,9},{9,8},{10,11... | collective-permute-start | bytes 3735560 | tf_op jit(solution)/shard_map/ppermute | solution.py:228
  106.2 15.6 %all-to-all-start.3 = ((bf16[16,48,256]{2,1,0:T(8,128)(2,1)}), bf16[16,48,256]{2,1,0:T(8,128)(2,1)S(1)}, u32[]{:S(2)}, u32[]{:S(2)}) async-start(bf16[16,48,256]{2,1,0:T(8,128)(2,1)} %get-tuple-element.74), calls=%async_computation.3 | async-start | bytes 786432 | tf_op jit(solution)/shard_map/all_to_all | solution.py:238
  121.8 2.9 %collective-permute-start.15 = (bf16[16,256,128]{2,1,0:T(8,128)(2,1)}, bf16[16,256,128]{2,1,0:T(8,128)(2,1)S(1)}, u32[]{:S(2)}, u32[]{:S(2)}) collective-permute-start(bf16[16,256,128]{2,1,0:T(8,128)(2,1)} %get-tuple-element.81), channel_id=1, source_target_pairs={{0,1},{1,0},{2,3},{3,2},{4,5},{5,4},{6,7},{7,6},{8,9},{9,8},{10,11... | collective-permute-start | bytes 3145736 | tf_op jit(solution)/shard_map/ppermute | solution.py:228
  128.3 24.5 %all-to-all-start.4 = ((bf16[16,304,128]{2,1,0:T(8,128)(2,1)}), bf16[16,304,128]{2,1,0:T(8,128)(2,1)S(1)}, u32[]{:S(2)}, u32[]{:S(2)}) async-start(bf16[16,304,128]{2,1,0:T(8,128)(2,1)} %merge.1), calls=%async_computation.4 | async-start | bytes 2490368 | tf_op jit(solution)/shard_map/all_to_all | solution.py:238
  135.8 8.7 %collective-permute-start.16 = (bf16[32,1280]{1,0:T(8,128)(2,1)S(1)}, bf16[32,1280]{1,0:T(8,128)(2,1)S(1)}, u32[]{:S(2)}, u32[]{:S(2)}) collective-permute-start(bf16[32,1280]{1,0:T(8,128)(2,1)S(1)} %get-tuple-element.85), channel_id=1, source_target_pairs={{0,4},{4,8},{8,12},{12,0},{1,5},{5,9},{9,13},{13,1},{2,6},{6,10},{... | collective-permute-start | bytes 245768 | tf_op jit(solution)/shard_map/ppermute | solution.py:234
  140.8 7.3 %collective-permute-start.17 = (bf16[32,1280]{1,0:T(8,128)(2,1)S(1)}, bf16[32,1280]{1,0:T(8,128)(2,1)S(1)}, u32[]{:S(2)}, u32[]{:S(2)}) collective-permute-start(bf16[32,1280]{1,0:T(8,128)(2,1)S(1)} %get-tuple-element.86), channel_id=1, source_target_pairs={{0,8},{4,12},{8,0},{12,4},{1,9},{5,13},{9,1},{13,5},{2,10},{6,14},... | collective-permute-start | bytes 245768 | tf_op jit(solution)/shard_map/ppermute | solution.py:234
  142.3 10.5 %collective-permute-start.18 = (bf16[32,1280]{1,0:T(8,128)(2,1)S(1)}, bf16[32,1280]{1,0:T(8,128)(2,1)S(1)}, u32[]{:S(2)}, u32[]{:S(2)}) collective-permute-start(bf16[32,1280]{1,0:T(8,128)(2,1)S(1)} %get-tuple-element.87), channel_id=1, source_target_pairs={{0,12},{4,0},{8,4},{12,8},{1,13},{5,1},{9,5},{13,9},{2,14},{6,2},{... | collective-permute-start | bytes 245768 | tf_op jit(solution)/shard_map/ppermute | solution.py:234
  158.8 18.1 %collective-permute-start.20 = (bf16[128,2560]{1,0:T(8,128)(2,1)S(1)}, bf16[128,2560]{1,0:T(8,128)(2,1)S(1)}, u32[]{:S(2)}, u32[]{:S(2)}) collective-permute-start(bf16[128,2560]{1,0:T(8,128)(2,1)S(1)} %fusion.1), channel_id=1, source_target_pairs={{0,2},{2,0},{1,3},{3,1},{4,6},{6,4},{5,7},{7,5},{8,10},{10,8},{9,1... | collective-permute-start | bytes 1966088 | tf_op jit(solution)/shard_map/ppermute | solution.py:228
  163.5 23.4 %all-to-all-start.5 = ((bf16[4,32,1920]{2,1,0:T(8,128)(2,1)}), bf16[4,32,1920]{2,1,0:T(8,128)(2,1)S(1)}, u32[]{:S(2)}, u32[]{:S(2)}) async-start(bf16[4,32,1920]{2,1,0:T(8,128)(2,1)} %unpack_grads.1), calls=%async_computation.5 | async-start | bytes 983040 | tf_op jit(solution)/shard_map/all_to_all | solution.py:418
  179.5 11.1 %collective-permute-start.21 = (bf16[128,2560]{1,0:T(8,128)(2,1)S(1)}, bf16[128,2560]{1,0:T(8,128)(2,1)S(1)}, u32[]{:S(2)}, u32[]{:S(2)}) collective-permute-start(bf16[128,2560]{1,0:T(8,128)(2,1)S(1)} %fusion.2.keep_ref), channel_id=1, source_target_pairs={{0,1},{1,0},{2,3},{3,2},{4,5},{5,4},{6,7},{7,6},{8,9},{9,8},{10,11... | collective-permute-start | bytes 1966088 | tf_op jit(solution)/shard_map/ppermute | solution.py:228
  186.8 3.0 %collective-permute-start.22 = (bf16[4,32,1920]{2,1,0:T(8,128)(2,1)S(1)}, bf16[4,32,1920]{2,1,0:T(8,128)(2,1)S(1)}, u32[]{:S(2)}, u32[]{:S(2)}) collective-permute-start(bf16[4,32,1920]{2,1,0:T(8,128)(2,1)S(1)} %all-to-all-done.5.back_ref), channel_id=1, source_target_pairs={{0,1},{1,0},{2,3},{3,2},{4,5},{5,4},{6,7},{7,6},{8,9},{9,8},{10,11... | collective-permute-start | bytes 1474568 | tf_op jit(solution)/shard_map/ppermute | solution.py:228
  (17 other events, 87.2 us)

commit v4 on v3

--- a/solution.py
+++ b/solution.py
@@ -12,8 +12,8 @@
 LOG2E = 1.4426950408889634
 SUB = 16
 W_GROUP, W_UNROLL = 4, 4
-V_GROUP, V_UNROLL = 8, True
-G_GROUP, G_UNROLL = 8, True
+V_GROUP = 8
+G_GROUP = 8
 VMEM_LIMIT = 52 * 2**20
 NT = (((1,), (1,)), ((), ()))
 NN = (((1,), (0,)), ((), ()))
@@ -75,77 +75,72 @@
     lax.fori_loop(0, 2 * blocks // W_GROUP, store, 0, unroll=W_UNROLL)
 
 
-def values_kernel(rows, z_ref, g_ref, va_ref, vb_ref, p_ref, w_ref, out_ref, d_ref, vt_scr):
-    blocks = va_ref.shape[0]
-    tile = p_ref.shape[1]
-
-    @pl.when(pl.program_id(0) == 0)
-    def _():
-        for half, ref in enumerate((va_ref, vb_ref)):
-            def turn(j, carry, half=half, ref=ref):
-                here = key_rows(half, j, V_GROUP, blocks, rows)
-                vt_scr[0:HD, here] = piece(ref, j, V_GROUP, 0, rows).T
-                vt_scr[HD:, here] = piece(ref, j, V_GROUP, rows, rows).T
-                return carry
-            lax.fori_loop(0, blocks // V_GROUP, turn, 0, unroll=V_UNROLL)
-
-    def add(j, carry):
-        both, tan = carry
-        here = key_rows(0, j, V_GROUP, blocks, rows)
-        both += dot(vt_scr[:, here], p_ref[here, :])
-        tan += dot(vt_scr[0:HD, here], w_ref[here, :])
-        return both, tan
-
-    zeros = jnp.zeros((2 * HD, tile), jnp.float32), jnp.zeros((HD, tile), jnp.float32)
-    both, tan = lax.fori_loop(0, 2 * blocks // V_GROUP, add, zeros, unroll=V_UNROLL)
-    attn = both[0:HD].astype(jnp.bfloat16)
-    g = g_ref[...].reshape(tile, HD)
-    d_ref[...] = jnp.sum(attn.astype(jnp.float32) * g.astype(jnp.float32).T, axis=0, keepdims=True)
-    out_ref[:, :, 0:HD] = both[0:HD].T.astype(jnp.bfloat16).reshape(-1, SUB, HD)
-    out_ref[:, :, HD:] = (both[HD:] + SCALE * tan).T.astype(jnp.bfloat16).reshape(-1, SUB, HD)
-
-
-def grads_kernel(rows, z_ref, q_ref, g_ref, ka_ref, kb_ref, va_ref, vb_ref, p_ref, d_ref, dq_ref, oa_ref, ob_ref, kt_scr, k_scr, v_scr):
-    blocks = ka_ref.shape[0]
-    tile = p_ref.shape[1]
+def window_rows(refs):
+    return jnp.concatenate([ref[...].reshape(-1, HD) for ref in refs], axis=0)
+
+
+def put_rows(ref, lanes, value):
+    blocks, window, _ = ref.shape
+    tile = blocks * SUB
+    for i in range(window // SUB):
+        ref[:, i * SUB:(i + 1) * SUB, lanes] = value[i * tile:(i + 1) * tile].astype(ref.dtype).reshape(blocks, SUB, HD)
+
+
+def values_kernel(last, z_ref, v_ref, t_ref, p_ref, w_ref, *refs):
     step = pl.program_id(0)
-    q = q_ref[...].reshape(tile, 2 * HD)[:, HD:]
-    g = g_ref[...].reshape(tile, HD)
-    dsum = d_ref[...]
+    if last:
+        *g_refs, start_ref, out_ref, d_ref, acc = refs
+    else:
+        acc = refs[0]
+    chunk = p_ref.shape[0]
+    v = v_ref[...].reshape(chunk, HD)
+    both = jnp.concatenate([v, t_ref[...].reshape(chunk, HD)], axis=1).T
 
     @pl.when(step == 0)
     def _():
-        for half, ref in enumerate((ka_ref, kb_ref)):
-            def turn(j, carry, half=half, ref=ref):
-                kt_scr[:, key_rows(half, j, G_GROUP, blocks, rows)] = piece(ref, j, G_GROUP, 0, rows, slice(0, HD)).T
-                return carry
-            lax.fori_loop(0, blocks // G_GROUP, turn, 0, unroll=G_UNROLL)
-        k_scr[...] = jnp.zeros_like(k_scr)
-        v_scr[...] = jnp.zeros_like(v_scr)
-
-    dq = jnp.zeros((HD, tile), jnp.float32)
-    for half, ref in enumerate((va_ref, vb_ref)):
-        def add(j, dq, half=half, ref=ref):
-            here = key_rows(half, j, G_GROUP, blocks, rows)
-            p = p_ref[here, :]
-            slopes = dot(piece(ref, j, G_GROUP, 0, rows), g, NT) - dsum
-            ds = (p.astype(jnp.float32) * slopes).astype(jnp.bfloat16)
-            k_scr[here, :] += dot(ds, q)
-            v_scr[here, :] += dot(p, g)
-            return dq + dot(kt_scr[:, here], ds)
-        dq = lax.fori_loop(0, blocks // G_GROUP, add, dq, unroll=G_UNROLL)
-    dq_ref[...] = (SCALE * dq).T.astype(jnp.bfloat16).reshape(-1, SUB, HD)
-
-    @pl.when(step == pl.num_programs(0) - 1)
+        acc[...] = start_ref[...] if last else jnp.zeros_like(acc)
+
+    acc[0:2 * HD, :] += dot(both, p_ref[...])
+    acc[2 * HD:, :] += dot(both[0:HD], w_ref[...])
+
+    if last:
+        @pl.when(step == pl.num_programs(0) - 1)
+        def _():
+            g = window_rows(g_refs).astype(jnp.float32)
+            attn = acc[0:HD, :].T.astype(jnp.bfloat16)
+            dsum = jnp.sum(attn.astype(jnp.float32) * g, axis=1, keepdims=True)
+            d_ref[...] = jnp.broadcast_to(dsum, (dsum.shape[0], HD)).T[0:1, :]
+            tan = acc[HD:2 * HD, :] + SCALE * acc[2 * HD:, :]
+            put_rows(out_ref, slice(0, HD), attn)
+            put_rows(out_ref, slice(HD, 2 * HD), tan.T)
+
+
+def grads_kernel(last, z_ref, k_ref, v_ref, p_ref, d_ref, *refs):
+    step = pl.program_id(0)
+    chunk, queries = p_ref.shape
+    count = (len(refs) - (5 if last else 3)) // 2
+    q, g, refs = window_rows(refs[:count]), window_rows(refs[count:2 * count]), refs[2 * count:]
+    if last:
+        start_ref, dk_ref, dv_ref, dq_ref, acc = refs
+    else:
+        dk_ref, dv_ref, acc = refs
+    k = k_ref[...].reshape(chunk, HD)
+    v = v_ref[...].reshape(chunk, HD)
+    p = p_ref[...]
+
+    @pl.when(step == 0)
     def _():
-        for half, ref in enumerate((oa_ref, ob_ref)):
-            def give(j, carry, half=half, ref=ref):
-                here = key_rows(half, j, G_GROUP, blocks, rows)
-                group = pl.ds(j * G_GROUP, G_GROUP)
-                ref[group, 0:rows, :] = (SCALE * k_scr[here, :]).astype(jnp.bfloat16).reshape(G_GROUP, rows, HD)
-                ref[group, rows:, :] = v_scr[here, :].astype(jnp.bfloat16).reshape(G_GROUP, rows, HD)
-                return carry
-            lax.fori_loop(0, blocks // G_GROUP, give, 0, unroll=G_UNROLL)
+        acc[...] = start_ref[...] if last else jnp.zeros_like(acc)
+
+    ds = (p.astype(jnp.float32) * (dot(v, g, NT) - d_ref[...])).astype(jnp.bfloat16)
+    dk_ref[...] = (SCALE * dot(ds, q)).astype(jnp.bfloat16).reshape(dk_ref.shape)
+    dv_ref[...] = dot(p, g).astype(jnp.bfloat16).reshape(dv_ref.shape)
+    acc[...] += dot(k.T, ds)
+
+    if last:
+        @pl.when(step == pl.num_programs(0) - 1)
+        def _():
+            put_rows(dq_ref, slice(0, HD), (SCALE * acc[...]).T)
 
 
 def whole(array):
@@ -192,32 +187,69 @@
         8 * keys * grid * tile * HD, 32 * 2**20)
 
 
+def windows(array, first, window, lane):
+    blocks = array.shape[0]
+    return [
+        (array, pl.BlockSpec((blocks, SUB, HD), lambda i, s, at=first // SUB + part: (0, at, lane)))
+        for part in range(window // SUB)
+    ]
+
+
 def attention_values(z, recv_v, other_v, probs, weights, rows, window):
     blocks = recv_v.shape[0]
-    _, g_spec, p_spec, d_spec, keys, tile, grid = specs(blocks, rows, window)
+    keys, queries = probs.shape
+    half = blocks // V_GROUP
+    sums = jax.ShapeDtypeStruct((3 * HD, queries), jnp.float32)
     out_shape = jax.ShapeDtypeStruct((blocks, window, 2 * HD), jnp.bfloat16)
-    d_shape = jax.ShapeDtypeStruct((1, grid * tile), jnp.float32)
+    d_shape = jax.ShapeDtypeStruct((1, queries), jnp.float32)
+
+    def ins(array, first):
+        p_spec = pl.BlockSpec((V_GROUP * rows, queries), lambda i, s: (first + i, 0))
+        return [
+            (array, pl.BlockSpec((V_GROUP, rows, HD), lambda i, s: (i, 0, 0))),
+            (array, pl.BlockSpec((V_GROUP, rows, HD), lambda i, s: (i, 1, 0))),
+            (probs, p_spec), (weights, p_spec),
+        ]
+
+    start = kernel_call(
+        functools.partial(values_kernel, False), "values_own", half, z, ins(recv_v, 0),
+        [(sums, whole(sums))], [], 3 * keys * queries * HD, 8 * 2**20)[0]
+    g = windows(recv_v, 2 * rows, window, 0)
     return kernel_call(
-        functools.partial(values_kernel, rows), "values", grid, z,
-        [(recv_v, g_spec), (recv_v, whole(recv_v)), (other_v, whole(other_v)), (probs, p_spec), (weights, p_spec)],
-        [(out_shape, pl.BlockSpec((blocks, SUB, 2 * HD), lambda i, s: (0, i, 0))), (d_shape, d_spec)],
-        [pltpu.VMEM((2 * HD, keys), jnp.bfloat16)],
-        6 * keys * grid * tile * HD, 16 * 2**20)
+        functools.partial(values_kernel, True), "values_other", half, z,
+        ins(other_v, half) + g + [(start, whole(start))],
+        [(out_shape, whole(out_shape)), (d_shape, whole(d_shape))],
+        [pltpu.VMEM(sums.shape, sums.dtype)], 3 * keys * queries * HD, 8 * 2**20)
 
 
 def attention_grads(z, recv_k, other_k, recv_v, other_v, probs, dsum, rows, window):
     blocks = recv_v.shape[0]
-    q_spec, g_spec, p_spec, d_spec, keys, tile, grid = specs(blocks, rows, window)
+    keys, queries = probs.shape
+    half = blocks // G_GROUP
     dq_shape = jax.ShapeDtypeStruct((blocks, window, HD), jnp.bfloat16)
-    shape = jax.ShapeDtypeStruct((blocks, 2 * rows, HD), jnp.bfloat16)
-    return kernel_call(
-        functools.partial(grads_kernel, rows), "grads", grid, z,
-        [(recv_k, q_spec), (recv_v, g_spec), (recv_k, whole(recv_k)), (other_k, whole(other_k)),
-         (recv_v, whole(recv_v)), (other_v, whole(other_v)), (probs, p_spec), (dsum, d_spec)],
-        [(dq_shape, pl.BlockSpec((blocks, SUB, HD), lambda i, s: (0, i, 0))),
-         (shape, whole(shape)), (shape, whole(shape))],
-        [pltpu.VMEM((HD, keys), jnp.bfloat16), pltpu.VMEM((keys, HD), jnp.float32), pltpu.VMEM((keys, HD), jnp.float32)],
-        10 * keys * grid * tile * HD, 32 * 2**20)
+    shape = jax.ShapeDtypeStruct((blocks, rows, HD), jnp.bfloat16)
+    sums = jax.ShapeDtypeStruct((HD, queries), jnp.float32)
+    g = windows(recv_v, 2 * rows, window, 0)
+    q = windows(recv_k, rows, window, 1)
+
+    def ins(k, v, first):
+        block = pl.BlockSpec((G_GROUP, rows, HD), lambda i, s: (i, 0, 0))
+        return [
+            (k, block), (v, block),
+            (probs, pl.BlockSpec((G_GROUP * rows, queries), lambda i, s: (first + i, 0))),
+            (dsum, whole(dsum)),
+        ] + q + g
+
+    out = (shape, pl.BlockSpec((G_GROUP, rows, HD), lambda i, s: (i, 0, 0)))
+    other_dk, other_dv, start = kernel_call(
+        functools.partial(grads_kernel, False), "grads_other", half, z, ins(other_k, other_v, half),
+        [out, out, (sums, whole(sums))], [], 5 * keys * queries * HD, 8 * 2**20)
+    own_dk, own_dv, dq = kernel_call(
+        functools.partial(grads_kernel, True), "grads_own", half, z,
+        ins(recv_k, recv_v, 0) + [(start, whole(start))],
+        [out, out, (dq_shape, whole(dq_shape))],
+        [pltpu.VMEM(sums.shape, sums.dtype)], 5 * keys * queries * HD, 8 * 2**20)
+    return dq, (own_dk, own_dv), (other_dk, other_dv)
 
 
 THIRDS = 3
@@ -402,11 +434,13 @@
                 out_ref[d, :, lanes] = column[d * part:(d + 1) * part]
 
 
-def merge_kernel(z_ref, own_ref, got_ref, dq_ref, out_ref):
-    rows = got_ref.shape[1]
-    total = own_ref[...].astype(jnp.float32) + got_ref[...].astype(jnp.float32)
-    out_ref[:, 0:rows, :] = total.astype(jnp.bfloat16)
-    out_ref[:, rows:, :] = dq_ref[...]
+def merge_kernel(z_ref, *refs):
+    own, got, dq_ref, out_ref = refs[:2], refs[2:4], refs[4], refs[5]
+    rows = own[0].shape[1]
+    for kind in range(2):
+        total = own[kind][...].astype(jnp.float32) + got[kind][...].astype(jnp.float32)
+        out_ref[:, kind * rows:(kind + 1) * rows, :] = total.astype(jnp.bfloat16)
+    out_ref[:, 2 * rows:, :] = dq_ref[...]
 
 
 def repack(body, name, z, ins, shapes, scratch=(), limit=VMEM_LIMIT):
@@ -439,7 +473,6 @@
     got_values = tuple(swap(kind, "c") for kind in (values, values_tan))
     kept = repack(keep_kernel, "keep_keys", core, kinds + got, [(slots, tokens // 2, len(kinds) * features)],
                   limit=60 * 2**20)[0]
-    kept, far = lax.optimization_barrier((kept, far))
     plane = over_planes(kept).reshape(rows, -1)
     cross = swap(far, "c")
     width = grad_out.shape[2]
@@ -472,16 +505,14 @@
     out, dsum = attention_values(z, recv_v, other_v, probs, weights, rows, window)
     back = over_chips(out)
     dq, own_grads, other_grads = attention_grads(z, recv_k, other_k, recv_v, other_v, probs, dsum, rows, window)
-    back, dq, own_grads, other_grads = lax.optimization_barrier((back, dq, own_grads, other_grads))
-    got = swap(other_grads, "c")
-    merged = repack(merge_kernel, "merge", z, [own_grads, got, dq], [(chips, 2 * rows + window, HD)])[0]
-    back, merged = lax.optimization_barrier((back, merged))
-    grads = over_chips(merged)
-
+    back, other_grads = lax.optimization_barrier((back, other_grads))
     shape = (tokens // 2, 2 * features)
     home = along_z(repack(functools.partial(out_unpack_kernel, heads), "unpack_out", place, [back], [shape] * slots,
                           [pltpu.VMEM((rows, 2 * features), jnp.bfloat16)]))
-    home, grads = lax.optimization_barrier((home, grads))
+    got = tuple(swap(grad, "c") for grad in other_grads)
+    merged = repack(merge_kernel, "merge", z, own_grads + got + (dq,), [(chips, 2 * rows + window, HD)])[0]
+    home, merged = lax.optimization_barrier((home, merged))
+    grads = over_chips(merged)
     own, other = repack(join_out_kernel, "join_out", place, home, [(slots * tokens // 2, features)] * 2)
 
     def project(chip):

time: 192 us -> 178 us (0.927)
  starting transfers between devices: 75.9 us -> 67.4 us
  waiting for transfers between devices: 47.1 us -> 41.9 us
    ppermute x17 -> x18, waiting for transfers between devices: 16.3 us -> 2.44 us  [swap(): return lax.ppermute(array, axis, SWAP)]
    all_to_all x4, waiting for transfers between devices: 9.36 us -> 21.2 us  [over_chips(): return lax.all_to_all(array, ('x', 'y'), 0, 0, tiled=True)]
    ppermute x17 -> x18, starting transfers between devices: 27.8 us -> 22.3 us  [swap(): return lax.ppermute(array, axis, SWAP)]
    ppermute x6, waiting for transfers between devices: 16.1 us -> 12.3 us  [along_z(): lax.ppermute(a, 'z', route)]
    all_to_all x4, starting transfers between devices: 21.1 us -> 18.7 us  [over_chips(): return lax.all_to_all(array, ('x', 'y'), 0, 0, tiled=True)]
    pallas_call x13 -> x15, Pallas kernels: 45.9 us -> 45.5 us  [kernel_call(): pl.pallas_call(body, grid_spec=pltpu.PrefetchScalarGridSpec(num_scalar_pr...]
  transfers between devices with their start and end apart: 29 -> 30, of which waited for: 16 -> 11; matrix products, arithmetic and copies ran while one was open for 8% -> 11% of each run, Pallas kernels for 23% -> 25%
where the time goes in v4:
time: 178 us; the launch traced here: 177 us
  starting transfers between devices  67.4 us (38%)
  Pallas kernels  45.5 us (26%)
  waiting for transfers between devices  41.9 us (24%)
  matrix products  18.8 us (11%)
  local copies, waits for them, and re-layouts  2.37 us (1%)
    pallas_call x15, Pallas kernels, kernel_call(): pl.pallas_call(body, grid_spec=pltpu.PrefetchScalarGridSpec(num_scalar_pr...  45.5 us
    ppermute x18, starting transfers between devices, swap(): return lax.ppermute(array, axis, SWAP)  22.3 us
    all_to_all x4, waiting for transfers between devices, over_chips(): return lax.all_to_all(array, ('x', 'y'), 0, 0, tiled=True)  21.2 us
    all_to_all x4, starting transfers between devices, over_chips(): return lax.all_to_all(array, ('x', 'y'), 0, 0, tiled=True)  18.7 us
    ppermute x6, starting transfers between devices, along_z(): lax.ppermute(a, 'z', route)  16.1 us
    ppermute x6, waiting for transfers between devices, along_z(): lax.ppermute(a, 'z', route)  12.3 us
    dot_general x4, matrix products, project(): jnp.dot(rows_of, lax.dynamic_slice_in_dim(weight, chip * 2 * width, 2 * w...  10.4 us
    all_to_all x2, starting transfers between devices, over_planes(): return lax.all_to_all(array, 'z', 0, 0, tiled=True)  10.4 us
  transfers between devices with their start and end apart: 30, of which 11 were waited for; matrix products, arithmetic and copies ran while one was open for 11% of the time, Pallas kernels for 25%

profile of v4, /device:TPU:1, one launch (start us, length us, event | category | flops | bytes accessed | tf_op | source)
XLA Modules:
  0.0 176.9 jit_solution(14645118466282044293)
XLA Ops:
  0.6 3.3 %collective-permute-start = (bf16[2,64,640]{2,1,0:T(8,128)(2,1)}, bf16[2,64,640]{2,1,0:T(8,128)(2,1)S(1)}, u32[]{:S(2)}, u32[]{:S(2)}) collective-permute-start(bf16[2,64,640]{2,1,0:T(8,128)(2,1)} %refs_0_.2), channel_id=1, source_target_pairs={{0,1},{1,0},{2,3},{3,2},{4,5},{5,4},{6,7},{7,6},{8,9},{9,8},{10,11... | collective-permute-start | bytes 491528 | tf_op jit(solution)/shard_map/ppermute | solution.py:260
  9.1 6.9 %all-to-all-start = ((bf16[4,32,2560]{2,1,0:T(8,128)(2,1)}), bf16[4,32,2560]{2,1,0:T(8,128)(2,1)S(1)}, u32[]{:S(2)}, u32[]{:S(2)}) async-start(bf16[4,32,2560]{2,1,0:T(8,128)(2,1)} %keep_keys.1), calls=%async_computation | async-start | bytes 1310720 | tf_op jit(solution)/shard_map/all_to_all | solution.py:452
  27.1 4.6 %all-to-all-done = bf16[4,32,2560]{2,1,0:T(8,128)(2,1)S(1)} async-done(((bf16[4,32,2560]{2,1,0:T(8,128)(2,1)}), bf16[4,32,2560]{2,1,0:T(8,128)(2,1)S(1)}, u32[]{:S(2)}, u32[]{:S(2)}) %all-to-all-start) | async-done | bytes 655392 | tf_op jit(solution)/shard_map/all_to_all | solution.py:452
  33.1 6.8 %all-to-all-start.1 = ((bf16[16,176,256]{2,1,0:T(8,128)(2,1)}), bf16[16,176,256]{2,1,0:T(8,128)(2,1)S(1)}, u32[]{:S(2)}, u32[]{:S(2)}) async-start(bf16[16,176,256]{2,1,0:T(8,128)(2,1)} %pack_keys.1), calls=%async_computation.1 | async-start | bytes 2883584 | tf_op jit(solution)/shard_map/all_to_all | solution.py:270
  39.8 4.6 %collective-permute-start.10 = (bf16[32,1920]{1,0:T(8,128)(2,1)S(1)}, bf16[32,1920]{1,0:T(8,128)(2,1)S(1)}, u32[]{:S(2)}, u32[]{:S(2)}) collective-permute-start(bf16[32,1920]{1,0:T(8,128)(2,1)S(1)} %get-tuple-element.57), channel_id=1, source_target_pairs={{0,4},{4,8},{8,12},{12,0},{1,5},{5,9},{9,13},{13,1},{2,6},{6,10},{... | collective-permute-start | bytes 368648 | tf_op jit(solution)/shard_map/ppermute | solution.py:266
  49.8 6.5 %collective-permute-done.11.refs_2_ = bf16[32,1920]{1,0:T(8,128)(2,1)S(1)} collective-permute-done((bf16[32,1920]{1,0:T(8,128)(2,1)S(1)}, bf16[32,1920]{1,0:T(8,128)(2,1)S(1)}, u32[]{:S(2)}, u32[]{:S(2)}) %collective-permute-start.11) | collective-permute-done | bytes 122912 | tf_op jit(solution)/shard_map/ppermute | solution.py:266
  56.3 3.8 %collective-permute-done.12.refs_3_ = bf16[32,1920]{1,0:T(8,128)(2,1)S(1)} collective-permute-done((bf16[32,1920]{1,0:T(8,128)(2,1)S(1)}, bf16[32,1920]{1,0:T(8,128)(2,1)S(1)}, u32[]{:S(2)}, u32[]{:S(2)}) %collective-permute-start.12) | collective-permute-done | bytes 122912 | tf_op jit(solution)/shard_map/ppermute | solution.py:266
  64.5 4.4 %all-to-all-start.2 = ((bf16[16,304,128]{2,1,0:T(8,128)(2,1)}), bf16[16,304,128]{2,1,0:T(8,128)(2,1)S(1)}, u32[]{:S(2)}, u32[]{:S(2)}) async-start(bf16[16,304,128]{2,1,0:T(8,128)(2,1)} %pack_values.1), calls=%async_computation.2 | async-start | bytes 2490368 | tf_op jit(solution)/shard_map/all_to_all | solution.py:270
  69.0 12.8 %weights.1 = (bf16[4096,768]{1,0:T(8,128)(2,1)}, bf16[4096,768]{1,0:T(8,128)(2,1)}) custom-call(s32[1]{0:T(128)} %bitcast.1.z_ref, bf16[16,176,256]{2,1,0:T(8,128)(2,1)S(1)} %all-to-all-done.1.q_ref.ka_ref.refs_0_.refs_1_.refs_2_.k_ref, bf16[16,176,256]{2,1,0:T(8,128)(2,1)S(1)} %all-to-all-done.1.q_ref.ka_ref.refs_0_.refs_1_.refs_2_.k_ref, ...), custom_call_target="tpu_custom_call" | custom-call | flops 3221225472 | bytes 33554432 | tf_op jit(solution)/shard_map/weights/pallas_call | solution.py:153
  81.8 6.8 %all-to-all-done.2.v_ref.t_ref.refs_0_.refs_1_.refs_2_.refs_3_.refs_4_.refs_5_ = bf16[16,304,128]{2,1,0:T(8,128)(2,1)S(1)} async-done(((bf16[16,304,128]{2,1,0:T(8,128)(2,1)}), bf16[16,304,128]{2,1,0:T(8,128)(2,1)S(1)}, u32[]{:S(2)}, u32[]{:S(2)}) %all-to-all-start.2) | async-done | bytes 1245216 | tf_op jit(solution)/shard_map/all_to_all | solution.py:270
  90.1 4.1 %values_own.1.refs_3_ = f32[384,768]{1,0:T(8,128)S(1)} custom-call(s32[1]{0:T(128)} %bitcast.1.z_ref, bf16[16,304,128]{2,1,0:T(8,128)(2,1)} %copy-done.3, bf16[16,304,128]{2,1,0:T(8,128)(2,1)} %copy-done.3, bf16[4096,768]{1,0:T(8,128)(2,1)} %get-tuple-element.68.p_ref, bf16[4096,768]{1,0:T(8,128)(2,1)} %get-tuple-element.69.w_ref), custom_call_target="tpu_custom_call" | custom-call | flops 1207959552 | bytes 8388608 | tf_op jit(solution)/shard_map/values_own/pallas_call | solution.py:153
  95.4 5.4 %values_other.1 = (bf16[16,48,256]{2,1,0:T(8,128)(2,1)}, f32[1,768]{1,0:T(1,128)S(1)}) custom-call(s32[1]{0:T(128)} %bitcast.1.z_ref, bf16[16,304,128]{2,1,0:T(8,128)(2,1)} %copy-done.4, bf16[16,304,128]{2,1,0:T(8,128)(2,1)} %copy-done.4, bf16[4096,768]{1,0:T(8,128)(2,1)} %get-tuple-element.68.p_ref, bf16[4096,768]{1,0:T(8,128)(2,1)} %get-tuple-element.69.w_ref, ...), custom_call_target="tpu_custom_call" | custom-call | flops 1207959552 | bytes 8388608 | tf_op jit(solution)/shard_map/values_other/pallas_call | solution.py:153
  100.8 3.6 %all-to-all-start.3 = ((bf16[16,48,256]{2,1,0:T(8,128)(2,1)}), bf16[16,48,256]{2,1,0:T(8,128)(2,1)S(1)}, u32[]{:S(2)}, u32[]{:S(2)}) async-start(bf16[16,48,256]{2,1,0:T(8,128)(2,1)} %get-tuple-element.70), calls=%async_computation.3 | async-start | bytes 786432 | tf_op jit(solution)/shard_map/all_to_all | solution.py:270
  104.3 5.3 %grads_other.1 = (bf16[16,128,128]{2,1,0:T(8,128)(2,1)S(1)}, bf16[16,128,128]{2,1,0:T(8,128)(2,1)S(1)}, f32[128,768]{1,0:T(8,128)S(1)}) custom-call(s32[1]{0:T(128)} %bitcast.1.z_ref, bf16[16,176,256]{2,1,0:T(8,128)(2,1)} %collective-permute-done.13.kb_ref.k_ref, bf16[16,304,128]{2,1,0:T(8,128)(2,1)} %copy-done.4, ...), custom_call_target="tpu_custom_call" | custom-call | flops 2013265920 | bytes 8388608 | tf_op jit(solution)/shard_map/grads_other/pallas_call | solution.py:153
  109.7 2.8 %all-to-all-done.3.back_ref = bf16[16,48,256]{2,1,0:T(8,128)(2,1)S(1)} async-done(((bf16[16,48,256]{2,1,0:T(8,128)(2,1)}), bf16[16,48,256]{2,1,0:T(8,128)(2,1)S(1)}, u32[]{:S(2)}, u32[]{:S(2)}) %all-to-all-start.3) | async-done | bytes 393248 | tf_op jit(solution)/shard_map/all_to_all | solution.py:270
  115.7 4.7 %collective-permute-start.15 = (bf16[32,1280]{1,0:T(8,128)(2,1)S(1)}, bf16[32,1280]{1,0:T(8,128)(2,1)S(1)}, u32[]{:S(2)}, u32[]{:S(2)}) collective-permute-start(bf16[32,1280]{1,0:T(8,128)(2,1)S(1)} %get-tuple-element.76), channel_id=1, source_target_pairs={{0,4},{4,8},{8,12},{12,0},{1,5},{5,9},{9,13},{13,1},{2,6},{6,10},{... | collective-permute-start | bytes 245768 | tf_op jit(solution)/shard_map/ppermute | solution.py:266
  123.8 5.4 %grads_own.1 = (bf16[16,128,128]{2,1,0:T(8,128)(2,1)S(1)}, bf16[16,128,128]{2,1,0:T(8,128)(2,1)S(1)}, bf16[16,48,128]{2,1,0:T(8,128)(2,1)S(1)}) custom-call(s32[1]{0:T(128)} %bitcast.1.z_ref, bf16[16,176,256]{2,1,0:T(8,128)(2,1)} %copy-done, bf16[16,304,128]{2,1,0:T(8,128)(2,1)} %copy-done.3, bf16[4096,768]{1,0:T(8,128)(2,1)} %get-tuple-element.68.p_ref, ...), custom_call_target="tpu_custom_call" | custom-call | flops 2013265920 | bytes 8388608 | tf_op jit(solution)/shard_map/grads_own/pallas_call | solution.py:153
  132.4 3.9 %all-to-all-start.4 = ((bf16[16,304,128]{2,1,0:T(8,128)(2,1)}), bf16[16,304,128]{2,1,0:T(8,128)(2,1)S(1)}, u32[]{:S(2)}, u32[]{:S(2)}) async-start(bf16[16,304,128]{2,1,0:T(8,128)(2,1)} %merge.1), calls=%async_computation.4 | async-start | bytes 2490368 | tf_op jit(solution)/shard_map/all_to_all | solution.py:270
  139.7 2.6 %fusion.1 = bf16[128,2560]{1,0:T(8,128)(2,1)S(1)} fusion(f32[128,2560]{1,0:T(8,128)S(1)} %fusion.4, bf16[128,640]{1,0:T(8,128)(2,1)S(1)} %get-tuple-element.90, bf16[640,5120]{1,0:T(8,128)(2,1)} %collective-permute-done.20, s32[]{:T(128)S(6)} %select_n.25), kind=kOutput, calls=%fused_computation.3 | convolution fusion | flops 420085760 | bytes 5406724 | tf_op jit(solution)/shard_map/dot_general | solution.py:520
  142.4 11.5 %all-to-all-done.4.back_ref = bf16[16,304,128]{2,1,0:T(8,128)(2,1)S(1)} async-done(((bf16[16,304,128]{2,1,0:T(8,128)(2,1)}), bf16[16,304,128]{2,1,0:T(8,128)(2,1)S(1)}, u32[]{:S(2)}, u32[]{:S(2)}) %all-to-all-start.4) | async-done | bytes 1245216 | tf_op jit(solution)/shard_map/all_to_all | solution.py:270
  154.8 3.5 %all-to-all-start.5 = ((bf16[4,32,1920]{2,1,0:T(8,128)(2,1)}), bf16[4,32,1920]{2,1,0:T(8,128)(2,1)S(1)}, u32[]{:S(2)}, u32[]{:S(2)}) async-start(bf16[4,32,1920]{2,1,0:T(8,128)(2,1)} %unpack_grads.1), calls=%async_computation.5 | async-start | bytes 983040 | tf_op jit(solution)/shard_map/all_to_all | solution.py:452
  160.9 2.6 %fusion.2.keep_ref = bf16[128,2560]{1,0:T(8,128)(2,1)S(1)} fusion(f32[128,2560]{1,0:T(8,128)S(1)} %fusion.7, bf16[128,640]{1,0:T(8,128)(2,1)S(1)} %get-tuple-element.90, bf16[640,5120]{1,0:T(8,128)(2,1)} %collective-permute-done.20, s32[]{:T(128)S(6)} %select_n.24, bf16[128,2560]{1,0:T(8,128)(2,1)S(1)} %collective-permute-done.21), kind=kOutput, calls=%fused_computation.4 | convolution fusion | flops 420741120 | bytes 6062084 | tf_op jit(solution)/shard_map/dot_general | solution.py:520
  163.5 3.7 %collective-permute-start.22 = (bf16[128,2560]{1,0:T(8,128)(2,1)S(1)}, bf16[128,2560]{1,0:T(8,128)(2,1)S(1)}, u32[]{:S(2)}, u32[]{:S(2)}) collective-permute-start(bf16[128,2560]{1,0:T(8,128)(2,1)S(1)} %fusion.2.keep_ref), channel_id=1, source_target_pairs={{0,1},{1,0},{2,3},{3,2},{4,5},{5,4},{6,7},{7,6},{8,9},{9,8},{10,11... | collective-permute-start | bytes 1966088 | tf_op jit(solution)/shard_map/ppermute | solution.py:260
  168.6 6.0 %collective-permute-start.23 = (bf16[4,32,1920]{2,1,0:T(8,128)(2,1)S(1)}, bf16[4,32,1920]{2,1,0:T(8,128)(2,1)S(1)}, u32[]{:S(2)}, u32[]{:S(2)}) collective-permute-start(bf16[4,32,1920]{2,1,0:T(8,128)(2,1)S(1)} %all-to-all-done.5.back_ref), channel_id=1, source_target_pairs={{0,1},{1,0},{2,3},{3,2},{4,5},{5,4},{6,7},{7,6},{8,9},{9,8},{10,11... | collective-permute-start | bytes 1474568 | tf_op jit(solution)/shard_map/ppermute | solution.py:260
  (82 shorter events, 50.1 us)
Async XLA Ops:
  4.6 13.5 %collective-permute-start.5 = (bf16[2,64,1280]{2,1,0:T(8,128)(2,1)}, bf16[2,64,1280]{2,1,0:T(8,128)(2,1)S(1)}, u32[]{:S(2)}, u32[]{:S(2)}) collective-permute-start(bf16[2,64,1280]{2,1,0:T(8,128)(2,1)} %param.15), channel_id=1, source_target_pairs={{0,2},{2,0},{1,3},{3,1},{4,6},{6,4},{5,7},{7,5},{8,10},{10,8},{9,1... | collective-permute-start | bytes 983048 | tf_op jit(solution)/shard_map/ppermute | solution.py:260
  5.2 15.4 %collective-permute-start.4 = (bf16[2,64,1280]{2,1,0:T(8,128)(2,1)}, bf16[2,64,1280]{2,1,0:T(8,128)(2,1)S(1)}, u32[]{:S(2)}, u32[]{:S(2)}) collective-permute-start(bf16[2,64,1280]{2,1,0:T(8,128)(2,1)} %param.15), channel_id=1, source_target_pairs={{0,1},{1,0},{2,3},{3,2},{4,5},{5,4},{6,7},{7,6},{8,9},{9,8},{10,11... | collective-permute-start | bytes 983048 | tf_op jit(solution)/shard_map/ppermute | solution.py:260
  5.6 19.7 %collective-permute-start.7 = (bf16[2,64,640]{2,1,0:T(8,128)(2,1)}, bf16[2,64,640]{2,1,0:T(8,128)(2,1)S(1)}, u32[]{:S(2)}, u32[]{:S(2)}) collective-permute-start(bf16[2,64,640]{2,1,0:T(8,128)(2,1)} %refs_0_.3), channel_id=1, source_target_pairs={{0,1},{1,0},{2,3},{3,2},{4,5},{5,4},{6,7},{7,6},{8,9},{9,8},{10,11... | collective-permute-start | bytes 491528 | tf_op jit(solution)/shard_map/ppermute | solution.py:260
  5.8 19.4 %collective-permute-start.8 = (bf16[2,64,640]{2,1,0:T(8,128)(2,1)}, bf16[2,64,640]{2,1,0:T(8,128)(2,1)S(1)}, u32[]{:S(2)}, u32[]{:S(2)}) collective-permute-start(bf16[2,64,640]{2,1,0:T(8,128)(2,1)} %refs_1_.3), channel_id=1, source_target_pairs={{0,1},{1,0},{2,3},{3,2},{4,5},{5,4},{6,7},{7,6},{8,9},{9,8},{10,11... | collective-permute-start | bytes 491528 | tf_op jit(solution)/shard_map/ppermute | solution.py:260
  6.1 133.6 %collective-permute-start.20 = (bf16[640,5120]{1,0:T(8,128)(2,1)}, bf16[640,5120]{1,0:T(8,128)(2,1)}, u32[]{:S(2)}, u32[]{:S(2)}) collective-permute-start(bf16[640,5120]{1,0:T(8,128)(2,1)} %param.14), channel_id=1, source_target_pairs={{0,1},{1,0},{2,3},{3,2},{4,5},{5,4},{6,7},{7,6},{8,9},{9,8},{10,11... | collective-permute-start | bytes 19660808 | tf_op jit(solution)/shard_map/ppermute | solution.py:260
  9.1 22.6 %all-to-all-start = ((bf16[4,32,2560]{2,1,0:T(8,128)(2,1)}), bf16[4,32,2560]{2,1,0:T(8,128)(2,1)S(1)}, u32[]{:S(2)}, u32[]{:S(2)}) async-start(bf16[4,32,2560]{2,1,0:T(8,128)(2,1)} %keep_keys.1), calls=%async_computation | async-start | bytes 1310720 | tf_op jit(solution)/shard_map/all_to_all | solution.py:452
  33.1 27.1 %all-to-all-start.1 = ((bf16[16,176,256]{2,1,0:T(8,128)(2,1)}), bf16[16,176,256]{2,1,0:T(8,128)(2,1)S(1)}, u32[]{:S(2)}, u32[]{:S(2)}) async-start(bf16[16,176,256]{2,1,0:T(8,128)(2,1)} %pack_keys.1), calls=%async_computation.1 | async-start | bytes 2883584 | tf_op jit(solution)/shard_map/all_to_all | solution.py:270
  39.8 10.0 %collective-permute-start.10 = (bf16[32,1920]{1,0:T(8,128)(2,1)S(1)}, bf16[32,1920]{1,0:T(8,128)(2,1)S(1)}, u32[]{:S(2)}, u32[]{:S(2)}) collective-permute-start(bf16[32,1920]{1,0:T(8,128)(2,1)S(1)} %get-tuple-element.57), channel_id=1, source_target_pairs={{0,4},{4,8},{8,12},{12,0},{1,5},{5,9},{9,13},{13,1},{2,6},{6,10},{... | collective-permute-start | bytes 368648 | tf_op jit(solution)/shard_map/ppermute | solution.py:266
  44.5 11.9 %collective-permute-start.11 = (bf16[32,1920]{1,0:T(8,128)(2,1)S(1)}, bf16[32,1920]{1,0:T(8,128)(2,1)S(1)}, u32[]{:S(2)}, u32[]{:S(2)}) collective-permute-start(bf16[32,1920]{1,0:T(8,128)(2,1)S(1)} %get-tuple-element.58), channel_id=1, source_target_pairs={{0,8},{4,12},{8,0},{12,4},{1,9},{5,13},{9,1},{13,5},{2,10},{6,14},... | collective-permute-start | bytes 368648 | tf_op jit(solution)/shard_map/ppermute | solution.py:266
  46.1 14.0 %collective-permute-start.12 = (bf16[32,1920]{1,0:T(8,128)(2,1)S(1)}, bf16[32,1920]{1,0:T(8,128)(2,1)S(1)}, u32[]{:S(2)}, u32[]{:S(2)}) collective-permute-start(bf16[32,1920]{1,0:T(8,128)(2,1)S(1)} %get-tuple-element.59), channel_id=1, source_target_pairs={{0,12},{4,0},{8,4},{12,8},{1,13},{5,1},{9,5},{13,9},{2,14},{6,2},{... | collective-permute-start | bytes 368648 | tf_op jit(solution)/shard_map/ppermute | solution.py:266
  60.1 8.8 %collective-permute-start.13 = (bf16[16,176,256]{2,1,0:T(8,128)(2,1)S(1)}, bf16[16,176,256]{2,1,0:T(8,128)(2,1)}, u32[]{:S(2)}, u32[]{:S(2)}) collective-permute-start(bf16[16,176,256]{2,1,0:T(8,128)(2,1)S(1)} %all-to-all-done.1.q_ref.ka_ref.refs_0_.refs_1_.refs_2_.k_ref), channel_id=1, source_target_pairs={{0,1},{1,0},{2,3},{3,2},{4,5},{5,4},{6,7},{7,6},{8,9},{9,8},{10,11... | collective-permute-start | bytes 4325384 | tf_op jit(solution)/shard_map/ppermute | solution.py:260
  64.5 24.1 %all-to-all-start.2 = ((bf16[16,304,128]{2,1,0:T(8,128)(2,1)}), bf16[16,304,128]{2,1,0:T(8,128)(2,1)S(1)}, u32[]{:S(2)}, u32[]{:S(2)}) async-start(bf16[16,304,128]{2,1,0:T(8,128)(2,1)} %pack_values.1), calls=%async_computation.2 | async-start | bytes 2490368 | tf_op jit(solution)/shard_map/all_to_all | solution.py:270
  88.6 5.7 %collective-permute-start.14 = (bf16[16,304,128]{2,1,0:T(8,128)(2,1)S(1)}, bf16[16,304,128]{2,1,0:T(8,128)(2,1)S(1)}, u32[]{:S(2)}, u32[]{:S(2)}) collective-permute-start(bf16[16,304,128]{2,1,0:T(8,128)(2,1)S(1)} %all-to-all-done.2.v_ref.t_ref.refs_0_.refs_1_.refs_2_.refs_3_.refs_4_.refs_5_), channel_id=1, source_target_pairs={{0,1},{1,0},{2,3},{3,2},{4,5},{5,4},{6,7},{7,6},{8,9},{9,8},{10,11... | collective-permute-start | bytes 3735560 | tf_op jit(solution)/shard_map/ppermute | solution.py:260
  100.8 11.7 %all-to-all-start.3 = ((bf16[16,48,256]{2,1,0:T(8,128)(2,1)}), bf16[16,48,256]{2,1,0:T(8,128)(2,1)S(1)}, u32[]{:S(2)}, u32[]{:S(2)}) async-start(bf16[16,48,256]{2,1,0:T(8,128)(2,1)} %get-tuple-element.70), calls=%async_computation.3 | async-start | bytes 786432 | tf_op jit(solution)/shard_map/all_to_all | solution.py:270
  112.5 9.6 %collective-permute-start.18 = (bf16[16,128,128]{2,1,0:T(8,128)(2,1)S(1)}, bf16[16,128,128]{2,1,0:T(8,128)(2,1)S(1)}, u32[]{:S(2)}, u32[]{:S(2)}) collective-permute-start(bf16[16,128,128]{2,1,0:T(8,128)(2,1)S(1)} %get-tuple-element.82), channel_id=1, source_target_pairs={{0,1},{1,0},{2,3},{3,2},{4,5},{5,4},{6,7},{7,6},{8,9},{9,8},{10,11... | collective-permute-start | bytes 1572872 | tf_op jit(solution)/shard_map/ppermute | solution.py:260
  115.1 14.1 %collective-permute-start.19 = (bf16[16,128,128]{2,1,0:T(8,128)(2,1)S(1)}, bf16[16,128,128]{2,1,0:T(8,128)(2,1)S(1)}, u32[]{:S(2)}, u32[]{:S(2)}) collective-permute-start(bf16[16,128,128]{2,1,0:T(8,128)(2,1)S(1)} %get-tuple-element.83), channel_id=1, source_target_pairs={{0,1},{1,0},{2,3},{3,2},{4,5},{5,4},{6,7},{7,6},{8,9},{9,8},{10,11... | collective-permute-start | bytes 1572872 | tf_op jit(solution)/shard_map/ppermute | solution.py:260
  115.7 16.7 %collective-permute-start.15 = (bf16[32,1280]{1,0:T(8,128)(2,1)S(1)}, bf16[32,1280]{1,0:T(8,128)(2,1)S(1)}, u32[]{:S(2)}, u32[]{:S(2)}) collective-permute-start(bf16[32,1280]{1,0:T(8,128)(2,1)S(1)} %get-tuple-element.76), channel_id=1, source_target_pairs={{0,4},{4,8},{8,12},{12,0},{1,5},{5,9},{9,13},{13,1},{2,6},{6,10},{... | collective-permute-start | bytes 245768 | tf_op jit(solution)/shard_map/ppermute | solution.py:266
  120.4 12.1 %collective-permute-start.16 = (bf16[32,1280]{1,0:T(8,128)(2,1)S(1)}, bf16[32,1280]{1,0:T(8,128)(2,1)S(1)}, u32[]{:S(2)}, u32[]{:S(2)}) collective-permute-start(bf16[32,1280]{1,0:T(8,128)(2,1)S(1)} %get-tuple-element.77), channel_id=1, source_target_pairs={{0,8},{4,12},{8,0},{12,4},{1,9},{5,13},{9,1},{13,5},{2,10},{6,14},... | collective-permute-start | bytes 245768 | tf_op jit(solution)/shard_map/ppermute | solution.py:266
  122.1 10.3 %collective-permute-start.17 = (bf16[32,1280]{1,0:T(8,128)(2,1)S(1)}, bf16[32,1280]{1,0:T(8,128)(2,1)S(1)}, u32[]{:S(2)}, u32[]{:S(2)}) collective-permute-start(bf16[32,1280]{1,0:T(8,128)(2,1)S(1)} %get-tuple-element.78), channel_id=1, source_target_pairs={{0,12},{4,0},{8,4},{12,8},{1,13},{5,1},{9,5},{13,9},{2,14},{6,2},{... | collective-permute-start | bytes 245768 | tf_op jit(solution)/shard_map/ppermute | solution.py:266
  132.4 21.5 %all-to-all-start.4 = ((bf16[16,304,128]{2,1,0:T(8,128)(2,1)}), bf16[16,304,128]{2,1,0:T(8,128)(2,1)S(1)}, u32[]{:S(2)}, u32[]{:S(2)}) async-start(bf16[16,304,128]{2,1,0:T(8,128)(2,1)} %merge.1), calls=%async_computation.4 | async-start | bytes 2490368 | tf_op jit(solution)/shard_map/all_to_all | solution.py:270
  142.3 18.6 %collective-permute-start.21 = (bf16[128,2560]{1,0:T(8,128)(2,1)S(1)}, bf16[128,2560]{1,0:T(8,128)(2,1)S(1)}, u32[]{:S(2)}, u32[]{:S(2)}) collective-permute-start(bf16[128,2560]{1,0:T(8,128)(2,1)S(1)} %fusion.1), channel_id=1, source_target_pairs={{0,2},{2,0},{1,3},{3,1},{4,6},{6,4},{5,7},{7,5},{8,10},{10,8},{9,1... | collective-permute-start | bytes 1966088 | tf_op jit(solution)/shard_map/ppermute | solution.py:260
  154.8 13.8 %all-to-all-start.5 = ((bf16[4,32,1920]{2,1,0:T(8,128)(2,1)}), bf16[4,32,1920]{2,1,0:T(8,128)(2,1)S(1)}, u32[]{:S(2)}, u32[]{:S(2)}) async-start(bf16[4,32,1920]{2,1,0:T(8,128)(2,1)} %unpack_grads.1), calls=%async_computation.5 | async-start | bytes 983040 | tf_op jit(solution)/shard_map/all_to_all | solution.py:452
  163.5 11.1 %collective-permute-start.22 = (bf16[128,2560]{1,0:T(8,128)(2,1)S(1)}, bf16[128,2560]{1,0:T(8,128)(2,1)S(1)}, u32[]{:S(2)}, u32[]{:S(2)}) collective-permute-start(bf16[128,2560]{1,0:T(8,128)(2,1)S(1)} %fusion.2.keep_ref), channel_id=1, source_target_pairs={{0,1},{1,0},{2,3},{3,2},{4,5},{5,4},{6,7},{7,6},{8,9},{9,8},{10,11... | collective-permute-start | bytes 1966088 | tf_op jit(solution)/shard_map/ppermute | solution.py:260
  168.6 7.5 %collective-permute-start.23 = (bf16[4,32,1920]{2,1,0:T(8,128)(2,1)S(1)}, bf16[4,32,1920]{2,1,0:T(8,128)(2,1)S(1)}, u32[]{:S(2)}, u32[]{:S(2)}) collective-permute-start(bf16[4,32,1920]{2,1,0:T(8,128)(2,1)S(1)} %all-to-all-done.5.back_ref), channel_id=1, source_target_pairs={{0,1},{1,0},{2,3},{3,2},{4,5},{5,4},{6,7},{7,6},{8,9},{9,8},{10,11... | collective-permute-start | bytes 1474568 | tf_op jit(solution)/shard_map/ppermute | solution.py:260
  (17 other events, 47.8 us)

commit v5 on v4

--- a/solution.py
+++ b/solution.py
@@ -79,11 +79,11 @@
     return jnp.concatenate([ref[...].reshape(-1, HD) for ref in refs], axis=0)
 
 
-def put_rows(ref, lanes, value):
-    blocks, window, _ = ref.shape
+def put_rows(ref, lanes, value, first=0):
+    blocks, height, _ = ref.shape
     tile = blocks * SUB
-    for i in range(window // SUB):
-        ref[:, i * SUB:(i + 1) * SUB, lanes] = value[i * tile:(i + 1) * tile].astype(ref.dtype).reshape(blocks, SUB, HD)
+    for i in range((height - first) // SUB):
+        ref[:, first + i * SUB:first + (i + 1) * SUB, lanes] = value[i * tile:(i + 1) * tile].astype(ref.dtype).reshape(blocks, SUB, HD)
 
 
 def values_kernel(last, z_ref, v_ref, t_ref, p_ref, w_ref, *refs):
@@ -121,7 +121,7 @@
     count = (len(refs) - (5 if last else 3)) // 2
     q, g, refs = window_rows(refs[:count]), window_rows(refs[count:2 * count]), refs[2 * count:]
     if last:
-        start_ref, dk_ref, dv_ref, dq_ref, acc = refs
+        start_ref, got_k_ref, got_v_ref, out_ref, acc = refs
     else:
         dk_ref, dv_ref, acc = refs
     k = k_ref[...].reshape(chunk, HD)
@@ -133,14 +133,22 @@
         acc[...] = start_ref[...] if last else jnp.zeros_like(acc)
 
     ds = (p.astype(jnp.float32) * (dot(v, g, NT) - d_ref[...])).astype(jnp.bfloat16)
-    dk_ref[...] = (SCALE * dot(ds, q)).astype(jnp.bfloat16).reshape(dk_ref.shape)
-    dv_ref[...] = dot(p, g).astype(jnp.bfloat16).reshape(dv_ref.shape)
+    dk = (SCALE * dot(ds, q)).reshape(k_ref.shape)
+    dv = dot(p, g).reshape(k_ref.shape)
     acc[...] += dot(k.T, ds)
 
     if last:
+        blocks, rows, _ = k_ref.shape
+        group = pl.ds(step * blocks, blocks)
+        out_ref[group, 0:rows, :] = (dk + got_k_ref[...].astype(jnp.float32)).astype(jnp.bfloat16)
+        out_ref[group, rows:2 * rows, :] = (dv + got_v_ref[...].astype(jnp.float32)).astype(jnp.bfloat16)
+
         @pl.when(step == pl.num_programs(0) - 1)
         def _():
-            put_rows(dq_ref, slice(0, HD), (SCALE * acc[...]).T)
+            put_rows(out_ref, slice(0, HD), (SCALE * acc[...]).T, 2 * rows)
+    else:
+        dk_ref[...] = dk.astype(jnp.bfloat16)
+        dv_ref[...] = dv.astype(jnp.bfloat16)
 
 
 def whole(array):
@@ -226,30 +234,29 @@
     blocks = recv_v.shape[0]
     keys, queries = probs.shape
     half = blocks // G_GROUP
-    dq_shape = jax.ShapeDtypeStruct((blocks, window, HD), jnp.bfloat16)
     shape = jax.ShapeDtypeStruct((blocks, rows, HD), jnp.bfloat16)
+    merged = jax.ShapeDtypeStruct((blocks, 2 * rows + window, HD), jnp.bfloat16)
     sums = jax.ShapeDtypeStruct((HD, queries), jnp.float32)
-    g = windows(recv_v, 2 * rows, window, 0)
-    q = windows(recv_k, rows, window, 1)
+    block = pl.BlockSpec((G_GROUP, rows, HD), lambda i, s: (i, 0, 0))
 
     def ins(k, v, first):
-        block = pl.BlockSpec((G_GROUP, rows, HD), lambda i, s: (i, 0, 0))
         return [
             (k, block), (v, block),
             (probs, pl.BlockSpec((G_GROUP * rows, queries), lambda i, s: (first + i, 0))),
             (dsum, whole(dsum)),
-        ] + q + g
-
-    out = (shape, pl.BlockSpec((G_GROUP, rows, HD), lambda i, s: (i, 0, 0)))
+        ] + windows(recv_k, rows, window, 1) + windows(recv_v, 2 * rows, window, 0)
+
     other_dk, other_dv, start = kernel_call(
         functools.partial(grads_kernel, False), "grads_other", half, z, ins(other_k, other_v, half),
-        [out, out, (sums, whole(sums))], [], 5 * keys * queries * HD, 8 * 2**20)
-    own_dk, own_dv, dq = kernel_call(
-        functools.partial(grads_kernel, True), "grads_own", half, z,
-        ins(recv_k, recv_v, 0) + [(start, whole(start))],
-        [out, out, (dq_shape, whole(dq_shape))],
-        [pltpu.VMEM(sums.shape, sums.dtype)], 5 * keys * queries * HD, 8 * 2**20)
-    return dq, (own_dk, own_dv), (other_dk, other_dv)
+        [(shape, block), (shape, block), (sums, whole(sums))], [], 5 * keys * queries * HD, 8 * 2**20)
+
+    def own(got):
+        return kernel_call(
+            functools.partial(grads_kernel, True), "grads_own", half, z,
+            ins(recv_k, recv_v, 0) + [(start, whole(start)), (got[0], block), (got[1], block)],
+            [(merged, whole(merged))], [pltpu.VMEM(sums.shape, sums.dtype)], 5 * keys * queries * HD, 8 * 2**20)[0]
+
+    return (other_dk, other_dv), own
 
 
 THIRDS = 3
@@ -434,16 +441,7 @@
                 out_ref[d, :, lanes] = column[d * part:(d + 1) * part]
 
 
-def merge_kernel(z_ref, *refs):
-    own, got, dq_ref, out_ref = refs[:2], refs[2:4], refs[4], refs[5]
-    rows = own[0].shape[1]
-    for kind in range(2):
-        total = own[kind][...].astype(jnp.float32) + got[kind][...].astype(jnp.float32)
-        out_ref[:, kind * rows:(kind + 1) * rows, :] = total.astype(jnp.bfloat16)
-    out_ref[:, 2 * rows:, :] = dq_ref[...]
-
-
-def repack(body, name, z, ins, shapes, scratch=(), limit=VMEM_LIMIT):
+def repack(body, name, z, ins, shapes, scratch=(), limit=20 * 2**20):
     shapes = [jax.ShapeDtypeStruct(s, jnp.bfloat16) for s in shapes]
     return kernel_call(body, name, 1, z, [(a, whole(a)) for a in ins], [(s, whole(s)) for s in shapes], list(scratch), limit=limit)
 
@@ -504,13 +502,13 @@
     other_v = swap(recv_v, "c")
     out, dsum = attention_values(z, recv_v, other_v, probs, weights, rows, window)
     back = over_chips(out)
-    dq, own_grads, other_grads = attention_grads(z, recv_k, other_k, recv_v, other_v, probs, dsum, rows, window)
+    other_grads, own_half = attention_grads(z, recv_k, other_k, recv_v, other_v, probs, dsum, rows, window)
     back, other_grads = lax.optimization_barrier((back, other_grads))
     shape = (tokens // 2, 2 * features)
     home = along_z(repack(functools.partial(out_unpack_kernel, heads), "unpack_out", place, [back], [shape] * slots,
                           [pltpu.VMEM((rows, 2 * features), jnp.bfloat16)]))
     got = tuple(swap(grad, "c") for grad in other_grads)
-    merged = repack(merge_kernel, "merge", z, own_grads + got + (dq,), [(chips, 2 * rows + window, HD)])[0]
+    merged = own_half(got)
     home, merged = lax.optimization_barrier((home, merged))
     grads = over_chips(merged)
     own, other = repack(join_out_kernel, "join_out", place, home, [(slots * tokens // 2, features)] * 2)

time: 178 us -> 176 us (0.989)
  waiting for transfers between devices: 41.9 us -> 45 us
  starting transfers between devices: 67.4 us -> 64.9 us
    ppermute x18, starting transfers between devices: 22.3 us -> 19.7 us  [swap(): return lax.ppermute(array, axis, SWAP)]
    pallas_call x15 -> x14, Pallas kernels: 45.5 us -> 44.4 us  [kernel_call(): pl.pallas_call(body, grid_spec=pltpu.PrefetchScalarGridSpec(num_scalar_pr...]
  transfers between devices with their start and end apart: 30 -> 30, of which waited for: 11 -> 12; matrix products, arithmetic and copies ran while one was open for 11% -> 11% of each run, Pallas kernels for 25% -> 25%
where the time goes in v5:
time: 176 us
  starting transfers between devices  64.9 us (37%)
  waiting for transfers between devices  45 us (26%)
  Pallas kernels  44.4 us (25%)
  matrix products  18.8 us (11%)
    pallas_call x14, Pallas kernels, kernel_call(): pl.pallas_call(body, grid_spec=pltpu.PrefetchScalarGridSpec(num_scalar_pr...  44.4 us
    all_to_all x4, waiting for transfers between devices, over_chips(): return lax.all_to_all(array, ('x', 'y'), 0, 0, tiled=True)  21.9 us
    ppermute x18, starting transfers between devices, swap(): return lax.ppermute(array, axis, SWAP)  19.7 us
    all_to_all x4, starting transfers between devices, over_chips(): return lax.all_to_all(array, ('x', 'y'), 0, 0, tiled=True)  18.7 us
    ppermute x6, starting transfers between devices, along_z(): lax.ppermute(a, 'z', route)  16.1 us
    ppermute x6, waiting for transfers between devices, along_z(): lax.ppermute(a, 'z', route)  13.5 us
    all_to_all x2, starting transfers between devices, over_planes(): return lax.all_to_all(array, 'z', 0, 0, tiled=True)  10.5 us
    dot_general x4, matrix products, project(): jnp.dot(rows_of, lax.dynamic_slice_in_dim(weight, chip * 2 * width, 2 * w...  10.4 us
  transfers between devices with their start and end apart: 30, of which 12 were waited for; matrix products, arithmetic and copies ran while one was open for 11% of the time, Pallas kernels for 25%

profile of v5, /device:TPU:1, one launch (start us, length us, event | category | flops | bytes accessed | tf_op | source)
XLA Modules:
  0.0 175.6 jit_solution(9879422605984970044)
XLA Ops:
  0.6 3.3 %collective-permute-start = (bf16[2,64,640]{2,1,0:T(8,128)(2,1)}, bf16[2,64,640]{2,1,0:T(8,128)(2,1)S(1)}, u32[]{:S(2)}, u32[]{:S(2)}) collective-permute-start(bf16[2,64,640]{2,1,0:T(8,128)(2,1)} %refs_0_.2), channel_id=1, source_target_pairs={{0,1},{1,0},{2,3},{3,2},{4,5},{5,4},{6,7},{7,6},{8,9},{9,8},{10,11... | collective-permute-start | bytes 491528 | tf_op jit(solution)/shard_map/ppermute | solution.py:267
  9.1 6.9 %all-to-all-start = ((bf16[4,32,2560]{2,1,0:T(8,128)(2,1)}), bf16[4,32,2560]{2,1,0:T(8,128)(2,1)S(1)}, u32[]{:S(2)}, u32[]{:S(2)}) async-start(bf16[4,32,2560]{2,1,0:T(8,128)(2,1)} %keep_keys.1), calls=%async_computation | async-start | bytes 1310720 | tf_op jit(solution)/shard_map/all_to_all | solution.py:450
  27.1 4.6 %all-to-all-done = bf16[4,32,2560]{2,1,0:T(8,128)(2,1)S(1)} async-done(((bf16[4,32,2560]{2,1,0:T(8,128)(2,1)}), bf16[4,32,2560]{2,1,0:T(8,128)(2,1)S(1)}, u32[]{:S(2)}, u32[]{:S(2)}) %all-to-all-start) | async-done | bytes 655392 | tf_op jit(solution)/shard_map/all_to_all | solution.py:450
  33.1 6.8 %all-to-all-start.1 = ((bf16[16,176,256]{2,1,0:T(8,128)(2,1)}), bf16[16,176,256]{2,1,0:T(8,128)(2,1)S(1)}, u32[]{:S(2)}, u32[]{:S(2)}) async-start(bf16[16,176,256]{2,1,0:T(8,128)(2,1)} %pack_keys.1), calls=%async_computation.1 | async-start | bytes 2883584 | tf_op jit(solution)/shard_map/all_to_all | solution.py:277
  39.9 4.6 %collective-permute-start.10 = (bf16[32,1920]{1,0:T(8,128)(2,1)S(1)}, bf16[32,1920]{1,0:T(8,128)(2,1)S(1)}, u32[]{:S(2)}, u32[]{:S(2)}) collective-permute-start(bf16[32,1920]{1,0:T(8,128)(2,1)S(1)} %get-tuple-element.54), channel_id=1, source_target_pairs={{0,4},{4,8},{8,12},{12,0},{1,5},{5,9},{9,13},{13,1},{2,6},{6,10},{... | collective-permute-start | bytes 368648 | tf_op jit(solution)/shard_map/ppermute | solution.py:273
  49.8 6.5 %collective-permute-done.11.refs_2_ = bf16[32,1920]{1,0:T(8,128)(2,1)S(1)} collective-permute-done((bf16[32,1920]{1,0:T(8,128)(2,1)S(1)}, bf16[32,1920]{1,0:T(8,128)(2,1)S(1)}, u32[]{:S(2)}, u32[]{:S(2)}) %collective-permute-start.11) | collective-permute-done | bytes 122912 | tf_op jit(solution)/shard_map/ppermute | solution.py:273
  56.3 3.8 %collective-permute-done.12.refs_3_ = bf16[32,1920]{1,0:T(8,128)(2,1)S(1)} collective-permute-done((bf16[32,1920]{1,0:T(8,128)(2,1)S(1)}, bf16[32,1920]{1,0:T(8,128)(2,1)S(1)}, u32[]{:S(2)}, u32[]{:S(2)}) %collective-permute-start.12) | collective-permute-done | bytes 122912 | tf_op jit(solution)/shard_map/ppermute | solution.py:273
  64.5 4.4 %all-to-all-start.2 = ((bf16[16,304,128]{2,1,0:T(8,128)(2,1)}), bf16[16,304,128]{2,1,0:T(8,128)(2,1)S(1)}, u32[]{:S(2)}, u32[]{:S(2)}) async-start(bf16[16,304,128]{2,1,0:T(8,128)(2,1)} %pack_values.1), calls=%async_computation.2 | async-start | bytes 2490368 | tf_op jit(solution)/shard_map/all_to_all | solution.py:277
  69.0 13.0 %weights.1 = (bf16[4096,768]{1,0:T(8,128)(2,1)}, bf16[4096,768]{1,0:T(8,128)(2,1)}) custom-call(s32[1]{0:T(128)} %bitcast.1.z_ref, bf16[16,176,256]{2,1,0:T(8,128)(2,1)S(1)} %all-to-all-done.1.q_ref.ka_ref.refs_0_.refs_1_.refs_2_.k_ref, bf16[16,176,256]{2,1,0:T(8,128)(2,1)S(1)} %all-to-all-done.1.q_ref.ka_ref.refs_0_.refs_1_.refs_2_.k_ref, ...), custom_call_target="tpu_custom_call" | custom-call | flops 3221225472 | bytes 33554432 | tf_op jit(solution)/shard_map/weights/pallas_call | solution.py:161
  82.0 6.6 %all-to-all-done.2.v_ref.t_ref.refs_0_.refs_1_.refs_2_.refs_3_.refs_4_.refs_5_ = bf16[16,304,128]{2,1,0:T(8,128)(2,1)S(1)} async-done(((bf16[16,304,128]{2,1,0:T(8,128)(2,1)}), bf16[16,304,128]{2,1,0:T(8,128)(2,1)S(1)}, u32[]{:S(2)}, u32[]{:S(2)}) %all-to-all-start.2) | async-done | bytes 1245216 | tf_op jit(solution)/shard_map/all_to_all | solution.py:277
  90.2 4.1 %values_own.1.refs_3_ = f32[384,768]{1,0:T(8,128)S(1)} custom-call(s32[1]{0:T(128)} %bitcast.1.z_ref, bf16[16,304,128]{2,1,0:T(8,128)(2,1)} %copy-done.3, bf16[16,304,128]{2,1,0:T(8,128)(2,1)} %copy-done.3, bf16[4096,768]{1,0:T(8,128)(2,1)} %get-tuple-element.65.p_ref, bf16[4096,768]{1,0:T(8,128)(2,1)} %get-tuple-element.66.w_ref), custom_call_target="tpu_custom_call" | custom-call | flops 1207959552 | bytes 8388608 | tf_op jit(solution)/shard_map/values_own/pallas_call | solution.py:161
  95.4 5.4 %values_other.1 = (bf16[16,48,256]{2,1,0:T(8,128)(2,1)}, f32[1,768]{1,0:T(1,128)S(1)}) custom-call(s32[1]{0:T(128)} %bitcast.1.z_ref, bf16[16,304,128]{2,1,0:T(8,128)(2,1)} %copy-done.4, bf16[16,304,128]{2,1,0:T(8,128)(2,1)} %copy-done.4, bf16[4096,768]{1,0:T(8,128)(2,1)} %get-tuple-element.65.p_ref, bf16[4096,768]{1,0:T(8,128)(2,1)} %get-tuple-element.66.w_ref, ...), custom_call_target="tpu_custom_call" | custom-call | flops 1207959552 | bytes 8388608 | tf_op jit(solution)/shard_map/values_other/pallas_call | solution.py:161
  100.8 3.6 %all-to-all-start.3 = ((bf16[16,48,256]{2,1,0:T(8,128)(2,1)}), bf16[16,48,256]{2,1,0:T(8,128)(2,1)S(1)}, u32[]{:S(2)}, u32[]{:S(2)}) async-start(bf16[16,48,256]{2,1,0:T(8,128)(2,1)} %get-tuple-element.67), calls=%async_computation.3 | async-start | bytes 786432 | tf_op jit(solution)/shard_map/all_to_all | solution.py:277
  104.4 5.3 %grads_other.1 = (bf16[16,128,128]{2,1,0:T(8,128)(2,1)S(1)}, bf16[16,128,128]{2,1,0:T(8,128)(2,1)S(1)}, f32[128,768]{1,0:T(8,128)S(1)}) custom-call(s32[1]{0:T(128)} %bitcast.1.z_ref, bf16[16,176,256]{2,1,0:T(8,128)(2,1)} %collective-permute-done.13.kb_ref.k_ref, bf16[16,304,128]{2,1,0:T(8,128)(2,1)} %copy-done.4, ...), custom_call_target="tpu_custom_call" | custom-call | flops 2013265920 | bytes 8388608 | tf_op jit(solution)/shard_map/grads_other/pallas_call | solution.py:161
  109.7 2.8 %all-to-all-done.3.back_ref = bf16[16,48,256]{2,1,0:T(8,128)(2,1)S(1)} async-done(((bf16[16,48,256]{2,1,0:T(8,128)(2,1)}), bf16[16,48,256]{2,1,0:T(8,128)(2,1)S(1)}, u32[]{:S(2)}, u32[]{:S(2)}) %all-to-all-start.3) | async-done | bytes 393248 | tf_op jit(solution)/shard_map/all_to_all | solution.py:277
  115.7 4.7 %collective-permute-start.15 = (bf16[32,1280]{1,0:T(8,128)(2,1)S(1)}, bf16[32,1280]{1,0:T(8,128)(2,1)S(1)}, u32[]{:S(2)}, u32[]{:S(2)}) collective-permute-start(bf16[32,1280]{1,0:T(8,128)(2,1)S(1)} %get-tuple-element.73), channel_id=1, source_target_pairs={{0,4},{4,8},{8,12},{12,0},{1,5},{5,9},{9,13},{13,1},{2,6},{6,10},{... | collective-permute-start | bytes 245768 | tf_op jit(solution)/shard_map/ppermute | solution.py:273
  123.8 6.5 %grads_own.1 = bf16[16,304,128]{2,1,0:T(8,128)(2,1)} custom-call(s32[1]{0:T(128)} %bitcast.1.z_ref, bf16[16,176,256]{2,1,0:T(8,128)(2,1)} %copy-done, bf16[16,304,128]{2,1,0:T(8,128)(2,1)} %copy-done.3, bf16[4096,768]{1,0:T(8,128)(2,1)} %get-tuple-element.65.p_ref, f32[1,768]{1,0:T(1,128)S(1)} %get-tuple-element.68.d_ref, bf16[16,176,256]{2,1,0:T(8,128)(2,1)} %copy-done, ...), custom_call_target="tpu_custom_call" | custom-call | flops 2013265920 | bytes 8388608 | tf_op jit(solution)/shard_map/grads_own/pallas_call | solution.py:161
  131.4 3.9 %all-to-all-start.4 = ((bf16[16,304,128]{2,1,0:T(8,128)(2,1)}), bf16[16,304,128]{2,1,0:T(8,128)(2,1)S(1)}, u32[]{:S(2)}, u32[]{:S(2)}) async-start(bf16[16,304,128]{2,1,0:T(8,128)(2,1)} %grads_own.1), calls=%async_computation.4 | async-start | bytes 2490368 | tf_op jit(solution)/shard_map/all_to_all | solution.py:277
  138.7 2.6 %fusion.1 = bf16[128,2560]{1,0:T(8,128)(2,1)S(1)} fusion(f32[128,2560]{1,0:T(8,128)S(1)} %fusion.4, bf16[128,640]{1,0:T(8,128)(2,1)S(1)} %get-tuple-element.84, bf16[640,5120]{1,0:T(8,128)(2,1)} %collective-permute-done.20, s32[]{:T(128)S(6)} %select_n.25), kind=kOutput, calls=%fused_computation.3 | convolution fusion | flops 420085760 | bytes 5406724 | tf_op jit(solution)/shard_map/dot_general | solution.py:518
  141.4 12.5 %all-to-all-done.4.back_ref = bf16[16,304,128]{2,1,0:T(8,128)(2,1)S(1)} async-done(((bf16[16,304,128]{2,1,0:T(8,128)(2,1)}), bf16[16,304,128]{2,1,0:T(8,128)(2,1)S(1)}, u32[]{:S(2)}, u32[]{:S(2)}) %all-to-all-start.4) | async-done | bytes 1245216 | tf_op jit(solution)/shard_map/all_to_all | solution.py:277
  154.8 3.6 %all-to-all-start.5 = ((bf16[4,32,1920]{2,1,0:T(8,128)(2,1)}), bf16[4,32,1920]{2,1,0:T(8,128)(2,1)S(1)}, u32[]{:S(2)}, u32[]{:S(2)}) async-start(bf16[4,32,1920]{2,1,0:T(8,128)(2,1)} %unpack_grads.1), calls=%async_computation.5 | async-start | bytes 983040 | tf_op jit(solution)/shard_map/all_to_all | solution.py:450
  161.0 2.6 %fusion.2.keep_ref = bf16[128,2560]{1,0:T(8,128)(2,1)S(1)} fusion(f32[128,2560]{1,0:T(8,128)S(1)} %fusion.7, bf16[128,640]{1,0:T(8,128)(2,1)S(1)} %get-tuple-element.84, bf16[640,5120]{1,0:T(8,128)(2,1)} %collective-permute-done.20, s32[]{:T(128)S(6)} %select_n.24, bf16[128,2560]{1,0:T(8,128)(2,1)S(1)} %collective-permute-done.21), kind=kOutput, calls=%fused_computation.4 | convolution fusion | flops 420741120 | bytes 6062084 | tf_op jit(solution)/shard_map/dot_general | solution.py:518
  163.6 2.8 %collective-permute-start.22 = (bf16[128,2560]{1,0:T(8,128)(2,1)S(1)}, bf16[128,2560]{1,0:T(8,128)(2,1)S(1)}, u32[]{:S(2)}, u32[]{:S(2)}) collective-permute-start(bf16[128,2560]{1,0:T(8,128)(2,1)S(1)} %fusion.2.keep_ref), channel_id=1, source_target_pairs={{0,1},{1,0},{2,3},{3,2},{4,5},{5,4},{6,7},{7,6},{8,9},{9,8},{10,11... | collective-permute-start | bytes 1966088 | tf_op jit(solution)/shard_map/ppermute | solution.py:267
  169.0 4.4 %collective-permute-start.23 = (bf16[4,32,1920]{2,1,0:T(8,128)(2,1)S(1)}, bf16[4,32,1920]{2,1,0:T(8,128)(2,1)S(1)}, u32[]{:S(2)}, u32[]{:S(2)}) collective-permute-start(bf16[4,32,1920]{2,1,0:T(8,128)(2,1)S(1)} %all-to-all-done.5.back_ref), channel_id=1, source_target_pairs={{0,1},{1,0},{2,3},{3,2},{4,5},{5,4},{6,7},{7,6},{8,9},{9,8},{10,11... | collective-permute-start | bytes 1474568 | tf_op jit(solution)/shard_map/ppermute | solution.py:267
  (79 shorter events, 49.3 us)
Async XLA Ops:
  4.6 13.5 %collective-permute-start.5 = (bf16[2,64,1280]{2,1,0:T(8,128)(2,1)}, bf16[2,64,1280]{2,1,0:T(8,128)(2,1)S(1)}, u32[]{:S(2)}, u32[]{:S(2)}) collective-permute-start(bf16[2,64,1280]{2,1,0:T(8,128)(2,1)} %param.15), channel_id=1, source_target_pairs={{0,2},{2,0},{1,3},{3,1},{4,6},{6,4},{5,7},{7,5},{8,10},{10,8},{9,1... | collective-permute-start | bytes 983048 | tf_op jit(solution)/shard_map/ppermute | solution.py:267
  5.2 15.4 %collective-permute-start.4 = (bf16[2,64,1280]{2,1,0:T(8,128)(2,1)}, bf16[2,64,1280]{2,1,0:T(8,128)(2,1)S(1)}, u32[]{:S(2)}, u32[]{:S(2)}) collective-permute-start(bf16[2,64,1280]{2,1,0:T(8,128)(2,1)} %param.15), channel_id=1, source_target_pairs={{0,1},{1,0},{2,3},{3,2},{4,5},{5,4},{6,7},{7,6},{8,9},{9,8},{10,11... | collective-permute-start | bytes 983048 | tf_op jit(solution)/shard_map/ppermute | solution.py:267
  5.6 19.7 %collective-permute-start.7 = (bf16[2,64,640]{2,1,0:T(8,128)(2,1)}, bf16[2,64,640]{2,1,0:T(8,128)(2,1)S(1)}, u32[]{:S(2)}, u32[]{:S(2)}) collective-permute-start(bf16[2,64,640]{2,1,0:T(8,128)(2,1)} %refs_0_.3), channel_id=1, source_target_pairs={{0,1},{1,0},{2,3},{3,2},{4,5},{5,4},{6,7},{7,6},{8,9},{9,8},{10,11... | collective-permute-start | bytes 491528 | tf_op jit(solution)/shard_map/ppermute | solution.py:267
  5.8 19.4 %collective-permute-start.8 = (bf16[2,64,640]{2,1,0:T(8,128)(2,1)}, bf16[2,64,640]{2,1,0:T(8,128)(2,1)S(1)}, u32[]{:S(2)}, u32[]{:S(2)}) collective-permute-start(bf16[2,64,640]{2,1,0:T(8,128)(2,1)} %refs_1_.3), channel_id=1, source_target_pairs={{0,1},{1,0},{2,3},{3,2},{4,5},{5,4},{6,7},{7,6},{8,9},{9,8},{10,11... | collective-permute-start | bytes 491528 | tf_op jit(solution)/shard_map/ppermute | solution.py:267
  6.1 132.6 %collective-permute-start.20 = (bf16[640,5120]{1,0:T(8,128)(2,1)}, bf16[640,5120]{1,0:T(8,128)(2,1)}, u32[]{:S(2)}, u32[]{:S(2)}) collective-permute-start(bf16[640,5120]{1,0:T(8,128)(2,1)} %param.14), channel_id=1, source_target_pairs={{0,1},{1,0},{2,3},{3,2},{4,5},{5,4},{6,7},{7,6},{8,9},{9,8},{10,11... | collective-permute-start | bytes 19660808 | tf_op jit(solution)/shard_map/ppermute | solution.py:267
  9.1 22.6 %all-to-all-start = ((bf16[4,32,2560]{2,1,0:T(8,128)(2,1)}), bf16[4,32,2560]{2,1,0:T(8,128)(2,1)S(1)}, u32[]{:S(2)}, u32[]{:S(2)}) async-start(bf16[4,32,2560]{2,1,0:T(8,128)(2,1)} %keep_keys.1), calls=%async_computation | async-start | bytes 1310720 | tf_op jit(solution)/shard_map/all_to_all | solution.py:450
  33.1 27.1 %all-to-all-start.1 = ((bf16[16,176,256]{2,1,0:T(8,128)(2,1)}), bf16[16,176,256]{2,1,0:T(8,128)(2,1)S(1)}, u32[]{:S(2)}, u32[]{:S(2)}) async-start(bf16[16,176,256]{2,1,0:T(8,128)(2,1)} %pack_keys.1), calls=%async_computation.1 | async-start | bytes 2883584 | tf_op jit(solution)/shard_map/all_to_all | solution.py:277
  39.9 10.0 %collective-permute-start.10 = (bf16[32,1920]{1,0:T(8,128)(2,1)S(1)}, bf16[32,1920]{1,0:T(8,128)(2,1)S(1)}, u32[]{:S(2)}, u32[]{:S(2)}) collective-permute-start(bf16[32,1920]{1,0:T(8,128)(2,1)S(1)} %get-tuple-element.54), channel_id=1, source_target_pairs={{0,4},{4,8},{8,12},{12,0},{1,5},{5,9},{9,13},{13,1},{2,6},{6,10},{... | collective-permute-start | bytes 368648 | tf_op jit(solution)/shard_map/ppermute | solution.py:273
  44.5 11.9 %collective-permute-start.11 = (bf16[32,1920]{1,0:T(8,128)(2,1)S(1)}, bf16[32,1920]{1,0:T(8,128)(2,1)S(1)}, u32[]{:S(2)}, u32[]{:S(2)}) collective-permute-start(bf16[32,1920]{1,0:T(8,128)(2,1)S(1)} %get-tuple-element.55), channel_id=1, source_target_pairs={{0,8},{4,12},{8,0},{12,4},{1,9},{5,13},{9,1},{13,5},{2,10},{6,14},... | collective-permute-start | bytes 368648 | tf_op jit(solution)/shard_map/ppermute | solution.py:273
  46.1 14.0 %collective-permute-start.12 = (bf16[32,1920]{1,0:T(8,128)(2,1)S(1)}, bf16[32,1920]{1,0:T(8,128)(2,1)S(1)}, u32[]{:S(2)}, u32[]{:S(2)}) collective-permute-start(bf16[32,1920]{1,0:T(8,128)(2,1)S(1)} %get-tuple-element.56), channel_id=1, source_target_pairs={{0,12},{4,0},{8,4},{12,8},{1,13},{5,1},{9,5},{13,9},{2,14},{6,2},{... | collective-permute-start | bytes 368648 | tf_op jit(solution)/shard_map/ppermute | solution.py:273
  60.2 8.8 %collective-permute-start.13 = (bf16[16,176,256]{2,1,0:T(8,128)(2,1)S(1)}, bf16[16,176,256]{2,1,0:T(8,128)(2,1)}, u32[]{:S(2)}, u32[]{:S(2)}) collective-permute-start(bf16[16,176,256]{2,1,0:T(8,128)(2,1)S(1)} %all-to-all-done.1.q_ref.ka_ref.refs_0_.refs_1_.refs_2_.k_ref), channel_id=1, source_target_pairs={{0,1},{1,0},{2,3},{3,2},{4,5},{5,4},{6,7},{7,6},{8,9},{9,8},{10,11... | collective-permute-start | bytes 4325384 | tf_op jit(solution)/shard_map/ppermute | solution.py:267
  64.5 24.1 %all-to-all-start.2 = ((bf16[16,304,128]{2,1,0:T(8,128)(2,1)}), bf16[16,304,128]{2,1,0:T(8,128)(2,1)S(1)}, u32[]{:S(2)}, u32[]{:S(2)}) async-start(bf16[16,304,128]{2,1,0:T(8,128)(2,1)} %pack_values.1), calls=%async_computation.2 | async-start | bytes 2490368 | tf_op jit(solution)/shard_map/all_to_all | solution.py:277
  88.6 5.7 %collective-permute-start.14 = (bf16[16,304,128]{2,1,0:T(8,128)(2,1)S(1)}, bf16[16,304,128]{2,1,0:T(8,128)(2,1)S(1)}, u32[]{:S(2)}, u32[]{:S(2)}) collective-permute-start(bf16[16,304,128]{2,1,0:T(8,128)(2,1)S(1)} %all-to-all-done.2.v_ref.t_ref.refs_0_.refs_1_.refs_2_.refs_3_.refs_4_.refs_5_), channel_id=1, source_target_pairs={{0,1},{1,0},{2,3},{3,2},{4,5},{5,4},{6,7},{7,6},{8,9},{9,8},{10,11... | collective-permute-start | bytes 3735560 | tf_op jit(solution)/shard_map/ppermute | solution.py:267
  100.8 11.7 %all-to-all-start.3 = ((bf16[16,48,256]{2,1,0:T(8,128)(2,1)}), bf16[16,48,256]{2,1,0:T(8,128)(2,1)S(1)}, u32[]{:S(2)}, u32[]{:S(2)}) async-start(bf16[16,48,256]{2,1,0:T(8,128)(2,1)} %get-tuple-element.67), calls=%async_computation.3 | async-start | bytes 786432 | tf_op jit(solution)/shard_map/all_to_all | solution.py:277
  112.5 9.6 %collective-permute-start.18 = (bf16[16,128,128]{2,1,0:T(8,128)(2,1)S(1)}, bf16[16,128,128]{2,1,0:T(8,128)(2,1)S(1)}, u32[]{:S(2)}, u32[]{:S(2)}) collective-permute-start(bf16[16,128,128]{2,1,0:T(8,128)(2,1)S(1)} %get-tuple-element.77), channel_id=1, source_target_pairs={{0,1},{1,0},{2,3},{3,2},{4,5},{5,4},{6,7},{7,6},{8,9},{9,8},{10,11... | collective-permute-start | bytes 1572872 | tf_op jit(solution)/shard_map/ppermute | solution.py:267
  115.1 8.7 %collective-permute-start.19 = (bf16[16,128,128]{2,1,0:T(8,128)(2,1)S(1)}, bf16[16,128,128]{2,1,0:T(8,128)(2,1)S(1)}, u32[]{:S(2)}, u32[]{:S(2)}) collective-permute-start(bf16[16,128,128]{2,1,0:T(8,128)(2,1)S(1)} %get-tuple-element.78), channel_id=1, source_target_pairs={{0,1},{1,0},{2,3},{3,2},{4,5},{5,4},{6,7},{7,6},{8,9},{9,8},{10,11... | collective-permute-start | bytes 1572872 | tf_op jit(solution)/shard_map/ppermute | solution.py:267
  115.7 14.6 %collective-permute-start.15 = (bf16[32,1280]{1,0:T(8,128)(2,1)S(1)}, bf16[32,1280]{1,0:T(8,128)(2,1)S(1)}, u32[]{:S(2)}, u32[]{:S(2)}) collective-permute-start(bf16[32,1280]{1,0:T(8,128)(2,1)S(1)} %get-tuple-element.73), channel_id=1, source_target_pairs={{0,4},{4,8},{8,12},{12,0},{1,5},{5,9},{9,13},{13,1},{2,6},{6,10},{... | collective-permute-start | bytes 245768 | tf_op jit(solution)/shard_map/ppermute | solution.py:273
  120.4 9.9 %collective-permute-start.16 = (bf16[32,1280]{1,0:T(8,128)(2,1)S(1)}, bf16[32,1280]{1,0:T(8,128)(2,1)S(1)}, u32[]{:S(2)}, u32[]{:S(2)}) collective-permute-start(bf16[32,1280]{1,0:T(8,128)(2,1)S(1)} %get-tuple-element.74), channel_id=1, source_target_pairs={{0,8},{4,12},{8,0},{12,4},{1,9},{5,13},{9,1},{13,5},{2,10},{6,14},... | collective-permute-start | bytes 245768 | tf_op jit(solution)/shard_map/ppermute | solution.py:273
  122.1 9.3 %collective-permute-start.17 = (bf16[32,1280]{1,0:T(8,128)(2,1)S(1)}, bf16[32,1280]{1,0:T(8,128)(2,1)S(1)}, u32[]{:S(2)}, u32[]{:S(2)}) collective-permute-start(bf16[32,1280]{1,0:T(8,128)(2,1)S(1)} %get-tuple-element.75), channel_id=1, source_target_pairs={{0,12},{4,0},{8,4},{12,8},{1,13},{5,1},{9,5},{13,9},{2,14},{6,2},{... | collective-permute-start | bytes 245768 | tf_op jit(solution)/shard_map/ppermute | solution.py:273
  131.4 22.4 %all-to-all-start.4 = ((bf16[16,304,128]{2,1,0:T(8,128)(2,1)}), bf16[16,304,128]{2,1,0:T(8,128)(2,1)S(1)}, u32[]{:S(2)}, u32[]{:S(2)}) async-start(bf16[16,304,128]{2,1,0:T(8,128)(2,1)} %grads_own.1), calls=%async_computation.4 | async-start | bytes 2490368 | tf_op jit(solution)/shard_map/all_to_all | solution.py:277
  141.3 19.7 %collective-permute-start.21 = (bf16[128,2560]{1,0:T(8,128)(2,1)S(1)}, bf16[128,2560]{1,0:T(8,128)(2,1)S(1)}, u32[]{:S(2)}, u32[]{:S(2)}) collective-permute-start(bf16[128,2560]{1,0:T(8,128)(2,1)S(1)} %fusion.1), channel_id=1, source_target_pairs={{0,2},{2,0},{1,3},{3,1},{4,6},{6,4},{5,7},{7,5},{8,10},{10,8},{9,1... | collective-permute-start | bytes 1966088 | tf_op jit(solution)/shard_map/ppermute | solution.py:267
  154.8 14.2 %all-to-all-start.5 = ((bf16[4,32,1920]{2,1,0:T(8,128)(2,1)}), bf16[4,32,1920]{2,1,0:T(8,128)(2,1)S(1)}, u32[]{:S(2)}, u32[]{:S(2)}) async-start(bf16[4,32,1920]{2,1,0:T(8,128)(2,1)} %unpack_grads.1), calls=%async_computation.5 | async-start | bytes 983040 | tf_op jit(solution)/shard_map/all_to_all | solution.py:450
  163.6 9.7 %collective-permute-start.22 = (bf16[128,2560]{1,0:T(8,128)(2,1)S(1)}, bf16[128,2560]{1,0:T(8,128)(2,1)S(1)}, u32[]{:S(2)}, u32[]{:S(2)}) collective-permute-start(bf16[128,2560]{1,0:T(8,128)(2,1)S(1)} %fusion.2.keep_ref), channel_id=1, source_target_pairs={{0,1},{1,0},{2,3},{3,2},{4,5},{5,4},{6,7},{7,6},{8,9},{9,8},{10,11... | collective-permute-start | bytes 1966088 | tf_op jit(solution)/shard_map/ppermute | solution.py:267
  169.0 5.8 %collective-permute-start.23 = (bf16[4,32,1920]{2,1,0:T(8,128)(2,1)S(1)}, bf16[4,32,1920]{2,1,0:T(8,128)(2,1)S(1)}, u32[]{:S(2)}, u32[]{:S(2)}) collective-permute-start(bf16[4,32,1920]{2,1,0:T(8,128)(2,1)S(1)} %all-to-all-done.5.back_ref), channel_id=1, source_target_pairs={{0,1},{1,0},{2,3},{3,2},{4,5},{5,4},{6,7},{7,6},{8,9},{9,8},{10,11... | collective-permute-start | bytes 1474568 | tf_op jit(solution)/shard_map/ppermute | solution.py:267
  (16 other events, 46.9 us)

commit v6 on v5

--- a/solution.py
+++ b/solution.py
@@ -13,7 +13,7 @@
 SUB = 16
 W_GROUP, W_UNROLL = 4, 4
 V_GROUP = 8
-G_GROUP = 8
+G_GROUP = 16
 VMEM_LIMIT = 52 * 2**20
 NT = (((1,), (1,)), ((), ()))
 NN = (((1,), (0,)), ((), ()))
@@ -303,14 +303,12 @@
 def keep_kernel(c_ref, *refs):
     out = refs[-1]
     kinds = len(refs) // 2
-    clips, tokens, width = refs[0].shape
-    rows = tokens // 2
+    clips, _, width = refs[0].shape
     core = c_ref[0]
-    start = pl.multiple_of(core * rows, rows)
     for part, group in ((core, refs[:kinds]), (1 - core, refs[kinds:2 * kinds])):
         for clip in range(clips):
             for index, ref in enumerate(group):
-                out[part * clips + clip, :, index * width:(index + 1) * width] = ref[clip, pl.ds(start, rows), :]
+                out[part * clips + clip, :, index * width:(index + 1) * width] = ref[clip]
 
 
 def home_kernel(c_ref, back_ref, got_ref, *outs):
@@ -469,8 +467,10 @@
     kinds = (keys, keys_tan, queries_tan, queries)
     got = tuple(swap(kind, "c") for kind in kinds)
     got_values = tuple(swap(kind, "c") for kind in (values, values_tan))
-    kept = repack(keep_kernel, "keep_keys", core, kinds + got, [(slots, tokens // 2, len(kinds) * features)],
-                  limit=60 * 2**20)[0]
+    half = pl.BlockSpec((clips, tokens // 2, features), lambda i, s: (0, s[0], 0))
+    shape = jax.ShapeDtypeStruct((slots, tokens // 2, len(kinds) * features), jnp.bfloat16)
+    kept = kernel_call(keep_kernel, "keep_keys", 1, core, [(a, half) for a in kinds + got],
+                       [(shape, whole(shape))], [], limit=60 * 2**20)[0]
     plane = over_planes(kept).reshape(rows, -1)
     cross = swap(far, "c")
     width = grad_out.shape[2]

time: 176 us -> 175 us (level)
  waiting for transfers between devices: 45 us -> 43.1 us
where the time goes in v6:
time: 175 us; the launch traced here: 174 us
  starting transfers between devices  66 us (38%)
  Pallas kernels  44 us (25%)
  waiting for transfers between devices  43.1 us (25%)
  matrix products  18.8 us (11%)
    pallas_call x14, Pallas kernels, kernel_call(): pl.pallas_call(body, grid_spec=pltpu.PrefetchScalarGridSpec(num_scalar_pr...  44 us
    all_to_all x4, waiting for transfers between devices, over_chips(): return lax.all_to_all(array, ('x', 'y'), 0, 0, tiled=True)  21.4 us
    ppermute x18, starting transfers between devices, swap(): return lax.ppermute(array, axis, SWAP)  21 us
    all_to_all x4, starting transfers between devices, over_chips(): return lax.all_to_all(array, ('x', 'y'), 0, 0, tiled=True)  18.4 us
    ppermute x6, starting transfers between devices, along_z(): lax.ppermute(a, 'z', route)  16.1 us
    ppermute x6, waiting for transfers between devices, along_z(): lax.ppermute(a, 'z', route)  13.5 us
    all_to_all x2, starting transfers between devices, over_planes(): return lax.all_to_all(array, 'z', 0, 0, tiled=True)  10.5 us
    dot_general x4, matrix products, project(): jnp.dot(rows_of, lax.dynamic_slice_in_dim(weight, chip * 2 * width, 2 * w...  10.4 us
  transfers between devices with their start and end apart: 30, of which 12 were waited for; matrix products, arithmetic and copies ran while one was open for 11% of the time, Pallas kernels for 25%

profile of v6, /device:TPU:1, one launch (start us, length us, event | category | flops | bytes accessed | tf_op | source)
XLA Modules:
  0.0 174.4 jit_solution(2176567008522327195)
XLA Ops:
  0.6 3.3 %collective-permute-start = (bf16[2,64,640]{2,1,0:T(8,128)(2,1)}, bf16[2,64,640]{2,1,0:T(8,128)(2,1)S(1)}, u32[]{:S(2)}, u32[]{:S(2)}) collective-permute-start(bf16[2,64,640]{2,1,0:T(8,128)(2,1)} %refs_0_.2), channel_id=1, source_target_pairs={{0,1},{1,0},{2,3},{3,2},{4,5},{5,4},{6,7},{7,6},{8,9},{9,8},{10,11... | collective-permute-start | bytes 491528 | tf_op jit(solution)/shard_map/ppermute | solution.py:267
  8.9 6.9 %all-to-all-start = ((bf16[4,32,2560]{2,1,0:T(8,128)(2,1)}), bf16[4,32,2560]{2,1,0:T(8,128)(2,1)S(1)}, u32[]{:S(2)}, u32[]{:S(2)}) async-start(bf16[4,32,2560]{2,1,0:T(8,128)(2,1)} %keep_keys.1), calls=%async_computation | async-start | bytes 1310720 | tf_op jit(solution)/shard_map/all_to_all | solution.py:448
  26.8 4.6 %all-to-all-done = bf16[4,32,2560]{2,1,0:T(8,128)(2,1)S(1)} async-done(((bf16[4,32,2560]{2,1,0:T(8,128)(2,1)}), bf16[4,32,2560]{2,1,0:T(8,128)(2,1)S(1)}, u32[]{:S(2)}, u32[]{:S(2)}) %all-to-all-start) | async-done | bytes 655392 | tf_op jit(solution)/shard_map/all_to_all | solution.py:448
  32.9 6.8 %all-to-all-start.1 = ((bf16[16,176,256]{2,1,0:T(8,128)(2,1)}), bf16[16,176,256]{2,1,0:T(8,128)(2,1)S(1)}, u32[]{:S(2)}, u32[]{:S(2)}) async-start(bf16[16,176,256]{2,1,0:T(8,128)(2,1)} %pack_keys.1), calls=%async_computation.1 | async-start | bytes 2883584 | tf_op jit(solution)/shard_map/all_to_all | solution.py:277
  39.6 4.6 %collective-permute-start.10 = (bf16[32,1920]{1,0:T(8,128)(2,1)S(1)}, bf16[32,1920]{1,0:T(8,128)(2,1)S(1)}, u32[]{:S(2)}, u32[]{:S(2)}) collective-permute-start(bf16[32,1920]{1,0:T(8,128)(2,1)S(1)} %get-tuple-element.54), channel_id=1, source_target_pairs={{0,4},{4,8},{8,12},{12,0},{1,5},{5,9},{9,13},{13,1},{2,6},{6,10},{... | collective-permute-start | bytes 368648 | tf_op jit(solution)/shard_map/ppermute | solution.py:273
  49.6 6.5 %collective-permute-done.11.refs_2_ = bf16[32,1920]{1,0:T(8,128)(2,1)S(1)} collective-permute-done((bf16[32,1920]{1,0:T(8,128)(2,1)S(1)}, bf16[32,1920]{1,0:T(8,128)(2,1)S(1)}, u32[]{:S(2)}, u32[]{:S(2)}) %collective-permute-start.11) | collective-permute-done | bytes 122912 | tf_op jit(solution)/shard_map/ppermute | solution.py:273
  56.1 3.8 %collective-permute-done.12.refs_3_ = bf16[32,1920]{1,0:T(8,128)(2,1)S(1)} collective-permute-done((bf16[32,1920]{1,0:T(8,128)(2,1)S(1)}, bf16[32,1920]{1,0:T(8,128)(2,1)S(1)}, u32[]{:S(2)}, u32[]{:S(2)}) %collective-permute-start.12) | collective-permute-done | bytes 122912 | tf_op jit(solution)/shard_map/ppermute | solution.py:273
  64.3 4.4 %all-to-all-start.2 = ((bf16[16,304,128]{2,1,0:T(8,128)(2,1)}), bf16[16,304,128]{2,1,0:T(8,128)(2,1)S(1)}, u32[]{:S(2)}, u32[]{:S(2)}) async-start(bf16[16,304,128]{2,1,0:T(8,128)(2,1)} %pack_values.1), calls=%async_computation.2 | async-start | bytes 2490368 | tf_op jit(solution)/shard_map/all_to_all | solution.py:277
  68.8 13.0 %weights.1 = (bf16[4096,768]{1,0:T(8,128)(2,1)}, bf16[4096,768]{1,0:T(8,128)(2,1)}) custom-call(s32[1]{0:T(128)} %bitcast.1.z_ref, bf16[16,176,256]{2,1,0:T(8,128)(2,1)S(1)} %all-to-all-done.1.q_ref.ka_ref.refs_0_.refs_1_.refs_2_.k_ref, bf16[16,176,256]{2,1,0:T(8,128)(2,1)S(1)} %all-to-all-done.1.q_ref.ka_ref.refs_0_.refs_1_.refs_2_.k_ref, ...), custom_call_target="tpu_custom_call" | custom-call | flops 3221225472 | bytes 33554432 | tf_op jit(solution)/shard_map/weights/pallas_call | solution.py:161
  81.8 6.6 %all-to-all-done.2.v_ref.t_ref.refs_0_.refs_1_.refs_2_.refs_3_.refs_4_.refs_5_ = bf16[16,304,128]{2,1,0:T(8,128)(2,1)S(1)} async-done(((bf16[16,304,128]{2,1,0:T(8,128)(2,1)}), bf16[16,304,128]{2,1,0:T(8,128)(2,1)S(1)}, u32[]{:S(2)}, u32[]{:S(2)}) %all-to-all-start.2) | async-done | bytes 1245216 | tf_op jit(solution)/shard_map/all_to_all | solution.py:277
  89.9 4.1 %values_own.1.refs_3_ = f32[384,768]{1,0:T(8,128)S(1)} custom-call(s32[1]{0:T(128)} %bitcast.1.z_ref, bf16[16,304,128]{2,1,0:T(8,128)(2,1)} %copy-done.3, bf16[16,304,128]{2,1,0:T(8,128)(2,1)} %copy-done.3, bf16[4096,768]{1,0:T(8,128)(2,1)} %get-tuple-element.65.p_ref, bf16[4096,768]{1,0:T(8,128)(2,1)} %get-tuple-element.66.w_ref), custom_call_target="tpu_custom_call" | custom-call | flops 1207959552 | bytes 8388608 | tf_op jit(solution)/shard_map/values_own/pallas_call | solution.py:161
  95.2 5.4 %values_other.1 = (bf16[16,48,256]{2,1,0:T(8,128)(2,1)}, f32[1,768]{1,0:T(1,128)S(1)}) custom-call(s32[1]{0:T(128)} %bitcast.1.z_ref, bf16[16,304,128]{2,1,0:T(8,128)(2,1)} %copy-done.4, bf16[16,304,128]{2,1,0:T(8,128)(2,1)} %copy-done.4, bf16[4096,768]{1,0:T(8,128)(2,1)} %get-tuple-element.65.p_ref, bf16[4096,768]{1,0:T(8,128)(2,1)} %get-tuple-element.66.w_ref, ...), custom_call_target="tpu_custom_call" | custom-call | flops 1207959552 | bytes 8388608 | tf_op jit(solution)/shard_map/values_other/pallas_call | solution.py:161
  100.6 3.6 %all-to-all-start.3 = ((bf16[16,48,256]{2,1,0:T(8,128)(2,1)}), bf16[16,48,256]{2,1,0:T(8,128)(2,1)S(1)}, u32[]{:S(2)}, u32[]{:S(2)}) async-start(bf16[16,48,256]{2,1,0:T(8,128)(2,1)} %get-tuple-element.67), calls=%async_computation.3 | async-start | bytes 786432 | tf_op jit(solution)/shard_map/all_to_all | solution.py:277
  104.1 5.3 %grads_other.1 = (bf16[16,128,128]{2,1,0:T(8,128)(2,1)S(1)}, bf16[16,128,128]{2,1,0:T(8,128)(2,1)S(1)}, f32[128,768]{1,0:T(8,128)S(1)}) custom-call(s32[1]{0:T(128)} %bitcast.1.z_ref, bf16[16,176,256]{2,1,0:T(8,128)(2,1)} %collective-permute-done.13.kb_ref.k_ref, bf16[16,304,128]{2,1,0:T(8,128)(2,1)} %copy-done.4, ...), custom_call_target="tpu_custom_call" | custom-call | flops 2013265920 | bytes 8388608 | tf_op jit(solution)/shard_map/grads_other/pallas_call | solution.py:161
  109.4 2.9 %all-to-all-done.3.back_ref = bf16[16,48,256]{2,1,0:T(8,128)(2,1)S(1)} async-done(((bf16[16,48,256]{2,1,0:T(8,128)(2,1)}), bf16[16,48,256]{2,1,0:T(8,128)(2,1)S(1)}, u32[]{:S(2)}, u32[]{:S(2)}) %all-to-all-start.3) | async-done | bytes 393248 | tf_op jit(solution)/shard_map/all_to_all | solution.py:277
  115.5 4.7 %collective-permute-start.15 = (bf16[32,1280]{1,0:T(8,128)(2,1)S(1)}, bf16[32,1280]{1,0:T(8,128)(2,1)S(1)}, u32[]{:S(2)}, u32[]{:S(2)}) collective-permute-start(bf16[32,1280]{1,0:T(8,128)(2,1)S(1)} %get-tuple-element.73), channel_id=1, source_target_pairs={{0,4},{4,8},{8,12},{12,0},{1,5},{5,9},{9,13},{13,1},{2,6},{6,10},{... | collective-permute-start | bytes 245768 | tf_op jit(solution)/shard_map/ppermute | solution.py:273
  123.5 6.4 %grads_own.1 = bf16[16,304,128]{2,1,0:T(8,128)(2,1)} custom-call(s32[1]{0:T(128)} %bitcast.1.z_ref, bf16[16,176,256]{2,1,0:T(8,128)(2,1)} %copy-done, bf16[16,304,128]{2,1,0:T(8,128)(2,1)} %copy-done.3, bf16[4096,768]{1,0:T(8,128)(2,1)} %get-tuple-element.65.p_ref, f32[1,768]{1,0:T(1,128)S(1)} %get-tuple-element.68.d_ref, bf16[16,176,256]{2,1,0:T(8,128)(2,1)} %copy-done, ...), custom_call_target="tpu_custom_call" | custom-call | flops 2013265920 | bytes 8388608 | tf_op jit(solution)/shard_map/grads_own/pallas_call | solution.py:161
  131.2 3.7 %all-to-all-start.4 = ((bf16[16,304,128]{2,1,0:T(8,128)(2,1)}), bf16[16,304,128]{2,1,0:T(8,128)(2,1)S(1)}, u32[]{:S(2)}, u32[]{:S(2)}) async-start(bf16[16,304,128]{2,1,0:T(8,128)(2,1)} %grads_own.1), calls=%async_computation.4 | async-start | bytes 2490368 | tf_op jit(solution)/shard_map/all_to_all | solution.py:277
  138.2 2.6 %fusion.1 = bf16[128,2560]{1,0:T(8,128)(2,1)S(1)} fusion(f32[128,2560]{1,0:T(8,128)S(1)} %fusion.4, bf16[128,640]{1,0:T(8,128)(2,1)S(1)} %get-tuple-element.84, bf16[640,5120]{1,0:T(8,128)(2,1)} %collective-permute-done.20, s32[]{:T(128)S(6)} %select_n.25), kind=kOutput, calls=%fused_computation.3 | convolution fusion | flops 420085760 | bytes 5406724 | tf_op jit(solution)/shard_map/dot_general | solution.py:518
  140.9 11.9 %all-to-all-done.4.back_ref = bf16[16,304,128]{2,1,0:T(8,128)(2,1)S(1)} async-done(((bf16[16,304,128]{2,1,0:T(8,128)(2,1)}), bf16[16,304,128]{2,1,0:T(8,128)(2,1)S(1)}, u32[]{:S(2)}, u32[]{:S(2)}) %all-to-all-start.4) | async-done | bytes 1245216 | tf_op jit(solution)/shard_map/all_to_all | solution.py:277
  153.7 3.6 %all-to-all-start.5 = ((bf16[4,32,1920]{2,1,0:T(8,128)(2,1)}), bf16[4,32,1920]{2,1,0:T(8,128)(2,1)S(1)}, u32[]{:S(2)}, u32[]{:S(2)}) async-start(bf16[4,32,1920]{2,1,0:T(8,128)(2,1)} %unpack_grads.1), calls=%async_computation.5 | async-start | bytes 983040 | tf_op jit(solution)/shard_map/all_to_all | solution.py:448
  159.9 2.6 %fusion.2.keep_ref = bf16[128,2560]{1,0:T(8,128)(2,1)S(1)} fusion(f32[128,2560]{1,0:T(8,128)S(1)} %fusion.7, bf16[128,640]{1,0:T(8,128)(2,1)S(1)} %get-tuple-element.84, bf16[640,5120]{1,0:T(8,128)(2,1)} %collective-permute-done.20, s32[]{:T(128)S(6)} %select_n.24, bf16[128,2560]{1,0:T(8,128)(2,1)S(1)} %collective-permute-done.21), kind=kOutput, calls=%fused_computation.4 | convolution fusion | flops 420741120 | bytes 6062084 | tf_op jit(solution)/shard_map/dot_general | solution.py:518
  162.5 3.4 %collective-permute-start.22 = (bf16[128,2560]{1,0:T(8,128)(2,1)S(1)}, bf16[128,2560]{1,0:T(8,128)(2,1)S(1)}, u32[]{:S(2)}, u32[]{:S(2)}) collective-permute-start(bf16[128,2560]{1,0:T(8,128)(2,1)S(1)} %fusion.2.keep_ref), channel_id=1, source_target_pairs={{0,1},{1,0},{2,3},{3,2},{4,5},{5,4},{6,7},{7,6},{8,9},{9,8},{10,11... | collective-permute-start | bytes 1966088 | tf_op jit(solution)/shard_map/ppermute | solution.py:267
  167.1 5.0 %collective-permute-start.23 = (bf16[4,32,1920]{2,1,0:T(8,128)(2,1)S(1)}, bf16[4,32,1920]{2,1,0:T(8,128)(2,1)S(1)}, u32[]{:S(2)}, u32[]{:S(2)}) collective-permute-start(bf16[4,32,1920]{2,1,0:T(8,128)(2,1)S(1)} %all-to-all-done.5.back_ref), channel_id=1, source_target_pairs={{0,1},{1,0},{2,3},{3,2},{4,5},{5,4},{6,7},{7,6},{8,9},{9,8},{10,11... | collective-permute-start | bytes 1474568 | tf_op jit(solution)/shard_map/ppermute | solution.py:267
  (79 shorter events, 47.8 us)
Async XLA Ops:
  4.6 13.3 %collective-permute-start.5 = (bf16[2,64,1280]{2,1,0:T(8,128)(2,1)}, bf16[2,64,1280]{2,1,0:T(8,128)(2,1)S(1)}, u32[]{:S(2)}, u32[]{:S(2)}) collective-permute-start(bf16[2,64,1280]{2,1,0:T(8,128)(2,1)} %param.15), channel_id=1, source_target_pairs={{0,2},{2,0},{1,3},{3,1},{4,6},{6,4},{5,7},{7,5},{8,10},{10,8},{9,1... | collective-permute-start | bytes 983048 | tf_op jit(solution)/shard_map/ppermute | solution.py:267
  5.2 15.2 %collective-permute-start.4 = (bf16[2,64,1280]{2,1,0:T(8,128)(2,1)}, bf16[2,64,1280]{2,1,0:T(8,128)(2,1)S(1)}, u32[]{:S(2)}, u32[]{:S(2)}) collective-permute-start(bf16[2,64,1280]{2,1,0:T(8,128)(2,1)} %param.15), channel_id=1, source_target_pairs={{0,1},{1,0},{2,3},{3,2},{4,5},{5,4},{6,7},{7,6},{8,9},{9,8},{10,11... | collective-permute-start | bytes 983048 | tf_op jit(solution)/shard_map/ppermute | solution.py:267
  5.6 19.4 %collective-permute-start.7 = (bf16[2,64,640]{2,1,0:T(8,128)(2,1)}, bf16[2,64,640]{2,1,0:T(8,128)(2,1)S(1)}, u32[]{:S(2)}, u32[]{:S(2)}) collective-permute-start(bf16[2,64,640]{2,1,0:T(8,128)(2,1)} %refs_0_.3), channel_id=1, source_target_pairs={{0,1},{1,0},{2,3},{3,2},{4,5},{5,4},{6,7},{7,6},{8,9},{9,8},{10,11... | collective-permute-start | bytes 491528 | tf_op jit(solution)/shard_map/ppermute | solution.py:267
  5.8 19.2 %collective-permute-start.8 = (bf16[2,64,640]{2,1,0:T(8,128)(2,1)}, bf16[2,64,640]{2,1,0:T(8,128)(2,1)S(1)}, u32[]{:S(2)}, u32[]{:S(2)}) collective-permute-start(bf16[2,64,640]{2,1,0:T(8,128)(2,1)} %refs_1_.3), channel_id=1, source_target_pairs={{0,1},{1,0},{2,3},{3,2},{4,5},{5,4},{6,7},{7,6},{8,9},{9,8},{10,11... | collective-permute-start | bytes 491528 | tf_op jit(solution)/shard_map/ppermute | solution.py:267
  6.1 132.1 %collective-permute-start.20 = (bf16[640,5120]{1,0:T(8,128)(2,1)}, bf16[640,5120]{1,0:T(8,128)(2,1)}, u32[]{:S(2)}, u32[]{:S(2)}) collective-permute-start(bf16[640,5120]{1,0:T(8,128)(2,1)} %param.14), channel_id=1, source_target_pairs={{0,1},{1,0},{2,3},{3,2},{4,5},{5,4},{6,7},{7,6},{8,9},{9,8},{10,11... | collective-permute-start | bytes 19660808 | tf_op jit(solution)/shard_map/ppermute | solution.py:267
  8.9 22.6 %all-to-all-start = ((bf16[4,32,2560]{2,1,0:T(8,128)(2,1)}), bf16[4,32,2560]{2,1,0:T(8,128)(2,1)S(1)}, u32[]{:S(2)}, u32[]{:S(2)}) async-start(bf16[4,32,2560]{2,1,0:T(8,128)(2,1)} %keep_keys.1), calls=%async_computation | async-start | bytes 1310720 | tf_op jit(solution)/shard_map/all_to_all | solution.py:448
  32.9 27.1 %all-to-all-start.1 = ((bf16[16,176,256]{2,1,0:T(8,128)(2,1)}), bf16[16,176,256]{2,1,0:T(8,128)(2,1)S(1)}, u32[]{:S(2)}, u32[]{:S(2)}) async-start(bf16[16,176,256]{2,1,0:T(8,128)(2,1)} %pack_keys.1), calls=%async_computation.1 | async-start | bytes 2883584 | tf_op jit(solution)/shard_map/all_to_all | solution.py:277
  39.6 10.0 %collective-permute-start.10 = (bf16[32,1920]{1,0:T(8,128)(2,1)S(1)}, bf16[32,1920]{1,0:T(8,128)(2,1)S(1)}, u32[]{:S(2)}, u32[]{:S(2)}) collective-permute-start(bf16[32,1920]{1,0:T(8,128)(2,1)S(1)} %get-tuple-element.54), channel_id=1, source_target_pairs={{0,4},{4,8},{8,12},{12,0},{1,5},{5,9},{9,13},{13,1},{2,6},{6,10},{... | collective-permute-start | bytes 368648 | tf_op jit(solution)/shard_map/ppermute | solution.py:273
  44.2 11.9 %collective-permute-start.11 = (bf16[32,1920]{1,0:T(8,128)(2,1)S(1)}, bf16[32,1920]{1,0:T(8,128)(2,1)S(1)}, u32[]{:S(2)}, u32[]{:S(2)}) collective-permute-start(bf16[32,1920]{1,0:T(8,128)(2,1)S(1)} %get-tuple-element.55), channel_id=1, source_target_pairs={{0,8},{4,12},{8,0},{12,4},{1,9},{5,13},{9,1},{13,5},{2,10},{6,14},... | collective-permute-start | bytes 368648 | tf_op jit(solution)/shard_map/ppermute | solution.py:273
  45.9 14.0 %collective-permute-start.12 = (bf16[32,1920]{1,0:T(8,128)(2,1)S(1)}, bf16[32,1920]{1,0:T(8,128)(2,1)S(1)}, u32[]{:S(2)}, u32[]{:S(2)}) collective-permute-start(bf16[32,1920]{1,0:T(8,128)(2,1)S(1)} %get-tuple-element.56), channel_id=1, source_target_pairs={{0,12},{4,0},{8,4},{12,8},{1,13},{5,1},{9,5},{13,9},{2,14},{6,2},{... | collective-permute-start | bytes 368648 | tf_op jit(solution)/shard_map/ppermute | solution.py:273
  59.9 8.8 %collective-permute-start.13 = (bf16[16,176,256]{2,1,0:T(8,128)(2,1)S(1)}, bf16[16,176,256]{2,1,0:T(8,128)(2,1)}, u32[]{:S(2)}, u32[]{:S(2)}) collective-permute-start(bf16[16,176,256]{2,1,0:T(8,128)(2,1)S(1)} %all-to-all-done.1.q_ref.ka_ref.refs_0_.refs_1_.refs_2_.k_ref), channel_id=1, source_target_pairs={{0,1},{1,0},{2,3},{3,2},{4,5},{5,4},{6,7},{7,6},{8,9},{9,8},{10,11... | collective-permute-start | bytes 4325384 | tf_op jit(solution)/shard_map/ppermute | solution.py:267
  64.3 24.1 %all-to-all-start.2 = ((bf16[16,304,128]{2,1,0:T(8,128)(2,1)}), bf16[16,304,128]{2,1,0:T(8,128)(2,1)S(1)}, u32[]{:S(2)}, u32[]{:S(2)}) async-start(bf16[16,304,128]{2,1,0:T(8,128)(2,1)} %pack_values.1), calls=%async_computation.2 | async-start | bytes 2490368 | tf_op jit(solution)/shard_map/all_to_all | solution.py:277
  88.4 5.7 %collective-permute-start.14 = (bf16[16,304,128]{2,1,0:T(8,128)(2,1)S(1)}, bf16[16,304,128]{2,1,0:T(8,128)(2,1)S(1)}, u32[]{:S(2)}, u32[]{:S(2)}) collective-permute-start(bf16[16,304,128]{2,1,0:T(8,128)(2,1)S(1)} %all-to-all-done.2.v_ref.t_ref.refs_0_.refs_1_.refs_2_.refs_3_.refs_4_.refs_5_), channel_id=1, source_target_pairs={{0,1},{1,0},{2,3},{3,2},{4,5},{5,4},{6,7},{7,6},{8,9},{9,8},{10,11... | collective-permute-start | bytes 3735560 | tf_op jit(solution)/shard_map/ppermute | solution.py:267
  100.6 11.7 %all-to-all-start.3 = ((bf16[16,48,256]{2,1,0:T(8,128)(2,1)}), bf16[16,48,256]{2,1,0:T(8,128)(2,1)S(1)}, u32[]{:S(2)}, u32[]{:S(2)}) async-start(bf16[16,48,256]{2,1,0:T(8,128)(2,1)} %get-tuple-element.67), calls=%async_computation.3 | async-start | bytes 786432 | tf_op jit(solution)/shard_map/all_to_all | solution.py:277
  112.3 9.6 %collective-permute-start.18 = (bf16[16,128,128]{2,1,0:T(8,128)(2,1)S(1)}, bf16[16,128,128]{2,1,0:T(8,128)(2,1)S(1)}, u32[]{:S(2)}, u32[]{:S(2)}) collective-permute-start(bf16[16,128,128]{2,1,0:T(8,128)(2,1)S(1)} %get-tuple-element.77), channel_id=1, source_target_pairs={{0,1},{1,0},{2,3},{3,2},{4,5},{5,4},{6,7},{7,6},{8,9},{9,8},{10,11... | collective-permute-start | bytes 1572872 | tf_op jit(solution)/shard_map/ppermute | solution.py:267
  114.8 8.7 %collective-permute-start.19 = (bf16[16,128,128]{2,1,0:T(8,128)(2,1)S(1)}, bf16[16,128,128]{2,1,0:T(8,128)(2,1)S(1)}, u32[]{:S(2)}, u32[]{:S(2)}) collective-permute-start(bf16[16,128,128]{2,1,0:T(8,128)(2,1)S(1)} %get-tuple-element.78), channel_id=1, source_target_pairs={{0,1},{1,0},{2,3},{3,2},{4,5},{5,4},{6,7},{7,6},{8,9},{9,8},{10,11... | collective-permute-start | bytes 1572872 | tf_op jit(solution)/shard_map/ppermute | solution.py:267
  115.5 14.5 %collective-permute-start.15 = (bf16[32,1280]{1,0:T(8,128)(2,1)S(1)}, bf16[32,1280]{1,0:T(8,128)(2,1)S(1)}, u32[]{:S(2)}, u32[]{:S(2)}) collective-permute-start(bf16[32,1280]{1,0:T(8,128)(2,1)S(1)} %get-tuple-element.73), channel_id=1, source_target_pairs={{0,4},{4,8},{8,12},{12,0},{1,5},{5,9},{9,13},{13,1},{2,6},{6,10},{... | collective-permute-start | bytes 245768 | tf_op jit(solution)/shard_map/ppermute | solution.py:273
  120.1 9.8 %collective-permute-start.16 = (bf16[32,1280]{1,0:T(8,128)(2,1)S(1)}, bf16[32,1280]{1,0:T(8,128)(2,1)S(1)}, u32[]{:S(2)}, u32[]{:S(2)}) collective-permute-start(bf16[32,1280]{1,0:T(8,128)(2,1)S(1)} %get-tuple-element.74), channel_id=1, source_target_pairs={{0,8},{4,12},{8,0},{12,4},{1,9},{5,13},{9,1},{13,5},{2,10},{6,14},... | collective-permute-start | bytes 245768 | tf_op jit(solution)/shard_map/ppermute | solution.py:273
  121.9 9.3 %collective-permute-start.17 = (bf16[32,1280]{1,0:T(8,128)(2,1)S(1)}, bf16[32,1280]{1,0:T(8,128)(2,1)S(1)}, u32[]{:S(2)}, u32[]{:S(2)}) collective-permute-start(bf16[32,1280]{1,0:T(8,128)(2,1)S(1)} %get-tuple-element.75), channel_id=1, source_target_pairs={{0,12},{4,0},{8,4},{12,8},{1,13},{5,1},{9,5},{13,9},{2,14},{6,2},{... | collective-permute-start | bytes 245768 | tf_op jit(solution)/shard_map/ppermute | solution.py:273
  131.2 21.6 %all-to-all-start.4 = ((bf16[16,304,128]{2,1,0:T(8,128)(2,1)}), bf16[16,304,128]{2,1,0:T(8,128)(2,1)S(1)}, u32[]{:S(2)}, u32[]{:S(2)}) async-start(bf16[16,304,128]{2,1,0:T(8,128)(2,1)} %grads_own.1), calls=%async_computation.4 | async-start | bytes 2490368 | tf_op jit(solution)/shard_map/all_to_all | solution.py:277
  140.8 19.1 %collective-permute-start.21 = (bf16[128,2560]{1,0:T(8,128)(2,1)S(1)}, bf16[128,2560]{1,0:T(8,128)(2,1)S(1)}, u32[]{:S(2)}, u32[]{:S(2)}) collective-permute-start(bf16[128,2560]{1,0:T(8,128)(2,1)S(1)} %fusion.1), channel_id=1, source_target_pairs={{0,2},{2,0},{1,3},{3,1},{4,6},{6,4},{5,7},{7,5},{8,10},{10,8},{9,1... | collective-permute-start | bytes 1966088 | tf_op jit(solution)/shard_map/ppermute | solution.py:267
  153.7 13.4 %all-to-all-start.5 = ((bf16[4,32,1920]{2,1,0:T(8,128)(2,1)}), bf16[4,32,1920]{2,1,0:T(8,128)(2,1)S(1)}, u32[]{:S(2)}, u32[]{:S(2)}) async-start(bf16[4,32,1920]{2,1,0:T(8,128)(2,1)} %unpack_grads.1), calls=%async_computation.5 | async-start | bytes 983040 | tf_op jit(solution)/shard_map/all_to_all | solution.py:448
  162.5 9.6 %collective-permute-start.22 = (bf16[128,2560]{1,0:T(8,128)(2,1)S(1)}, bf16[128,2560]{1,0:T(8,128)(2,1)S(1)}, u32[]{:S(2)}, u32[]{:S(2)}) collective-permute-start(bf16[128,2560]{1,0:T(8,128)(2,1)S(1)} %fusion.2.keep_ref), channel_id=1, source_target_pairs={{0,1},{1,0},{2,3},{3,2},{4,5},{5,4},{6,7},{7,6},{8,9},{9,8},{10,11... | collective-permute-start | bytes 1966088 | tf_op jit(solution)/shard_map/ppermute | solution.py:267
  167.1 6.5 %collective-permute-start.23 = (bf16[4,32,1920]{2,1,0:T(8,128)(2,1)S(1)}, bf16[4,32,1920]{2,1,0:T(8,128)(2,1)S(1)}, u32[]{:S(2)}, u32[]{:S(2)}) collective-permute-start(bf16[4,32,1920]{2,1,0:T(8,128)(2,1)S(1)} %all-to-all-done.5.back_ref), channel_id=1, source_target_pairs={{0,1},{1,0},{2,3},{3,2},{4,5},{5,4},{6,7},{7,6},{8,9},{9,8},{10,11... | collective-permute-start | bytes 1474568 | tf_op jit(solution)/shard_map/ppermute | solution.py:267
  (16 other events, 46.7 us)

commit v7 on v6

--- a/solution.py
+++ b/solution.py
@@ -108,8 +108,8 @@
         def _():
             g = window_rows(g_refs).astype(jnp.float32)
             attn = acc[0:HD, :].T.astype(jnp.bfloat16)
-            dsum = jnp.sum(attn.astype(jnp.float32) * g, axis=1, keepdims=True)
-            d_ref[...] = jnp.broadcast_to(dsum, (dsum.shape[0], HD)).T[0:1, :]
+            rounded = acc[0:HD, :].astype(jnp.bfloat16).astype(jnp.float32)
+            d_ref[...] = jnp.sum(rounded * g.T, axis=0, keepdims=True)
             tan = acc[HD:2 * HD, :] + SCALE * acc[2 * HD:, :]
             put_rows(out_ref, slice(0, HD), attn)
             put_rows(out_ref, slice(HD, 2 * HD), tan.T)

time: 175 us -> 175 us (level)
  no operation moved by 1% of the time
where the time goes in v7:
time: 175 us; the launch traced here: 174 us
  starting transfers between devices  66 us (38%)
  Pallas kernels  43.8 us (25%)
  waiting for transfers between devices  43.1 us (25%)
  matrix products  18.8 us (11%)
    pallas_call x14, Pallas kernels, kernel_call(): pl.pallas_call(body, grid_spec=pltpu.PrefetchScalarGridSpec(num_scalar_pr...  43.8 us
    all_to_all x4, waiting for transfers between devices, over_chips(): return lax.all_to_all(array, ('x', 'y'), 0, 0, tiled=True)  21.4 us
    ppermute x18, starting transfers between devices, swap(): return lax.ppermute(array, axis, SWAP)  21 us
    all_to_all x4, starting transfers between devices, over_chips(): return lax.all_to_all(array, ('x', 'y'), 0, 0, tiled=True)  18.4 us
    ppermute x6, starting transfers between devices, along_z(): lax.ppermute(a, 'z', route)  16.1 us
    ppermute x6, waiting for transfers between devices, along_z(): lax.ppermute(a, 'z', route)  13.5 us
    all_to_all x2, starting transfers between devices, over_planes(): return lax.all_to_all(array, 'z', 0, 0, tiled=True)  10.5 us
    dot_general x4, matrix products, project(): jnp.dot(rows_of, lax.dynamic_slice_in_dim(weight, chip * 2 * width, 2 * w...  10.4 us
  transfers between devices with their start and end apart: 30, of which 12 were waited for; matrix products, arithmetic and copies ran while one was open for 11% of the time, Pallas kernels for 25%

profile of v7, /device:TPU:1, one launch (start us, length us, event | category | flops | bytes accessed | tf_op | source)
XLA Modules:
  0.0 174.2 jit_solution(2567788479272925890)
XLA Ops:
  0.6 3.3 %collective-permute-start = (bf16[2,64,640]{2,1,0:T(8,128)(2,1)}, bf16[2,64,640]{2,1,0:T(8,128)(2,1)S(1)}, u32[]{:S(2)}, u32[]{:S(2)}) collective-permute-start(bf16[2,64,640]{2,1,0:T(8,128)(2,1)} %refs_0_.2), channel_id=1, source_target_pairs={{0,1},{1,0},{2,3},{3,2},{4,5},{5,4},{6,7},{7,6},{8,9},{9,8},{10,11... | collective-permute-start | bytes 491528 | tf_op jit(solution)/shard_map/ppermute | solution.py:267
  8.9 6.9 %all-to-all-start = ((bf16[4,32,2560]{2,1,0:T(8,128)(2,1)}), bf16[4,32,2560]{2,1,0:T(8,128)(2,1)S(1)}, u32[]{:S(2)}, u32[]{:S(2)}) async-start(bf16[4,32,2560]{2,1,0:T(8,128)(2,1)} %keep_keys.1), calls=%async_computation | async-start | bytes 1310720 | tf_op jit(solution)/shard_map/all_to_all | solution.py:448
  26.8 4.6 %all-to-all-done = bf16[4,32,2560]{2,1,0:T(8,128)(2,1)S(1)} async-done(((bf16[4,32,2560]{2,1,0:T(8,128)(2,1)}), bf16[4,32,2560]{2,1,0:T(8,128)(2,1)S(1)}, u32[]{:S(2)}, u32[]{:S(2)}) %all-to-all-start) | async-done | bytes 655392 | tf_op jit(solution)/shard_map/all_to_all | solution.py:448
  32.9 6.8 %all-to-all-start.1 = ((bf16[16,176,256]{2,1,0:T(8,128)(2,1)}), bf16[16,176,256]{2,1,0:T(8,128)(2,1)S(1)}, u32[]{:S(2)}, u32[]{:S(2)}) async-start(bf16[16,176,256]{2,1,0:T(8,128)(2,1)} %pack_keys.1), calls=%async_computation.1 | async-start | bytes 2883584 | tf_op jit(solution)/shard_map/all_to_all | solution.py:277
  39.6 4.6 %collective-permute-start.10 = (bf16[32,1920]{1,0:T(8,128)(2,1)S(1)}, bf16[32,1920]{1,0:T(8,128)(2,1)S(1)}, u32[]{:S(2)}, u32[]{:S(2)}) collective-permute-start(bf16[32,1920]{1,0:T(8,128)(2,1)S(1)} %get-tuple-element.54), channel_id=1, source_target_pairs={{0,4},{4,8},{8,12},{12,0},{1,5},{5,9},{9,13},{13,1},{2,6},{6,10},{... | collective-permute-start | bytes 368648 | tf_op jit(solution)/shard_map/ppermute | solution.py:273
  49.6 6.5 %collective-permute-done.11.refs_2_ = bf16[32,1920]{1,0:T(8,128)(2,1)S(1)} collective-permute-done((bf16[32,1920]{1,0:T(8,128)(2,1)S(1)}, bf16[32,1920]{1,0:T(8,128)(2,1)S(1)}, u32[]{:S(2)}, u32[]{:S(2)}) %collective-permute-start.11) | collective-permute-done | bytes 122912 | tf_op jit(solution)/shard_map/ppermute | solution.py:273
  56.1 3.8 %collective-permute-done.12.refs_3_ = bf16[32,1920]{1,0:T(8,128)(2,1)S(1)} collective-permute-done((bf16[32,1920]{1,0:T(8,128)(2,1)S(1)}, bf16[32,1920]{1,0:T(8,128)(2,1)S(1)}, u32[]{:S(2)}, u32[]{:S(2)}) %collective-permute-start.12) | collective-permute-done | bytes 122912 | tf_op jit(solution)/shard_map/ppermute | solution.py:273
  64.3 4.4 %all-to-all-start.2 = ((bf16[16,304,128]{2,1,0:T(8,128)(2,1)}), bf16[16,304,128]{2,1,0:T(8,128)(2,1)S(1)}, u32[]{:S(2)}, u32[]{:S(2)}) async-start(bf16[16,304,128]{2,1,0:T(8,128)(2,1)} %pack_values.1), calls=%async_computation.2 | async-start | bytes 2490368 | tf_op jit(solution)/shard_map/all_to_all | solution.py:277
  68.8 13.0 %weights.1 = (bf16[4096,768]{1,0:T(8,128)(2,1)}, bf16[4096,768]{1,0:T(8,128)(2,1)}) custom-call(s32[1]{0:T(128)} %bitcast.1.z_ref, bf16[16,176,256]{2,1,0:T(8,128)(2,1)S(1)} %all-to-all-done.1.q_ref.ka_ref.refs_0_.refs_1_.refs_2_.k_ref, bf16[16,176,256]{2,1,0:T(8,128)(2,1)S(1)} %all-to-all-done.1.q_ref.ka_ref.refs_0_.refs_1_.refs_2_.k_ref, ...), custom_call_target="tpu_custom_call" | custom-call | flops 3221225472 | bytes 33554432 | tf_op jit(solution)/shard_map/weights/pallas_call | solution.py:161
  81.8 6.6 %all-to-all-done.2.v_ref.t_ref.refs_0_.refs_1_.refs_2_.refs_3_.refs_4_.refs_5_ = bf16[16,304,128]{2,1,0:T(8,128)(2,1)S(1)} async-done(((bf16[16,304,128]{2,1,0:T(8,128)(2,1)}), bf16[16,304,128]{2,1,0:T(8,128)(2,1)S(1)}, u32[]{:S(2)}, u32[]{:S(2)}) %all-to-all-start.2) | async-done | bytes 1245216 | tf_op jit(solution)/shard_map/all_to_all | solution.py:277
  89.9 4.1 %values_own.1.refs_3_ = f32[384,768]{1,0:T(8,128)S(1)} custom-call(s32[1]{0:T(128)} %bitcast.1.z_ref, bf16[16,304,128]{2,1,0:T(8,128)(2,1)} %copy-done.3, bf16[16,304,128]{2,1,0:T(8,128)(2,1)} %copy-done.3, bf16[4096,768]{1,0:T(8,128)(2,1)} %get-tuple-element.65.p_ref, bf16[4096,768]{1,0:T(8,128)(2,1)} %get-tuple-element.66.w_ref), custom_call_target="tpu_custom_call" | custom-call | flops 1207959552 | bytes 8388608 | tf_op jit(solution)/shard_map/values_own/pallas_call | solution.py:161
  95.2 5.2 %values_other.1 = (bf16[16,48,256]{2,1,0:T(8,128)(2,1)}, f32[1,768]{1,0:T(1,128)S(1)}) custom-call(s32[1]{0:T(128)} %bitcast.1.z_ref, bf16[16,304,128]{2,1,0:T(8,128)(2,1)} %copy-done.4, bf16[16,304,128]{2,1,0:T(8,128)(2,1)} %copy-done.4, bf16[4096,768]{1,0:T(8,128)(2,1)} %get-tuple-element.65.p_ref, bf16[4096,768]{1,0:T(8,128)(2,1)} %get-tuple-element.66.w_ref, ...), custom_call_target="tpu_custom_call" | custom-call | flops 1207959552 | bytes 8388608 | tf_op jit(solution)/shard_map/values_other/pallas_call | solution.py:161
  100.4 3.6 %all-to-all-start.3 = ((bf16[16,48,256]{2,1,0:T(8,128)(2,1)}), bf16[16,48,256]{2,1,0:T(8,128)(2,1)S(1)}, u32[]{:S(2)}, u32[]{:S(2)}) async-start(bf16[16,48,256]{2,1,0:T(8,128)(2,1)} %get-tuple-element.67), calls=%async_computation.3 | async-start | bytes 786432 | tf_op jit(solution)/shard_map/all_to_all | solution.py:277
  103.9 5.3 %grads_other.1 = (bf16[16,128,128]{2,1,0:T(8,128)(2,1)S(1)}, bf16[16,128,128]{2,1,0:T(8,128)(2,1)S(1)}, f32[128,768]{1,0:T(8,128)S(1)}) custom-call(s32[1]{0:T(128)} %bitcast.1.z_ref, bf16[16,176,256]{2,1,0:T(8,128)(2,1)} %collective-permute-done.13.kb_ref.k_ref, bf16[16,304,128]{2,1,0:T(8,128)(2,1)} %copy-done.4, ...), custom_call_target="tpu_custom_call" | custom-call | flops 2013265920 | bytes 8388608 | tf_op jit(solution)/shard_map/grads_other/pallas_call | solution.py:161
  109.2 2.9 %all-to-all-done.3.back_ref = bf16[16,48,256]{2,1,0:T(8,128)(2,1)S(1)} async-done(((bf16[16,48,256]{2,1,0:T(8,128)(2,1)}), bf16[16,48,256]{2,1,0:T(8,128)(2,1)S(1)}, u32[]{:S(2)}, u32[]{:S(2)}) %all-to-all-start.3) | async-done | bytes 393248 | tf_op jit(solution)/shard_map/all_to_all | solution.py:277
  115.3 4.7 %collective-permute-start.15 = (bf16[32,1280]{1,0:T(8,128)(2,1)S(1)}, bf16[32,1280]{1,0:T(8,128)(2,1)S(1)}, u32[]{:S(2)}, u32[]{:S(2)}) collective-permute-start(bf16[32,1280]{1,0:T(8,128)(2,1)S(1)} %get-tuple-element.73), channel_id=1, source_target_pairs={{0,4},{4,8},{8,12},{12,0},{1,5},{5,9},{9,13},{13,1},{2,6},{6,10},{... | collective-permute-start | bytes 245768 | tf_op jit(solution)/shard_map/ppermute | solution.py:273
  123.4 6.4 %grads_own.1 = bf16[16,304,128]{2,1,0:T(8,128)(2,1)} custom-call(s32[1]{0:T(128)} %bitcast.1.z_ref, bf16[16,176,256]{2,1,0:T(8,128)(2,1)} %copy-done, bf16[16,304,128]{2,1,0:T(8,128)(2,1)} %copy-done.3, bf16[4096,768]{1,0:T(8,128)(2,1)} %get-tuple-element.65.p_ref, f32[1,768]{1,0:T(1,128)S(1)} %get-tuple-element.68.d_ref, bf16[16,176,256]{2,1,0:T(8,128)(2,1)} %copy-done, ...), custom_call_target="tpu_custom_call" | custom-call | flops 2013265920 | bytes 8388608 | tf_op jit(solution)/shard_map/grads_own/pallas_call | solution.py:161
  131.0 3.7 %all-to-all-start.4 = ((bf16[16,304,128]{2,1,0:T(8,128)(2,1)}), bf16[16,304,128]{2,1,0:T(8,128)(2,1)S(1)}, u32[]{:S(2)}, u32[]{:S(2)}) async-start(bf16[16,304,128]{2,1,0:T(8,128)(2,1)} %grads_own.1), calls=%async_computation.4 | async-start | bytes 2490368 | tf_op jit(solution)/shard_map/all_to_all | solution.py:277
  138.0 2.6 %fusion.1 = bf16[128,2560]{1,0:T(8,128)(2,1)S(1)} fusion(f32[128,2560]{1,0:T(8,128)S(1)} %fusion.4, bf16[128,640]{1,0:T(8,128)(2,1)S(1)} %get-tuple-element.84, bf16[640,5120]{1,0:T(8,128)(2,1)} %collective-permute-done.20, s32[]{:T(128)S(6)} %select_n.25), kind=kOutput, calls=%fused_computation.3 | convolution fusion | flops 420085760 | bytes 5406724 | tf_op jit(solution)/shard_map/dot_general | solution.py:518
  140.8 11.9 %all-to-all-done.4.back_ref = bf16[16,304,128]{2,1,0:T(8,128)(2,1)S(1)} async-done(((bf16[16,304,128]{2,1,0:T(8,128)(2,1)}), bf16[16,304,128]{2,1,0:T(8,128)(2,1)S(1)}, u32[]{:S(2)}, u32[]{:S(2)}) %all-to-all-start.4) | async-done | bytes 1245216 | tf_op jit(solution)/shard_map/all_to_all | solution.py:277
  153.6 3.6 %all-to-all-start.5 = ((bf16[4,32,1920]{2,1,0:T(8,128)(2,1)}), bf16[4,32,1920]{2,1,0:T(8,128)(2,1)S(1)}, u32[]{:S(2)}, u32[]{:S(2)}) async-start(bf16[4,32,1920]{2,1,0:T(8,128)(2,1)} %unpack_grads.1), calls=%async_computation.5 | async-start | bytes 983040 | tf_op jit(solution)/shard_map/all_to_all | solution.py:448
  159.7 2.6 %fusion.2.keep_ref = bf16[128,2560]{1,0:T(8,128)(2,1)S(1)} fusion(f32[128,2560]{1,0:T(8,128)S(1)} %fusion.7, bf16[128,640]{1,0:T(8,128)(2,1)S(1)} %get-tuple-element.84, bf16[640,5120]{1,0:T(8,128)(2,1)} %collective-permute-done.20, s32[]{:T(128)S(6)} %select_n.24, bf16[128,2560]{1,0:T(8,128)(2,1)S(1)} %collective-permute-done.21), kind=kOutput, calls=%fused_computation.4 | convolution fusion | flops 420741120 | bytes 6062084 | tf_op jit(solution)/shard_map/dot_general | solution.py:518
  162.3 3.4 %collective-permute-start.22 = (bf16[128,2560]{1,0:T(8,128)(2,1)S(1)}, bf16[128,2560]{1,0:T(8,128)(2,1)S(1)}, u32[]{:S(2)}, u32[]{:S(2)}) collective-permute-start(bf16[128,2560]{1,0:T(8,128)(2,1)S(1)} %fusion.2.keep_ref), channel_id=1, source_target_pairs={{0,1},{1,0},{2,3},{3,2},{4,5},{5,4},{6,7},{7,6},{8,9},{9,8},{10,11... | collective-permute-start | bytes 1966088 | tf_op jit(solution)/shard_map/ppermute | solution.py:267
  166.9 5.0 %collective-permute-start.23 = (bf16[4,32,1920]{2,1,0:T(8,128)(2,1)S(1)}, bf16[4,32,1920]{2,1,0:T(8,128)(2,1)S(1)}, u32[]{:S(2)}, u32[]{:S(2)}) collective-permute-start(bf16[4,32,1920]{2,1,0:T(8,128)(2,1)S(1)} %all-to-all-done.5.back_ref), channel_id=1, source_target_pairs={{0,1},{1,0},{2,3},{3,2},{4,5},{5,4},{6,7},{7,6},{8,9},{9,8},{10,11... | collective-permute-start | bytes 1474568 | tf_op jit(solution)/shard_map/ppermute | solution.py:267
  (79 shorter events, 47.7 us)
Async XLA Ops:
  4.6 13.3 %collective-permute-start.5 = (bf16[2,64,1280]{2,1,0:T(8,128)(2,1)}, bf16[2,64,1280]{2,1,0:T(8,128)(2,1)S(1)}, u32[]{:S(2)}, u32[]{:S(2)}) collective-permute-start(bf16[2,64,1280]{2,1,0:T(8,128)(2,1)} %param.15), channel_id=1, source_target_pairs={{0,2},{2,0},{1,3},{3,1},{4,6},{6,4},{5,7},{7,5},{8,10},{10,8},{9,1... | collective-permute-start | bytes 983048 | tf_op jit(solution)/shard_map/ppermute | solution.py:267
  5.2 15.2 %collective-permute-start.4 = (bf16[2,64,1280]{2,1,0:T(8,128)(2,1)}, bf16[2,64,1280]{2,1,0:T(8,128)(2,1)S(1)}, u32[]{:S(2)}, u32[]{:S(2)}) collective-permute-start(bf16[2,64,1280]{2,1,0:T(8,128)(2,1)} %param.15), channel_id=1, source_target_pairs={{0,1},{1,0},{2,3},{3,2},{4,5},{5,4},{6,7},{7,6},{8,9},{9,8},{10,11... | collective-permute-start | bytes 983048 | tf_op jit(solution)/shard_map/ppermute | solution.py:267
  5.6 19.4 %collective-permute-start.7 = (bf16[2,64,640]{2,1,0:T(8,128)(2,1)}, bf16[2,64,640]{2,1,0:T(8,128)(2,1)S(1)}, u32[]{:S(2)}, u32[]{:S(2)}) collective-permute-start(bf16[2,64,640]{2,1,0:T(8,128)(2,1)} %refs_0_.3), channel_id=1, source_target_pairs={{0,1},{1,0},{2,3},{3,2},{4,5},{5,4},{6,7},{7,6},{8,9},{9,8},{10,11... | collective-permute-start | bytes 491528 | tf_op jit(solution)/shard_map/ppermute | solution.py:267
  5.8 19.2 %collective-permute-start.8 = (bf16[2,64,640]{2,1,0:T(8,128)(2,1)}, bf16[2,64,640]{2,1,0:T(8,128)(2,1)S(1)}, u32[]{:S(2)}, u32[]{:S(2)}) collective-permute-start(bf16[2,64,640]{2,1,0:T(8,128)(2,1)} %refs_1_.3), channel_id=1, source_target_pairs={{0,1},{1,0},{2,3},{3,2},{4,5},{5,4},{6,7},{7,6},{8,9},{9,8},{10,11... | collective-permute-start | bytes 491528 | tf_op jit(solution)/shard_map/ppermute | solution.py:267
  6.1 131.9 %collective-permute-start.20 = (bf16[640,5120]{1,0:T(8,128)(2,1)}, bf16[640,5120]{1,0:T(8,128)(2,1)}, u32[]{:S(2)}, u32[]{:S(2)}) collective-permute-start(bf16[640,5120]{1,0:T(8,128)(2,1)} %param.14), channel_id=1, source_target_pairs={{0,1},{1,0},{2,3},{3,2},{4,5},{5,4},{6,7},{7,6},{8,9},{9,8},{10,11... | collective-permute-start | bytes 19660808 | tf_op jit(solution)/shard_map/ppermute | solution.py:267
  8.9 22.6 %all-to-all-start = ((bf16[4,32,2560]{2,1,0:T(8,128)(2,1)}), bf16[4,32,2560]{2,1,0:T(8,128)(2,1)S(1)}, u32[]{:S(2)}, u32[]{:S(2)}) async-start(bf16[4,32,2560]{2,1,0:T(8,128)(2,1)} %keep_keys.1), calls=%async_computation | async-start | bytes 1310720 | tf_op jit(solution)/shard_map/all_to_all | solution.py:448
  32.9 27.1 %all-to-all-start.1 = ((bf16[16,176,256]{2,1,0:T(8,128)(2,1)}), bf16[16,176,256]{2,1,0:T(8,128)(2,1)S(1)}, u32[]{:S(2)}, u32[]{:S(2)}) async-start(bf16[16,176,256]{2,1,0:T(8,128)(2,1)} %pack_keys.1), calls=%async_computation.1 | async-start | bytes 2883584 | tf_op jit(solution)/shard_map/all_to_all | solution.py:277
  39.6 10.0 %collective-permute-start.10 = (bf16[32,1920]{1,0:T(8,128)(2,1)S(1)}, bf16[32,1920]{1,0:T(8,128)(2,1)S(1)}, u32[]{:S(2)}, u32[]{:S(2)}) collective-permute-start(bf16[32,1920]{1,0:T(8,128)(2,1)S(1)} %get-tuple-element.54), channel_id=1, source_target_pairs={{0,4},{4,8},{8,12},{12,0},{1,5},{5,9},{9,13},{13,1},{2,6},{6,10},{... | collective-permute-start | bytes 368648 | tf_op jit(solution)/shard_map/ppermute | solution.py:273
  44.2 11.9 %collective-permute-start.11 = (bf16[32,1920]{1,0:T(8,128)(2,1)S(1)}, bf16[32,1920]{1,0:T(8,128)(2,1)S(1)}, u32[]{:S(2)}, u32[]{:S(2)}) collective-permute-start(bf16[32,1920]{1,0:T(8,128)(2,1)S(1)} %get-tuple-element.55), channel_id=1, source_target_pairs={{0,8},{4,12},{8,0},{12,4},{1,9},{5,13},{9,1},{13,5},{2,10},{6,14},... | collective-permute-start | bytes 368648 | tf_op jit(solution)/shard_map/ppermute | solution.py:273
  45.9 14.0 %collective-permute-start.12 = (bf16[32,1920]{1,0:T(8,128)(2,1)S(1)}, bf16[32,1920]{1,0:T(8,128)(2,1)S(1)}, u32[]{:S(2)}, u32[]{:S(2)}) collective-permute-start(bf16[32,1920]{1,0:T(8,128)(2,1)S(1)} %get-tuple-element.56), channel_id=1, source_target_pairs={{0,12},{4,0},{8,4},{12,8},{1,13},{5,1},{9,5},{13,9},{2,14},{6,2},{... | collective-permute-start | bytes 368648 | tf_op jit(solution)/shard_map/ppermute | solution.py:273
  59.9 8.8 %collective-permute-start.13 = (bf16[16,176,256]{2,1,0:T(8,128)(2,1)S(1)}, bf16[16,176,256]{2,1,0:T(8,128)(2,1)}, u32[]{:S(2)}, u32[]{:S(2)}) collective-permute-start(bf16[16,176,256]{2,1,0:T(8,128)(2,1)S(1)} %all-to-all-done.1.q_ref.ka_ref.refs_0_.refs_1_.refs_2_.k_ref), channel_id=1, source_target_pairs={{0,1},{1,0},{2,3},{3,2},{4,5},{5,4},{6,7},{7,6},{8,9},{9,8},{10,11... | collective-permute-start | bytes 4325384 | tf_op jit(solution)/shard_map/ppermute | solution.py:267
  64.3 24.1 %all-to-all-start.2 = ((bf16[16,304,128]{2,1,0:T(8,128)(2,1)}), bf16[16,304,128]{2,1,0:T(8,128)(2,1)S(1)}, u32[]{:S(2)}, u32[]{:S(2)}) async-start(bf16[16,304,128]{2,1,0:T(8,128)(2,1)} %pack_values.1), calls=%async_computation.2 | async-start | bytes 2490368 | tf_op jit(solution)/shard_map/all_to_all | solution.py:277
  88.4 5.7 %collective-permute-start.14 = (bf16[16,304,128]{2,1,0:T(8,128)(2,1)S(1)}, bf16[16,304,128]{2,1,0:T(8,128)(2,1)S(1)}, u32[]{:S(2)}, u32[]{:S(2)}) collective-permute-start(bf16[16,304,128]{2,1,0:T(8,128)(2,1)S(1)} %all-to-all-done.2.v_ref.t_ref.refs_0_.refs_1_.refs_2_.refs_3_.refs_4_.refs_5_), channel_id=1, source_target_pairs={{0,1},{1,0},{2,3},{3,2},{4,5},{5,4},{6,7},{7,6},{8,9},{9,8},{10,11... | collective-permute-start | bytes 3735560 | tf_op jit(solution)/shard_map/ppermute | solution.py:267
  100.4 11.7 %all-to-all-start.3 = ((bf16[16,48,256]{2,1,0:T(8,128)(2,1)}), bf16[16,48,256]{2,1,0:T(8,128)(2,1)S(1)}, u32[]{:S(2)}, u32[]{:S(2)}) async-start(bf16[16,48,256]{2,1,0:T(8,128)(2,1)} %get-tuple-element.67), calls=%async_computation.3 | async-start | bytes 786432 | tf_op jit(solution)/shard_map/all_to_all | solution.py:277
  112.1 9.6 %collective-permute-start.18 = (bf16[16,128,128]{2,1,0:T(8,128)(2,1)S(1)}, bf16[16,128,128]{2,1,0:T(8,128)(2,1)S(1)}, u32[]{:S(2)}, u32[]{:S(2)}) collective-permute-start(bf16[16,128,128]{2,1,0:T(8,128)(2,1)S(1)} %get-tuple-element.77), channel_id=1, source_target_pairs={{0,1},{1,0},{2,3},{3,2},{4,5},{5,4},{6,7},{7,6},{8,9},{9,8},{10,11... | collective-permute-start | bytes 1572872 | tf_op jit(solution)/shard_map/ppermute | solution.py:267
  114.7 8.7 %collective-permute-start.19 = (bf16[16,128,128]{2,1,0:T(8,128)(2,1)S(1)}, bf16[16,128,128]{2,1,0:T(8,128)(2,1)S(1)}, u32[]{:S(2)}, u32[]{:S(2)}) collective-permute-start(bf16[16,128,128]{2,1,0:T(8,128)(2,1)S(1)} %get-tuple-element.78), channel_id=1, source_target_pairs={{0,1},{1,0},{2,3},{3,2},{4,5},{5,4},{6,7},{7,6},{8,9},{9,8},{10,11... | collective-permute-start | bytes 1572872 | tf_op jit(solution)/shard_map/ppermute | solution.py:267
  115.3 14.5 %collective-permute-start.15 = (bf16[32,1280]{1,0:T(8,128)(2,1)S(1)}, bf16[32,1280]{1,0:T(8,128)(2,1)S(1)}, u32[]{:S(2)}, u32[]{:S(2)}) collective-permute-start(bf16[32,1280]{1,0:T(8,128)(2,1)S(1)} %get-tuple-element.73), channel_id=1, source_target_pairs={{0,4},{4,8},{8,12},{12,0},{1,5},{5,9},{9,13},{13,1},{2,6},{6,10},{... | collective-permute-start | bytes 245768 | tf_op jit(solution)/shard_map/ppermute | solution.py:273
  120.0 9.8 %collective-permute-start.16 = (bf16[32,1280]{1,0:T(8,128)(2,1)S(1)}, bf16[32,1280]{1,0:T(8,128)(2,1)S(1)}, u32[]{:S(2)}, u32[]{:S(2)}) collective-permute-start(bf16[32,1280]{1,0:T(8,128)(2,1)S(1)} %get-tuple-element.74), channel_id=1, source_target_pairs={{0,8},{4,12},{8,0},{12,4},{1,9},{5,13},{9,1},{13,5},{2,10},{6,14},... | collective-permute-start | bytes 245768 | tf_op jit(solution)/shard_map/ppermute | solution.py:273
  121.7 9.3 %collective-permute-start.17 = (bf16[32,1280]{1,0:T(8,128)(2,1)S(1)}, bf16[32,1280]{1,0:T(8,128)(2,1)S(1)}, u32[]{:S(2)}, u32[]{:S(2)}) collective-permute-start(bf16[32,1280]{1,0:T(8,128)(2,1)S(1)} %get-tuple-element.75), channel_id=1, source_target_pairs={{0,12},{4,0},{8,4},{12,8},{1,13},{5,1},{9,5},{13,9},{2,14},{6,2},{... | collective-permute-start | bytes 245768 | tf_op jit(solution)/shard_map/ppermute | solution.py:273
  131.0 21.6 %all-to-all-start.4 = ((bf16[16,304,128]{2,1,0:T(8,128)(2,1)}), bf16[16,304,128]{2,1,0:T(8,128)(2,1)S(1)}, u32[]{:S(2)}, u32[]{:S(2)}) async-start(bf16[16,304,128]{2,1,0:T(8,128)(2,1)} %grads_own.1), calls=%async_computation.4 | async-start | bytes 2490368 | tf_op jit(solution)/shard_map/all_to_all | solution.py:277
  140.7 19.1 %collective-permute-start.21 = (bf16[128,2560]{1,0:T(8,128)(2,1)S(1)}, bf16[128,2560]{1,0:T(8,128)(2,1)S(1)}, u32[]{:S(2)}, u32[]{:S(2)}) collective-permute-start(bf16[128,2560]{1,0:T(8,128)(2,1)S(1)} %fusion.1), channel_id=1, source_target_pairs={{0,2},{2,0},{1,3},{3,1},{4,6},{6,4},{5,7},{7,5},{8,10},{10,8},{9,1... | collective-permute-start | bytes 1966088 | tf_op jit(solution)/shard_map/ppermute | solution.py:267
  153.6 13.3 %all-to-all-start.5 = ((bf16[4,32,1920]{2,1,0:T(8,128)(2,1)}), bf16[4,32,1920]{2,1,0:T(8,128)(2,1)S(1)}, u32[]{:S(2)}, u32[]{:S(2)}) async-start(bf16[4,32,1920]{2,1,0:T(8,128)(2,1)} %unpack_grads.1), calls=%async_computation.5 | async-start | bytes 983040 | tf_op jit(solution)/shard_map/all_to_all | solution.py:448
  162.3 9.6 %collective-permute-start.22 = (bf16[128,2560]{1,0:T(8,128)(2,1)S(1)}, bf16[128,2560]{1,0:T(8,128)(2,1)S(1)}, u32[]{:S(2)}, u32[]{:S(2)}) collective-permute-start(bf16[128,2560]{1,0:T(8,128)(2,1)S(1)} %fusion.2.keep_ref), channel_id=1, source_target_pairs={{0,1},{1,0},{2,3},{3,2},{4,5},{5,4},{6,7},{7,6},{8,9},{9,8},{10,11... | collective-permute-start | bytes 1966088 | tf_op jit(solution)/shard_map/ppermute | solution.py:267
  166.9 6.5 %collective-permute-start.23 = (bf16[4,32,1920]{2,1,0:T(8,128)(2,1)S(1)}, bf16[4,32,1920]{2,1,0:T(8,128)(2,1)S(1)}, u32[]{:S(2)}, u32[]{:S(2)}) collective-permute-start(bf16[4,32,1920]{2,1,0:T(8,128)(2,1)S(1)} %all-to-all-done.5.back_ref), channel_id=1, source_target_pairs={{0,1},{1,0},{2,3},{3,2},{4,5},{5,4},{6,7},{7,6},{8,9},{9,8},{10,11... | collective-permute-start | bytes 1474568 | tf_op jit(solution)/shard_map/ppermute | solution.py:267
  (16 other events, 46.7 us)
